TPU v7x, 32 devices: a whole 2x2x4 slice. The times are simulated.
32 devices in a mesh: samp: 16 (over z, y, x), var: 2 (over core).
Axes of the slice: x: 2, y: 2, z: 4, core: 2. Of those that a mesh axis runs over, the one named last changes fastest.
Arguments:
- genotypes: bfloat16 [8192, 32768], P('samp', 'var'), may hold values from 0 to 2
- frequency: float32 [32768], P('var'), may hold values from 0.05 to 0.5
- start_block: float32 [32768, 16], P('var'), may hold values from -6 to 6
Outputs:
- loadings: float32 [32768, 16], P('var')
- scores: float32 [8192, 16], P('samp')
All inputs are finite; a program needn't handle non-finite values.
Results may differ from a plain program's by a relative error of at most 0.013.
Values may be sent and summed in bfloat16 or wider, within the bound.
No kernel may reach another device: no remote copies, remote signals or barrier semaphores. Data moves between devices by JAX's collectives and lax.ppermute only.
A program may use at most 64 MiB of HBM per device.

v0:
```python
import jax
import jax.numpy as jnp
from jax import lax
from jax.sharding import PartitionSpec as P

VARIANTS = 32768
ITERS = 2


def project_rounded(standardized, narrow):
    partial_rows = jnp.dot(standardized, narrow, preferred_element_type=jnp.float32)
    return lax.psum(partial_rows.astype(jnp.bfloat16), "var")


def new_basis(variant_block, gram_matrix):
    factor = jnp.linalg.cholesky(gram_matrix)
    return jax.scipy.linalg.solve_triangular(factor, variant_block.T, lower=True).T


def local(genotypes, frequency, start_block):
    centre = 2.0 * frequency
    standardized = (
        (genotypes.astype(jnp.float32) - centre) / jnp.sqrt(centre * (1.0 - frequency))
    ).astype(jnp.bfloat16)
    narrow = start_block.astype(jnp.bfloat16)
    basis_cols = start_block
    for iteration in range(ITERS):
        sample_block = project_rounded(standardized, narrow)
        partial_terms = lax.dot_general(
            standardized, sample_block, (((0,), (0,)), ((), ())), preferred_element_type=jnp.float32
        )
        variant_block = lax.psum(partial_terms, "samp")
        local_gram = jnp.dot(variant_block.T, variant_block, precision=lax.Precision.HIGHEST)
        gram_matrix = lax.psum(local_gram, "var")
        basis_cols = new_basis(variant_block, gram_matrix)
        narrow = basis_cols.astype(jnp.bfloat16)
    scaling = jnp.sqrt(jnp.float32(VARIANTS))
    loadings = basis_cols * scaling
    partial_scores = jnp.dot(standardized, narrow, preferred_element_type=jnp.float32)
    scores = lax.psum(partial_scores, "var")
    return (loadings, scores)


def solution(mesh):
    placed = (P("samp", "var"), P("var"), P("var", None))
    return jax.shard_map(
        local,
        mesh=mesh,
        in_specs=placed,
        out_specs=(P("var", None), P("samp", None)),
        check_vma=False,
    )
```

profile of v0, /device:TPU:0, one launch (start us, length us, event | category | flops | bytes accessed | tf_op | source)
XLA Modules:
  0.0 333.6 jit_solution(14465291028961206797)
XLA Ops:
  7.2 0.0 all-reduce.3.cloned.1.call-start
  7.2 0.9 broadcast_multiply_fusion
  8.1 0.0 copy-start.1
  8.1 9.8 %divide_convert_fusion = bf16[512,16384]{1,0:T(8,128)(2,1)S(1)} fusion(bf16[512,16384]{1,0:T(8,128)(2,1)} %param.6, f32[16384]{0:T(1024)S(1)} %get-tuple-element.5, f32[16384]{0:T(1024)S(1)} %get-tuple-element.4), kind=kLoop, calls=%fused_computation | loop fusion | flops 33554432 | bytes 33685504 | tf_op jit(solution)/shard_map/convert_element_type | solution.py:24
  17.9 0.0 copy-start
  17.9 5.7 %copy-done = bf16[512,16384]{1,0:T(8,128)(2,1)} copy-done((bf16[512,16384]{1,0:T(8,128)(2,1)}, bf16[512,16384]{1,0:T(8,128)(2,1)S(1)}, u32[]{:S(2)}) %copy-start) | copy-done | bytes 16777240
  23.6 0.0 copy-done.1
  23.7 4.4 %convolution_convert_fusion.2 = bf16[512,16]{1,0:T(8,128)(2,1)S(1)} fusion(bf16[512,16384]{1,0:T(8,128)(2,1)S(1)} %divide_convert_fusion, f32[16384,16]{0,1:T(8,128)S(1)} %copy-done.1), kind=kOutput, calls=%fused_computation.3 | convolution fusion | flops 268705792 | bytes 17842176 | tf_op jit(solution)/shard_map/dot_general | solution.py:11
  28.1 4.0 %psum.49 = bf16[512,16]{1,0:T(8,128)(2,1)S(1)} all-reduce(bf16[512,16]{1,0:T(8,128)(2,1)S(1)} %convolution_convert_fusion.2), channel_id=1, replica_groups=mesh['samp'=16,'var'=2] {'var'}, use_global_device_ids=true, to_apply=%region_0.0 | all-reduce | flops 8192 | bytes 32768 | tf_op jit(solution)/shard_map/psum | solution.py:12
  32.2 9.1 %fusion.14 = f32[16384,16]{0,1:T(8,128)} fusion(bf16[512,16384]{1,0:T(8,128)(2,1)} %copy-done, bf16[512,16]{1,0:T(8,128)(2,1)S(1)} %psum.49), kind=kOutput, calls=%fused_computation.30 | convolution fusion | flops 268435456 | bytes 17842176 | tf_op jit(solution)/shard_map/dot_general | solution.py:29
  41.2 0.0 all-reduce.3.cloned.1.call-update
  41.3 0.0 all-reduce.5.cloned.1.call-start
  41.3 114.3 %all-reduce.3.cloned.1.call-done = f32[16384,16]{0,1:T(8,128)} async-done(((f32[16384,16]{0,1:T(8,128)}), f32[16384,16]{0,1:T(8,128)}) %all-reduce.3.cloned.1.call-update) | async-done | bytes 1048592 | tf_op jit(solution)/shard_map/psum | solution.py:32
  155.6 3.1 fusion.15
  158.7 2.5 psum.51
  161.2 0.1 copy.6
  161.3 1.5 cholesky.44
  162.8 0.6 compare_reduce_fusion.1
  163.4 0.6 fusion.6
  164.1 1.2 custom-call.6
  165.3 2.3 convolution_convert_fusion
  167.6 8.1 %convolution_convert_fusion.1 = bf16[512,16]{1,0:T(8,128)(2,1)S(1)} fusion(bf16[512,16384]{1,0:T(8,128)(2,1)} %copy-done, bf16[16,16384]{1,0:T(8,128)(2,1)S(1)} %convolution_convert_fusion), kind=kOutput, calls=%fused_computation.2 | convolution fusion | flops 268443648 | bytes 17317888 | tf_op jit(solution)/shard_map/dot_general | solution.py:11
  175.7 3.8 %psum.52 = bf16[512,16]{1,0:T(8,128)(2,1)S(1)} all-reduce(bf16[512,16]{1,0:T(8,128)(2,1)S(1)} %convolution_convert_fusion.1), channel_id=1, replica_groups=mesh['samp'=16,'var'=2] {'var'}, use_global_device_ids=true, to_apply=%region_5.0 | all-reduce | flops 8192 | bytes 32768 | tf_op jit(solution)/shard_map/psum | solution.py:12
  179.5 9.1 %fusion.16 = f32[16384,16]{0,1:T(8,128)} fusion(bf16[512,16384]{1,0:T(8,128)(2,1)} %copy-done, bf16[512,16]{1,0:T(8,128)(2,1)S(1)} %psum.52), kind=kOutput, calls=%fused_computation.32 | convolution fusion | flops 268435456 | bytes 17842176 | tf_op jit(solution)/shard_map/dot_general | solution.py:29
  188.5 0.0 all-reduce.5.cloned.1.call-update
  188.6 111.0 %all-reduce.5.cloned.1.call-done = f32[16384,16]{0,1:T(8,128)} async-done(((f32[16384,16]{0,1:T(8,128)}), f32[16384,16]{0,1:T(8,128)}) %all-reduce.5.cloned.1.call-update) | async-done | bytes 1048592 | tf_op jit(solution)/shard_map/psum | solution.py:32
  299.5 3.1 fusion.17
  302.6 2.5 psum.54
  305.1 0.1 copy.8
  305.2 1.5 cholesky.55
  306.7 0.6 compare_reduce_fusion
  307.3 0.6 fusion.7
  308.0 1.2 custom-call.7
  309.2 2.3 fusion
  311.5 10.2 %fusion.3 = f32[512,16]{0,1:T(8,128)S(1)} fusion(bf16[512,16384]{1,0:T(8,128)(2,1)} %copy-done, f32[16,16384]{1,0:T(8,128)S(1)} %fusion), kind=kOutput, calls=%fused_computation.8 | convolution fusion | flops 268697600 | bytes 17858560 | tf_op jit(solution)/shard_map/dot_general | solution.py:39
  321.7 1.1 multiply_bitcast_fusion
  322.7 4.0 %psum.55 = f32[512,16]{0,1:T(8,128)} all-reduce(f32[512,16]{0,1:T(8,128)S(1)} %fusion.3), channel_id=1, replica_groups=mesh['samp'=16,'var'=2] {'var'}, use_global_device_ids=true, to_apply=%region_8.11 | all-reduce | flops 8192 | bytes 65536 | tf_op jit(solution)/shard_map/psum | solution.py:40
  (4 shorter events, 0.1 us)
Async XLA Ops:
  7.2 148.5 %all-reduce.3.cloned.1.call-start = ((), (), s32[]{:S(2)}) async-start(), calls=%async_computation | async-start | bytes 2097152 | tf_op jit(solution)/shard_map/psum | solution.py:32
  8.1 15.6 %copy-start.1 = (f32[16384,16]{0,1:T(8,128)S(1)}, f32[16384,16]{0,1:T(8,128)}, u32[]{:S(2)}) copy-start(f32[16384,16]{0,1:T(8,128)} %param.8) | copy-start | bytes 3145732
  17.9 5.7 %copy-start = (bf16[512,16384]{1,0:T(8,128)(2,1)}, bf16[512,16384]{1,0:T(8,128)(2,1)S(1)}, u32[]{:S(2)}) copy-start(bf16[512,16384]{1,0:T(8,128)(2,1)S(1)} %divide_convert_fusion) | copy-start | bytes 50331652
  41.3 258.2 %all-reduce.5.cloned.1.call-start = ((), (), s32[]{:S(2)}) async-start(), calls=%async_computation.1 | async-start | bytes 2097152 | tf_op jit(solution)/shard_map/psum | solution.py:32
Sparse Core Ops, SparseCore 0:
  41.4 114.1 all-reduce.2
  188.7 110.7 all-reduce.4
where the time goes:
time: 334 us
  waiting for transfers between devices  225 us (67%)
  matrix products  51.6 us (15%)
  other arithmetic  19.8 us (6%)
  blocking collectives  16.8 us (5%)
  between operations  14.1 us (4%)
  local copies, waits for them, and re-layouts  5.86 us (2%)
    psum x2, waiting for transfers between devices, local(): variant_block = lax.psum(partial_terms, 'samp')  225 us
    dot_general x2, matrix products, local(): lax.dot_general(standardized, sample_block, (((0,), (0,)), ((), ())), pre...  18.2 us
    dot_general x2, matrix products, project_rounded(): jnp.dot(standardized, narrow, preferred_element_type=jnp.float32)  12.6 us
    dot_general x1, matrix products, local(): jnp.dot(standardized, narrow, preferred_element_type=jnp.float32)  10.2 us
    convert_element_type x1, other arithmetic, local(): standardized = ((genotypes.astype(jnp.float32) - centre) / jnp.sqrt(centr...  9.84 us
    psum x2, blocking collectives, project_rounded(): return lax.psum(partial_rows.astype(jnp.bfloat16), 'var')  7.8 us
  transfers between devices with their start and end apart: 2, of which 2 were waited for; matrix products, arithmetic and copies ran while one was open for 0% of the time, Pallas kernels for 0%

commit v1 on v0

v1 whole, which is shorter than its diff:
```python
import functools

import jax
import jax.numpy as jnp
from jax import lax
from jax.experimental import pallas as pl
from jax.experimental.pallas import tpu as pltpu
from jax.sharding import PartitionSpec as P

ITERS = 2
HALVES = 2
MIB = 1 << 20
LANES = 128
HERE = pl.BlockSpec(memory_space=pltpu.VMEM)
KEPT = pl.BlockSpec(memory_space=pltpu.VMEM)


def dot(a, b, over):
    return lax.dot_general(a, b, ((over[:1], over[1:]), ((), ())), preferred_element_type=jnp.float32)


def shape(dims, dtype=jnp.bfloat16):
    return jax.ShapeDtypeStruct(dims, dtype)


def call(body, out, operands, flops, name, vmem=4 * MIB):
    moved = sum(x.size * x.dtype.itemsize for x in operands)
    return pl.pallas_call(
        body,
        out_shape=out,
        in_specs=[HERE] * len(operands),
        out_specs=jax.tree.map(lambda _: HERE, out),
        compiler_params=pltpu.CompilerParams(vmem_limit_bytes=vmem),
        cost_estimate=pl.CostEstimate(flops=flops, bytes_accessed=moved, transcendentals=0),
        name=name,
    )(*operands)


def in_vmem(x):
    return pltpu.with_memory_space_constraint(x, pltpu.VMEM)


def in_hbm(x):
    return pltpu.with_memory_space_constraint(x, pltpu.HBM)


def in_parts(x, count):
    parts = []
    for _ in range(count):
        parts.append(x.astype(jnp.bfloat16).astype(jnp.float32))
        x = x - parts[-1]
    return parts


def load_body(width, group, g_ref, f_ref, b_ref, a_ref, t_ref, s_ref, centre_ref, root_ref, rows_ref, *scratch):
    f_vm, b_vm, inverse, parts, sems = scratch
    block = b_ref.shape[0]
    rows, cols = a_ref.shape
    steps = cols // width
    bodies = steps // group

    def columns(i, size):
        return pl.ds(pl.multiple_of(i * size, size), size)

    def chunk(i):
        here = columns(i, width)
        return pltpu.make_async_copy(g_ref.at[:, here], a_ref.at[:, here], sems.at[i])

    def start_chunk(i):
        here = columns(i, width * group)
        return pltpu.make_async_copy(b_ref.at[:, here], b_vm.at[:, here], sems.at[steps + 1 + i])

    table = pltpu.make_async_copy(f_ref, f_vm, sems.at[steps])
    table.start()

    @pl.loop(0, bodies)
    def _(i):
        start_chunk(i).start()
        for k in range(group):
            chunk(i * group + k).start()

    parts[...] = jnp.zeros(parts.shape, jnp.float32)
    table.wait()

    @pl.loop(0, f_vm.shape[0] // 8)
    def _(i):
        frequency = f_vm[columns(i, 8), :]
        centre = 2.0 * frequency
        root = jnp.sqrt(centre * (1.0 - frequency))
        scale = 1.0 / root
        high, middle, low = in_parts(centre, 3)
        for r in range(8):
            here = columns(8 * i + r, LANES)
            one = slice(r, r + 1)
            centre_ref[:, here] = centre[one]
            root_ref[:, here] = root[one]
            inverse[:, here] = scale[one]
            parts[0:1, here] = high[one]
            parts[1:2, here] = middle[one]
            parts[2:3, here] = low[one]

    def body(i, carry):
        total, shift = carry
        start_chunk(i).wait()
        for k in range(group):
            at = i * group + k
            here = columns(at, width)
            three = parts[:, here]
            three = jnp.concatenate([three, jnp.zeros_like(three)], axis=0).astype(jnp.bfloat16)
            rows_ref[:, here] = three
            narrow = (b_vm[:, here] * inverse[:, here]).astype(jnp.bfloat16)
            shift = shift + dot(narrow, three, (1, 1))
            chunk(at).wait()
            turned = a_ref[:, here].T
            t_ref[here, :] = turned
            total = total + dot(narrow, turned, (1, 0))
        return total, shift

    carry = (jnp.zeros((block, rows), jnp.float32), jnp.zeros((block, block), jnp.float32))
    total, shift = lax.fori_loop(0, bodies, body, carry)
    s_ref[...] = (total - jnp.sum(shift, axis=1, keepdims=True)).astype(jnp.bfloat16)


def load(genotypes, frequency, start_rows):
    rows, cols = genotypes.shape
    block = start_rows.shape[0]
    width = cols // 16
    anywhere = pl.BlockSpec(memory_space=pltpu.HBM)
    return pl.pallas_call(
        functools.partial(load_body, width, 8),
        in_specs=[anywhere] * 3,
        out_specs=[KEPT] * 2 + [HERE] * 4,
        out_shape=[
            pltpu.VMEM((rows, cols), jnp.bfloat16),
            pltpu.VMEM((cols, rows), jnp.bfloat16),
            shape((block, rows)),
            shape((1, cols), jnp.float32),
            shape((1, cols), jnp.float32),
            shape((block, cols)),
        ],
        scratch_shapes=[
            pltpu.VMEM((cols // LANES, LANES), jnp.float32),
            pltpu.VMEM((block, cols), jnp.float32),
            pltpu.VMEM((1, cols), jnp.float32),
            pltpu.VMEM((8, cols), jnp.float32),
            pltpu.SemaphoreType.DMA((cols // width + 3,)),
        ],
        compiler_params=pltpu.CompilerParams(vmem_limit_bytes=8 * MIB),
        name="load",
    )(in_hbm(genotypes), in_hbm(frequency.reshape(cols // LANES, LANES)), in_hbm(start_rows))


def columns_of(key, inner, width, cols):
    turn, half = key
    group = cols // inner
    place = lax.rem(lax.axis_index("samp"), inner) ^ turn
    return pl.ds(pl.multiple_of(place * group + (half or 0) * (group // HALVES), group // HALVES), width)


def terms_body(key, inner, centre_ref, a_ref, *refs):
    t_ref = refs[-1]
    columns = columns_of(key, inner, *(t_ref.shape[1], a_ref.shape[1]))
    rows = refs[0][...]
    if len(refs) == 3:
        rows = (rows.astype(jnp.float32) + refs[1][...].astype(jnp.float32)).astype(jnp.bfloat16)
    sums = jnp.sum(rows.astype(jnp.float32), axis=1, keepdims=True)
    t_ref[...] = (dot(rows, a_ref[:, columns], (1, 0)) - sums * centre_ref[:, columns]).astype(t_ref.dtype)


def terms(sample_rows, kept, centre, key, inner, dtype=jnp.bfloat16):
    width = kept.shape[1] // inner // (HALVES if key[1] is not None else 1)
    return call(
        functools.partial(terms_body, key, inner),
        shape((sample_rows[0].shape[0], width), dtype),
        (centre, in_vmem(kept), *sample_rows),
        10000,
        "terms%d%d" % (HALVES if key[1] is None else key[1], key[0]),
    )


def inner_sum_body(half, own_ref, *refs):
    value = own_ref[...]
    width = value.shape[1]
    for part in refs[:-1]:
        first = half * width if part.shape[1] > width else 0
        value = value + part[:, first : first + width].astype(jnp.float32)
    refs[-1][...] = value.astype(jnp.bfloat16)


def pair_sum_body(own_ref, other_ref, out_ref):
    out_ref[...] = (own_ref[...].astype(jnp.float32) + other_ref[...].astype(jnp.float32)).astype(jnp.bfloat16)


def outer_sum_body(key, inner, root_ref, own_ref, other_ref, out_ref):
    root = root_ref[:, columns_of(key, inner, out_ref.shape[1], root_ref.shape[1])]
    value = own_ref[...].astype(jnp.float32) + other_ref[...].astype(jnp.float32)
    out_ref[...] = (value / (root * root)).astype(jnp.bfloat16)


def stack_body(*refs):
    width = refs[0].shape[1]
    for k, part in enumerate(refs[:-1]):
        refs[-1][:, k * width : (k + 1) * width] = part[...]


def swap(x, axis, size, turn):
    return lax.ppermute(x, axis, [(d, d ^ turn) for d in range(size)])


def swap_across(x, size, turns_by_core):
    cores = len(turns_by_core)
    pairs = [(d * cores + v, (d ^ t) * cores + v) for d in range(size) for v, t in enumerate(turns_by_core)]
    return lax.ppermute(x, ("samp", "var"), pairs)


def sum_over_samples(sample_rows, kept, centre, root, inner):
    count, near, far = 4 * inner, inner, 2 * inner
    x, y, diagonal = 1, 2, 3
    across = swap(terms(sample_rows, kept, centre, (diagonal, None), inner), "samp", count, diagonal)
    pieces = {}
    for h in range(HALVES):
        received = [swap(terms(sample_rows, kept, centre, (t, h), inner), "samp", count, t) for t in (x, y)]
        own = terms(sample_rows, kept, centre, (0, h), inner, jnp.float32)
        piece = shape(own.shape)
        body = functools.partial(inner_sum_body, h)
        plane = call(body, piece, (own, *received, across), own.size * inner, "inner_sum%d" % h)
        pair = call(pair_sum_body, piece, (plane, swap_across(plane, count, (near, far))), own.size, "pair_sum%d" % h)
        body = functools.partial(outer_sum_body, (0, h), inner)
        whole = call(body, piece, (root, pair, swap_across(pair, count, (far, near))), own.size, "outer_sum%d" % h)
        pieces[0, h] = whole
        for t in (y, x):
            pieces[t, h] = swap(whole, "samp", count, t)
    both = [pieces[0, h] for h in range(HALVES)]
    group = shape((both[0].shape[0], HALVES * both[0].shape[1]))
    pieces[diagonal, None] = swap(call(stack_body, group, tuple(both), 0, "stack"), "samp", count, diagonal)
    order = [(0, 0), (y, 0), (x, 0), (0, 1), (diagonal, None), (y, 1), (x, 1)]
    return {key: pieces[key] for key in order}


def project_body(keys, inner, rows_ref, root_ref, turned_ref, *refs):
    pieces, out = refs[: len(keys)], refs[-1]
    block = pieces[0].shape[0]
    cols, rows = turned_ref.shape
    total = jnp.zeros((block, rows), jnp.float32)
    shift = jnp.zeros((block, block), jnp.float32)
    gram = jnp.zeros((block, block), jnp.float32)
    for key, piece in zip(keys, pieces):
        columns = columns_of(key, inner, piece.shape[1], cols)
        value = (piece[...].astype(jnp.float32) * root_ref[:, columns]).astype(jnp.bfloat16)
        gram += dot(value, value, (1, 1))
        shift += dot(piece[...], rows_ref[:, columns], (1, 1))
        total += dot(piece[...], turned_ref[columns, :], (1, 0))
    total -= jnp.sum(shift, axis=1, keepdims=True)
    gram = jnp.concatenate([gram, jnp.zeros((block, LANES - block), jnp.float32)], axis=1)
    if len(refs) == len(keys) + 2:
        total += refs[-2][:, :rows]
        gram += refs[-2][:, rows:]
    out[:, :rows] = total
    out[:, rows:] = gram


def project(pieces, turned, centre_rows, root, inner):
    order = list(pieces)
    block = centre_rows.shape[0]
    rows = turned.shape[1]
    total = ()
    for first, last in ((0, 4), (4, 5), (5, 6), (6, 7)):
        keys = order[first:last]
        operands = (centre_rows, root, in_vmem(turned), *(pieces[key] for key in keys)) + total
        body = functools.partial(project_body, keys, inner)
        out = shape((block, rows + LANES), jnp.float32)
        flops = (7 if first == 0 else 1) * 2 * rows * sum(pieces[key].size for key in keys)
        total = (call(body, out, operands, flops, "project%d" % first),)
    return total[0]


def inverse_factor(gram):
    block = gram.shape[0]
    dims = gram.shape
    row = lax.broadcasted_iota(jnp.int32, dims, 0)
    lane = lax.broadcasted_iota(jnp.int32, dims, 1)
    columns = [jnp.broadcast_to(gram[:, j : j + 1], dims) for j in range(block)]
    right = jnp.where(row == lane, 1.0, 0.0)
    scale = jnp.zeros(dims, jnp.float32)
    for k in range(block):
        pivot = jnp.broadcast_to(columns[k][k : k + 1], dims)
        factor = jnp.where(row > k, columns[k] / pivot, 0.0)
        scale = jnp.where(row == k, lax.rsqrt(pivot), scale)
        right = right - factor * jnp.broadcast_to(right[k : k + 1], dims)
        for j in range(k + 1, block):
            columns[j] = columns[j] - factor * jnp.broadcast_to(columns[j][k : k + 1], dims)
    return (right * scale)[:, :block]


def solve_both(own_ref, other_ref):
    rows = own_ref.shape[1] - LANES
    inverse = inverse_factor(own_ref[:, rows:] + other_ref[:, rows:])
    projected = lax.dot_general(
        inverse,
        own_ref[:, :rows] + other_ref[:, :rows],
        (((1,), (0,)), ((), ())),
        precision=lax.Precision.HIGHEST,
        preferred_element_type=jnp.float32,
    )
    return inverse, projected


def solve_body(own_ref, other_ref, out_ref):
    out_ref[...] = solve_both(own_ref, other_ref)[1].astype(out_ref.dtype)


def solve(own, other):
    block, rows = own.shape
    return call(solve_body, shape((block, rows - LANES)), (own, other), 6 * 32 * own.size, "solve")


def finish_body(scaling, order, inner, own_ref, other_ref, root_ref, *refs):
    pieces, (out, scores, held, kept_scores, sems) = refs[:-5], refs[-5:]
    block, cols = held.shape
    inverse, projected = solve_both(own_ref, other_ref)
    kept_scores[...] = projected
    copies = [pltpu.make_async_copy(kept_scores, scores, sems.at[len(order)])]
    copies[0].start()
    split = jnp.concatenate(in_parts(inverse * scaling, 2), axis=0).astype(jnp.bfloat16)
    done = 0
    for at, (key, piece) in enumerate(zip(order, pieces)):
        width = piece.shape[1]
        columns = columns_of(key, inner, width, cols)
        value = dot(split, piece[...], (1, 0))
        here = slice(done, done + width)
        held[:, here] = (value[:block] + value[block:]) * root_ref[:, columns]
        copies.append(pltpu.make_async_copy(held.at[:, here], out.at[:, columns], sems.at[at]))
        copies[-1].start()
        done += width
    for copy in copies:
        copy.wait()


def finish(own, other, root, pieces, scaling, inner):
    block, cols = own.shape[0], root.shape[1]
    rows = own.shape[1] - LANES
    order = list(pieces)
    return pl.pallas_call(
        functools.partial(finish_body, scaling, order, inner),
        out_shape=[shape((block, cols), jnp.float32), shape((block, rows), jnp.float32)],
        in_specs=[HERE] * (3 + len(order)),
        out_specs=[pl.BlockSpec(memory_space=pltpu.HBM)] * 2,
        scratch_shapes=[
            pltpu.VMEM((block, cols), jnp.float32),
            pltpu.VMEM((block, rows), jnp.float32),
            pltpu.SemaphoreType.DMA((len(order) + 1,)),
        ],
        compiler_params=pltpu.CompilerParams(vmem_limit_bytes=8 * MIB),
        name="finish",
    )(own, other, root, *pieces.values())


def make_local(inner, var):
    def local(genotypes, frequency, start_block):
        scaling = float(start_block.shape[0] * var) ** 0.5
        kept, turned, own, centre, root, centre_rows = load(genotypes, frequency, start_block.T)
        sample_rows = (own, swap(own, "var", var, 1))
        for iteration in range(ITERS):
            pieces = sum_over_samples(sample_rows, kept, centre, root, inner)
            own = project(pieces, turned, centre_rows, root, inner)
            other = swap(own, "var", var, 1)
            if iteration < ITERS - 1:
                sample_rows = (solve(own, other),)
        loadings, scores = finish(own, other, root, pieces, scaling, inner)
        return loadings.T, scores.T

    return local


def dot_plain(a, b, dims, **kw):
    return lax.dot_general(a, b, (dims, ((), ())), preferred_element_type=jnp.float32, **kw)


def make_plain(samp, var):
    def local(genotypes, frequency, start_block):
        block = start_block.shape[1]
        centre = 2.0 * frequency
        kept = ((genotypes.astype(jnp.float32) - centre) / jnp.sqrt(centre * (1.0 - frequency))).astype(jnp.bfloat16)
        narrow = start_block.astype(jnp.bfloat16).T
        sample_rows = lax.psum(dot_plain(narrow, kept, ((1,), (1,))).astype(jnp.bfloat16), "var")
        for iteration in range(ITERS):
            rows = dot_plain(sample_rows.astype(jnp.bfloat16), kept, ((1,), (0,)))
            rows = lax.psum(rows, "samp").astype(jnp.bfloat16)
            gram = lax.psum(dot_plain(rows, rows, ((1,), (1,))), "var")
            factor = jnp.linalg.cholesky(gram)
            eye = jnp.eye(block, dtype=jnp.float32)
            inverse = jax.scipy.linalg.solve_triangular(factor, eye, lower=True)
            projected = lax.psum(dot_plain(rows, kept, ((1,), (1,))), "var")
            high = lax.Precision.HIGHEST
            sample_rows = dot_plain(inverse, projected, ((1,), (0,)), precision=high)
        scaling = float(start_block.shape[0] * var) ** 0.5
        loadings = dot_plain(inverse * scaling, rows.astype(jnp.float32), ((1,), (0,)), precision=high)
        return loadings.T, sample_rows.T

    return local


def solution(mesh):
    samp, var = mesh.shape["samp"], mesh.shape["var"]

    def whole(genotypes, frequency, start_block):
        cols = start_block.shape[0] // var
        if samp == 16 and var == 2 and cols % (samp * LANES) == 0:
            local = make_local(samp // 4, var)
        else:
            local = make_plain(samp, var)
        placed = (P("samp", "var"), P("var"), P("var", None))
        return jax.shard_map(
            local, mesh=mesh, in_specs=placed, out_specs=(P("var", None), P("samp", None)), check_vma=False
        )(genotypes, frequency, start_block)

    return whole
```

time: 334 us -> 75.5 us (0.23)
  waiting for transfers between devices: 225 us -> 14.8 us
  matrix products: 51.6 us -> 0 us
  starting transfers between devices: 0.08 us -> 37.6 us
  Pallas kernels: 0 us -> 22.1 us
  other arithmetic: 19.8 us -> 0 us
  blocking collectives: 16.8 us -> 0 us
  between operations: 14.1 us -> 0.92 us
  local copies, waits for them, and re-layouts: 5.86 us -> 0 us
    psum x2 -> x0, waiting for transfers between devices: 225 us -> none  [local(): variant_block = lax.psum(partial_terms, 'samp')]
    dot_general x7 -> x0, matrix products: 47.1 us -> none  [the longest x2 18.2 us: local(): lax.dot_general(standardized, sample_block, (((0,), (0,)), ((), ())), pre...]
    ppermute x0 -> x31, starting transfers between devices: none -> 37.6 us  [the longest x23 24.5 us: swap(): return lax.ppermute(x, axis, [(d, d ^ turn) for d in range(size)])]
    pallas_call x0 -> x39, Pallas kernels: none -> 22.1 us  [the longest x37 13 us: call(): pl.pallas_call(body, out_shape=out, in_specs=[HERE] * len(operands), out_...]
    psum x5 -> x0, blocking collectives: 16.8 us -> none  [the longest x2 7.8 us: project_rounded(): return lax.psum(partial_rows.astype(jnp.bfloat16), 'var')]
    ppermute x0 -> x31, waiting for transfers between devices: none -> 14.8 us  [the longest x23 8.66 us: swap(): return lax.ppermute(x, axis, [(d, d ^ turn) for d in range(size)])]
    convert_element_type x1 -> x0, other arithmetic: 9.84 us -> none  [local(): standardized = ((genotypes.astype(jnp.float32) - centre) / jnp.sqrt(centr...]
    another operation x10 -> x0, other arithmetic: 8.01 us -> none  [the longest x6 4.26 us: new_basis(): factor = jnp.linalg.cholesky(gram_matrix)]
  transfers between devices with their start and end apart: 2 -> 31, of which waited for: 2 -> 19; matrix products, arithmetic and copies ran while one was open for 0% -> 0% of each run, Pallas kernels for 0% -> 14%
where the time goes in v1:
time: 75.5 us; the launch traced here: 75.3 us
  starting transfers between devices  37.6 us (50%)
  Pallas kernels  22.1 us (29%)
  waiting for transfers between devices  14.8 us (20%)
  between operations  0.92 us (1%)
    ppermute x23, starting transfers between devices, swap(): return lax.ppermute(x, axis, [(d, d ^ turn) for d in range(size)])  24.5 us
    ppermute x8, starting transfers between devices, swap_across(): return lax.ppermute(x, ('samp', 'var'), pairs)  13 us
    pallas_call x37, Pallas kernels, call(): pl.pallas_call(body, out_shape=out, in_specs=[HERE] * len(operands), out_...  13 us
    ppermute x23, waiting for transfers between devices, swap(): return lax.ppermute(x, axis, [(d, d ^ turn) for d in range(size)])  8.66 us
    pallas_call x1, Pallas kernels, load(): pl.pallas_call(functools.partial(load_body, width, 8), in_specs=[anywhere...  7.5 us
    ppermute x8, waiting for transfers between devices, swap_across(): return lax.ppermute(x, ('samp', 'var'), pairs)  6.13 us
    pallas_call x1, Pallas kernels, finish(): pl.pallas_call(functools.partial(finish_body, scaling, order, inner), out...  1.56 us
  transfers between devices with their start and end apart: 31, of which 19 were waited for; matrix products, arithmetic and copies ran while one was open for 0% of the time, Pallas kernels for 14%

profile of v1, /device:TPU:0, one launch (start us, length us, event | category | flops | bytes accessed | tf_op | source)
XLA Modules:
  0.0 75.3 jit_solution(14153578514744917267)
XLA Ops:
  0.6 7.5 %load.1 = (bf16[512,16384]{1,0:T(8,128)(2,1)S(1)}, bf16[16384,512]{1,0:T(8,128)(2,1)S(1)}, bf16[16,512]{1,0:T(8,128)(2,1)S(1)}, f32[1,16384]{1,0:T(1,128)S(1)}, ...) custom-call(bf16[512,16384]{1,0:T(8,128)(2,1)} %g_ref.1, f32[128,128]{1,0:T(8,128)} %bitcast.5, f32[16,16384]{1,0:T(8,128)} %bitcast.4), custom_call_target="tpu_custom_call" | custom-call | tf_op jit(solution)/shard_map/load/pallas_call | solution.py:129
  8.1 0.5 collective-permute-start
  8.7 0.8 %collective-permute-done.refs_1_ = bf16[16,512]{1,0:T(8,128)(2,1)S(1)} collective-permute-done((bf16[16,512]{1,0:T(8,128)(2,1)S(1)}, bf16[16,512]{1,0:T(8,128)(2,1)S(1)}, u32[]{:S(2)}, u32[]{:S(2)}) %collective-permute-start) | collective-permute-done | bytes 16416 | tf_op jit(solution)/shard_map/ppermute | solution.py:207
  9.5 0.7 terms23.2
  10.1 3.8 %collective-permute-start.3 = (bf16[16,4096]{1,0:T(8,128)(2,1)S(1)}, bf16[16,4096]{1,0:T(8,128)(2,1)S(1)}, u32[]{:S(2)}, u32[]{:S(2)}) collective-permute-start(bf16[16,4096]{1,0:T(8,128)(2,1)S(1)} %terms23.2), channel_id=1, source_target_pairs={{0,6},{2,4},{4,2},{6,0},{8,14},{10,12},{12,10},{14,8},{16,22},{18,... | collective-permute-start | bytes 393224 | tf_op jit(solution)/shard_map/ppermute | solution.py:207
  13.9 0.4 terms02.2
  14.3 0.5 collective-permute-start.9
  14.9 0.4 terms01.2
  15.3 0.4 terms12.2
  15.7 2.0 %collective-permute-start.2 = (bf16[16,2048]{1,0:T(8,128)(2,1)S(1)}, bf16[16,2048]{1,0:T(8,128)(2,1)S(1)}, u32[]{:S(2)}, u32[]{:S(2)}) collective-permute-start(bf16[16,2048]{1,0:T(8,128)(2,1)S(1)} %terms12.2), channel_id=1, source_target_pairs={{0,4},{2,6},{4,0},{6,2},{8,12},{10,14},{12,8},{14,10},{16,20},{18,... | collective-permute-start | bytes 196616 | tf_op jit(solution)/shard_map/ppermute | solution.py:207
  17.7 0.4 terms11.2
  18.1 1.5 %collective-permute-start.1 = (bf16[16,2048]{1,0:T(8,128)(2,1)S(1)}, bf16[16,2048]{1,0:T(8,128)(2,1)S(1)}, u32[]{:S(2)}, u32[]{:S(2)}) collective-permute-start(bf16[16,2048]{1,0:T(8,128)(2,1)S(1)} %terms11.2), channel_id=1, source_target_pairs={{0,2},{2,0},{4,6},{6,4},{8,10},{10,8},{12,14},{14,12},{16,18},{18,... | collective-permute-start | bytes 196616 | tf_op jit(solution)/shard_map/ppermute | solution.py:207
  19.6 0.4 terms00.2.own_ref
  20.0 1.6 %collective-permute-start.10 = (bf16[16,2048]{1,0:T(8,128)(2,1)S(1)}, bf16[16,2048]{1,0:T(8,128)(2,1)S(1)}, u32[]{:S(2)}, u32[]{:S(2)}) collective-permute-start(bf16[16,2048]{1,0:T(8,128)(2,1)S(1)} %inner_sum0.2.own_ref), channel_id=1, source_target_pairs={{0,8},{1,17},{2,10},{3,19},{4,12},{5,21},{6,14},{7,23},{8,0},{9,25... | collective-permute-start | bytes 196616 | tf_op jit(solution)/shard_map/ppermute | solution.py:213
  21.7 0.4 terms10.2.own_ref
  22.4 1.6 %collective-permute-start.4 = (bf16[16,2048]{1,0:T(8,128)(2,1)S(1)}, bf16[16,2048]{1,0:T(8,128)(2,1)S(1)}, u32[]{:S(2)}, u32[]{:S(2)}) collective-permute-start(bf16[16,2048]{1,0:T(8,128)(2,1)S(1)} %inner_sum1.2.own_ref), channel_id=1, source_target_pairs={{0,8},{1,17},{2,10},{3,19},{4,12},{5,21},{6,14},{7,23},{8,0},{9,25... | collective-permute-start | bytes 196616 | tf_op jit(solution)/shard_map/ppermute | solution.py:213
  24.4 2.7 %collective-permute-start.11 = (bf16[16,2048]{1,0:T(8,128)(2,1)S(1)}, bf16[16,2048]{1,0:T(8,128)(2,1)S(1)}, u32[]{:S(2)}, u32[]{:S(2)}) collective-permute-start(bf16[16,2048]{1,0:T(8,128)(2,1)S(1)} %pair_sum0.2.own_ref), channel_id=1, source_target_pairs={{0,16},{1,9},{2,18},{3,11},{4,20},{5,13},{6,22},{7,15},{8,24},{9,1... | collective-permute-start | bytes 196616 | tf_op jit(solution)/shard_map/ppermute | solution.py:213
  27.1 0.8 %collective-permute-done.4.other_ref = bf16[16,2048]{1,0:T(8,128)(2,1)S(1)} collective-permute-done((bf16[16,2048]{1,0:T(8,128)(2,1)S(1)}, bf16[16,2048]{1,0:T(8,128)(2,1)S(1)}, u32[]{:S(2)}, u32[]{:S(2)}) %collective-permute-start.4) | collective-permute-done | bytes 65568 | tf_op jit(solution)/shard_map/ppermute | solution.py:213
  27.9 1.5 %collective-permute-start.5 = (bf16[16,2048]{1,0:T(8,128)(2,1)S(1)}, bf16[16,2048]{1,0:T(8,128)(2,1)S(1)}, u32[]{:S(2)}, u32[]{:S(2)}) collective-permute-start(bf16[16,2048]{1,0:T(8,128)(2,1)S(1)} %pair_sum1.2.own_ref), channel_id=1, source_target_pairs={{0,16},{1,9},{2,18},{3,11},{4,20},{5,13},{6,22},{7,15},{8,24},{9,1... | collective-permute-start | bytes 196616 | tf_op jit(solution)/shard_map/ppermute | solution.py:213
  29.7 1.6 %collective-permute-start.13 = (bf16[16,2048]{1,0:T(8,128)(2,1)S(1)}, bf16[16,2048]{1,0:T(8,128)(2,1)S(1)}, u32[]{:S(2)}, u32[]{:S(2)}) collective-permute-start(bf16[16,2048]{1,0:T(8,128)(2,1)S(1)} %outer_sum0.2.refs_0_), channel_id=1, source_target_pairs={{0,4},{2,6},{4,0},{6,2},{8,12},{10,14},{12,8},{14,10},{16,20},{18,... | collective-permute-start | bytes 196616 | tf_op jit(solution)/shard_map/ppermute | solution.py:207
  31.3 0.8 %collective-permute-start.14 = (bf16[16,2048]{1,0:T(8,128)(2,1)S(1)}, bf16[16,2048]{1,0:T(8,128)(2,1)S(1)}, u32[]{:S(2)}, u32[]{:S(2)}) collective-permute-start(bf16[16,2048]{1,0:T(8,128)(2,1)S(1)} %outer_sum0.2.refs_0_), channel_id=1, source_target_pairs={{0,2},{2,0},{4,6},{6,4},{8,10},{10,8},{12,14},{14,12},{16,18},{18,... | collective-permute-start | bytes 196616 | tf_op jit(solution)/shard_map/ppermute | solution.py:207
  32.1 1.0 %collective-permute-done.5.other_ref = bf16[16,2048]{1,0:T(8,128)(2,1)S(1)} collective-permute-done((bf16[16,2048]{1,0:T(8,128)(2,1)S(1)}, bf16[16,2048]{1,0:T(8,128)(2,1)S(1)}, u32[]{:S(2)}, u32[]{:S(2)}) %collective-permute-start.5) | collective-permute-done | bytes 65568 | tf_op jit(solution)/shard_map/ppermute | solution.py:213
  33.2 1.7 %collective-permute-start.12 = (bf16[16,4096]{1,0:T(8,128)(2,1)S(1)}, bf16[16,4096]{1,0:T(8,128)(2,1)S(1)}, u32[]{:S(2)}, u32[]{:S(2)}) collective-permute-start(bf16[16,4096]{1,0:T(8,128)(2,1)S(1)} %stack.2), channel_id=1, source_target_pairs={{0,6},{2,4},{4,2},{6,0},{8,14},{10,12},{12,10},{14,8},{16,22},{18,... | collective-permute-start | bytes 393224 | tf_op jit(solution)/shard_map/ppermute | solution.py:207
  34.9 2.0 %collective-permute-start.7 = (bf16[16,2048]{1,0:T(8,128)(2,1)S(1)}, bf16[16,2048]{1,0:T(8,128)(2,1)S(1)}, u32[]{:S(2)}, u32[]{:S(2)}) collective-permute-start(bf16[16,2048]{1,0:T(8,128)(2,1)S(1)} %outer_sum1.2.refs_1_.refs_3_), channel_id=1, source_target_pairs={{0,4},{2,6},{4,0},{6,2},{8,12},{10,14},{12,8},{14,10},{16,20},{18,... | collective-permute-start | bytes 196616 | tf_op jit(solution)/shard_map/ppermute | solution.py:207
  36.9 1.5 %project0.2.refs_1_ = f32[16,640]{1,0:T(8,128)S(1)} custom-call(bf16[16,16384]{1,0:T(8,128)(2,1)S(1)} %get-tuple-element.10.rows_ref, f32[1,16384]{1,0:T(1,128)S(1)} %get-tuple-element.11.root_ref, bf16[16384,512]{1,0:T(8,128)(2,1)S(1)} %get-tuple-element.12.turned_ref, bf16[16,2048]{1,0:T(8,128)(2,1)S(1)} %outer_sum0.2.refs_0_, ...), custom_call_target="tpu_custom_call" | custom-call | flops 939524096 | bytes 17629184 | tf_op jit(solution)/shard_map/project0/pallas_call | solution.py:28
  38.4 0.8 %collective-permute-done.12.refs_0_ = bf16[16,4096]{1,0:T(8,128)(2,1)S(1)} collective-permute-done((bf16[16,4096]{1,0:T(8,128)(2,1)S(1)}, bf16[16,4096]{1,0:T(8,128)(2,1)S(1)}, u32[]{:S(2)}, u32[]{:S(2)}) %collective-permute-start.12) | collective-permute-done | bytes 131104 | tf_op jit(solution)/shard_map/ppermute | solution.py:207
  39.2 0.8 %project4.2.refs_1_ = f32[16,640]{1,0:T(8,128)S(1)} custom-call(bf16[16,16384]{1,0:T(8,128)(2,1)S(1)} %get-tuple-element.10.rows_ref, f32[1,16384]{1,0:T(1,128)S(1)} %get-tuple-element.11.root_ref, bf16[16384,512]{1,0:T(8,128)(2,1)S(1)} %get-tuple-element.12.turned_ref, bf16[16,4096]{1,0:T(8,128)(2,1)S(1)} %collective-permute-done.12.refs_0_, ...), custom_call_target="tpu_custom_call" | custom-call | flops 67108864 | bytes 17539072 | tf_op jit(solution)/shard_map/project4/pallas_call | solution.py:28
  40.0 0.5 project5.2.refs_1_
  40.4 0.7 collective-permute-done.6.refs_0_
  41.2 0.5 project6.2.own_ref
  41.6 1.2 %collective-permute-done.15.other_ref = f32[16,640]{1,0:T(8,128)S(1)} collective-permute-done((f32[16,640]{1,0:T(8,128)S(1)}, f32[16,640]{1,0:T(8,128)S(1)}, u32[]{:S(2)}, u32[]{:S(2)}) %collective-permute-start.15) | collective-permute-done | bytes 40992 | tf_op jit(solution)/shard_map/ppermute | solution.py:207
  42.9 0.4 solve.1.refs_0_
  43.3 0.7 terms23.3
  44.0 1.0 %collective-permute-start.18 = (bf16[16,4096]{1,0:T(8,128)(2,1)S(1)}, bf16[16,4096]{1,0:T(8,128)(2,1)S(1)}, u32[]{:S(2)}, u32[]{:S(2)}) collective-permute-start(bf16[16,4096]{1,0:T(8,128)(2,1)S(1)} %terms23.3), channel_id=1, source_target_pairs={{0,6},{2,4},{4,2},{6,0},{8,14},{10,12},{12,10},{14,8},{16,22},{18,... | collective-permute-start | bytes 393224 | tf_op jit(solution)/shard_map/ppermute | solution.py:207
  45.0 0.4 terms02.3
  45.3 2.0 %collective-permute-start.24 = (bf16[16,2048]{1,0:T(8,128)(2,1)S(1)}, bf16[16,2048]{1,0:T(8,128)(2,1)S(1)}, u32[]{:S(2)}, u32[]{:S(2)}) collective-permute-start(bf16[16,2048]{1,0:T(8,128)(2,1)S(1)} %terms02.3), channel_id=1, source_target_pairs={{0,4},{2,6},{4,0},{6,2},{8,12},{10,14},{12,8},{14,10},{16,20},{18,... | collective-permute-start | bytes 196616 | tf_op jit(solution)/shard_map/ppermute | solution.py:207
  47.3 0.4 terms01.3
  47.7 0.5 collective-permute-start.23
  48.3 0.4 terms12.3
  48.6 0.7 collective-permute-start.17
  49.4 0.4 terms11.3
  49.7 0.8 %collective-permute-start.16 = (bf16[16,2048]{1,0:T(8,128)(2,1)S(1)}, bf16[16,2048]{1,0:T(8,128)(2,1)S(1)}, u32[]{:S(2)}, u32[]{:S(2)}) collective-permute-start(bf16[16,2048]{1,0:T(8,128)(2,1)S(1)} %terms11.3), channel_id=1, source_target_pairs={{0,2},{2,0},{4,6},{6,4},{8,10},{10,8},{12,14},{14,12},{16,18},{18,... | collective-permute-start | bytes 196616 | tf_op jit(solution)/shard_map/ppermute | solution.py:207
  50.6 0.4 terms00.3.own_ref
  51.0 1.0 %collective-permute-done.24.refs_1_ = bf16[16,2048]{1,0:T(8,128)(2,1)S(1)} collective-permute-done((bf16[16,2048]{1,0:T(8,128)(2,1)S(1)}, bf16[16,2048]{1,0:T(8,128)(2,1)S(1)}, u32[]{:S(2)}, u32[]{:S(2)}) %collective-permute-start.24) | collective-permute-done | bytes 65568 | tf_op jit(solution)/shard_map/ppermute | solution.py:207
  51.9 0.7 collective-permute-done.23.refs_0_
  52.6 0.5 collective-permute-start.25
  53.2 0.4 terms10.3.own_ref
  53.5 0.5 collective-permute-done.16.refs_0_
  54.1 1.7 %collective-permute-start.19 = (bf16[16,2048]{1,0:T(8,128)(2,1)S(1)}, bf16[16,2048]{1,0:T(8,128)(2,1)S(1)}, u32[]{:S(2)}, u32[]{:S(2)}) collective-permute-start(bf16[16,2048]{1,0:T(8,128)(2,1)S(1)} %inner_sum1.3.own_ref), channel_id=1, source_target_pairs={{0,8},{1,17},{2,10},{3,19},{4,12},{5,21},{6,14},{7,23},{8,0},{9,25... | collective-permute-start | bytes 196616 | tf_op jit(solution)/shard_map/ppermute | solution.py:213
  55.8 1.2 %collective-permute-done.25.other_ref = bf16[16,2048]{1,0:T(8,128)(2,1)S(1)} collective-permute-done((bf16[16,2048]{1,0:T(8,128)(2,1)S(1)}, bf16[16,2048]{1,0:T(8,128)(2,1)S(1)}, u32[]{:S(2)}, u32[]{:S(2)}) %collective-permute-start.25) | collective-permute-done | bytes 65568 | tf_op jit(solution)/shard_map/ppermute | solution.py:213
  57.1 1.3 %collective-permute-start.26 = (bf16[16,2048]{1,0:T(8,128)(2,1)S(1)}, bf16[16,2048]{1,0:T(8,128)(2,1)S(1)}, u32[]{:S(2)}, u32[]{:S(2)}) collective-permute-start(bf16[16,2048]{1,0:T(8,128)(2,1)S(1)} %pair_sum0.3.own_ref), channel_id=1, source_target_pairs={{0,16},{1,9},{2,18},{3,11},{4,20},{5,13},{6,22},{7,15},{8,24},{9,1... | collective-permute-start | bytes 196616 | tf_op jit(solution)/shard_map/ppermute | solution.py:213
  58.6 2.0 %collective-permute-start.20 = (bf16[16,2048]{1,0:T(8,128)(2,1)S(1)}, bf16[16,2048]{1,0:T(8,128)(2,1)S(1)}, u32[]{:S(2)}, u32[]{:S(2)}) collective-permute-start(bf16[16,2048]{1,0:T(8,128)(2,1)S(1)} %pair_sum1.3.own_ref), channel_id=1, source_target_pairs={{0,16},{1,9},{2,18},{3,11},{4,20},{5,13},{6,22},{7,15},{8,24},{9,1... | collective-permute-start | bytes 196616 | tf_op jit(solution)/shard_map/ppermute | solution.py:213
  60.6 2.1 %collective-permute-done.26.other_ref = bf16[16,2048]{1,0:T(8,128)(2,1)S(1)} collective-permute-done((bf16[16,2048]{1,0:T(8,128)(2,1)S(1)}, bf16[16,2048]{1,0:T(8,128)(2,1)S(1)}, u32[]{:S(2)}, u32[]{:S(2)}) %collective-permute-start.26) | collective-permute-done | bytes 65568 | tf_op jit(solution)/shard_map/ppermute | solution.py:213
  62.9 0.9 %collective-permute-start.29 = (bf16[16,2048]{1,0:T(8,128)(2,1)S(1)}, bf16[16,2048]{1,0:T(8,128)(2,1)S(1)}, u32[]{:S(2)}, u32[]{:S(2)}) collective-permute-start(bf16[16,2048]{1,0:T(8,128)(2,1)S(1)} %outer_sum0.3.refs_0_), channel_id=1, source_target_pairs={{0,2},{2,0},{4,6},{6,4},{8,10},{10,8},{12,14},{14,12},{16,18},{18,... | collective-permute-start | bytes 196616 | tf_op jit(solution)/shard_map/ppermute | solution.py:207
  63.9 3.3 %collective-permute-start.27 = (bf16[16,4096]{1,0:T(8,128)(2,1)S(1)}, bf16[16,4096]{1,0:T(8,128)(2,1)S(1)}, u32[]{:S(2)}, u32[]{:S(2)}) collective-permute-start(bf16[16,4096]{1,0:T(8,128)(2,1)S(1)} %stack.3), channel_id=1, source_target_pairs={{0,6},{2,4},{4,2},{6,0},{8,14},{10,12},{12,10},{14,8},{16,22},{18,... | collective-permute-start | bytes 393224 | tf_op jit(solution)/shard_map/ppermute | solution.py:207
  67.2 0.6 collective-permute-start.21
  67.9 1.5 %project0.3.refs_1_ = f32[16,640]{1,0:T(8,128)S(1)} custom-call(bf16[16,16384]{1,0:T(8,128)(2,1)S(1)} %get-tuple-element.10.rows_ref, f32[1,16384]{1,0:T(1,128)S(1)} %get-tuple-element.11.root_ref, bf16[16384,512]{1,0:T(8,128)(2,1)S(1)} %get-tuple-element.12.turned_ref, bf16[16,2048]{1,0:T(8,128)(2,1)S(1)} %outer_sum0.3.refs_0_, ...), custom_call_target="tpu_custom_call" | custom-call | flops 939524096 | bytes 17629184 | tf_op jit(solution)/shard_map/project0/pallas_call | solution.py:28
  69.3 0.8 %collective-permute-done.27.refs_0_.refs_4_ = bf16[16,4096]{1,0:T(8,128)(2,1)S(1)} collective-permute-done((bf16[16,4096]{1,0:T(8,128)(2,1)S(1)}, bf16[16,4096]{1,0:T(8,128)(2,1)S(1)}, u32[]{:S(2)}, u32[]{:S(2)}) %collective-permute-start.27) | collective-permute-done | bytes 131104 | tf_op jit(solution)/shard_map/ppermute | solution.py:207
  70.2 0.8 %project4.3.refs_1_ = f32[16,640]{1,0:T(8,128)S(1)} custom-call(bf16[16,16384]{1,0:T(8,128)(2,1)S(1)} %get-tuple-element.10.rows_ref, f32[1,16384]{1,0:T(1,128)S(1)} %get-tuple-element.11.root_ref, bf16[16384,512]{1,0:T(8,128)(2,1)S(1)} %get-tuple-element.12.turned_ref, bf16[16,4096]{1,0:T(8,128)(2,1)S(1)} %collective-permute-done.27.refs_0_.refs_4_, ...), custom_call_target="tpu_custom_call" | custom-call | flops 67108864 | bytes 17539072 | tf_op jit(solution)/shard_map/project4/pallas_call | solution.py:28
  70.9 0.5 collective-permute-done.22.refs_0_.refs_5_
  71.5 0.5 project5.3.refs_1_
  71.9 0.5 project6.3.own_ref
  72.4 1.2 %collective-permute-done.30.other_ref = f32[16,640]{1,0:T(8,128)S(1)} collective-permute-done((f32[16,640]{1,0:T(8,128)S(1)}, f32[16,640]{1,0:T(8,128)S(1)}, u32[]{:S(2)}, u32[]{:S(2)}) %collective-permute-start.30) | collective-permute-done | bytes 40992 | tf_op jit(solution)/shard_map/ppermute | solution.py:207
  73.6 1.6 %finish.1 = (f32[16,16384]{1,0:T(8,128)}, f32[16,512]{1,0:T(8,128)}) custom-call(f32[16,640]{1,0:T(8,128)S(1)} %project6.3.own_ref, f32[16,640]{1,0:T(8,128)S(1)} %collective-permute-done.30.other_ref, f32[1,16384]{1,0:T(1,128)S(1)} %get-tuple-element.11.root_ref, bf16[16,2048]{1,0:T(8,128)(2,1)S(1)} %outer_sum0.3.refs_0_, ...), custom_call_target="tpu_custom_call" | custom-call | tf_op jit(solution)/shard_map/finish/pallas_call | solution.py:343
  (37 shorter events, 1.8 us)
Async XLA Ops:
  8.1 1.4 %collective-permute-start = (bf16[16,512]{1,0:T(8,128)(2,1)S(1)}, bf16[16,512]{1,0:T(8,128)(2,1)S(1)}, u32[]{:S(2)}, u32[]{:S(2)}) collective-permute-start(bf16[16,512]{1,0:T(8,128)(2,1)S(1)} %get-tuple-element.15.refs_0_), channel_id=1, source_target_pairs={{0,1},{1,0},{2,3},{3,2},{4,5},{5,4},{6,7},{7,6},{8,9},{9,8},{10,11... | collective-permute-start | bytes 49160 | tf_op jit(solution)/shard_map/ppermute | solution.py:207
  10.1 9.8 %collective-permute-start.3 = (bf16[16,4096]{1,0:T(8,128)(2,1)S(1)}, bf16[16,4096]{1,0:T(8,128)(2,1)S(1)}, u32[]{:S(2)}, u32[]{:S(2)}) collective-permute-start(bf16[16,4096]{1,0:T(8,128)(2,1)S(1)} %terms23.2), channel_id=1, source_target_pairs={{0,6},{2,4},{4,2},{6,0},{8,14},{10,12},{12,10},{14,8},{16,22},{18,... | collective-permute-start | bytes 393224 | tf_op jit(solution)/shard_map/ppermute | solution.py:207
  14.3 5.6 %collective-permute-start.9 = (bf16[16,2048]{1,0:T(8,128)(2,1)S(1)}, bf16[16,2048]{1,0:T(8,128)(2,1)S(1)}, u32[]{:S(2)}, u32[]{:S(2)}) collective-permute-start(bf16[16,2048]{1,0:T(8,128)(2,1)S(1)} %terms02.2), channel_id=1, source_target_pairs={{0,4},{2,6},{4,0},{6,2},{8,12},{10,14},{12,8},{14,10},{16,20},{18,... | collective-permute-start | bytes 196616 | tf_op jit(solution)/shard_map/ppermute | solution.py:207
  15.2 4.7 %collective-permute-start.8 = (bf16[16,2048]{1,0:T(8,128)(2,1)S(1)}, bf16[16,2048]{1,0:T(8,128)(2,1)S(1)}, u32[]{:S(2)}, u32[]{:S(2)}) collective-permute-start(bf16[16,2048]{1,0:T(8,128)(2,1)S(1)} %terms01.2), channel_id=1, source_target_pairs={{0,2},{2,0},{4,6},{6,4},{8,10},{10,8},{12,14},{14,12},{16,18},{18,... | collective-permute-start | bytes 196616 | tf_op jit(solution)/shard_map/ppermute | solution.py:207
  15.7 6.4 %collective-permute-start.2 = (bf16[16,2048]{1,0:T(8,128)(2,1)S(1)}, bf16[16,2048]{1,0:T(8,128)(2,1)S(1)}, u32[]{:S(2)}, u32[]{:S(2)}) collective-permute-start(bf16[16,2048]{1,0:T(8,128)(2,1)S(1)} %terms12.2), channel_id=1, source_target_pairs={{0,4},{2,6},{4,0},{6,2},{8,12},{10,14},{12,8},{14,10},{16,20},{18,... | collective-permute-start | bytes 196616 | tf_op jit(solution)/shard_map/ppermute | solution.py:207
  18.1 4.3 %collective-permute-start.1 = (bf16[16,2048]{1,0:T(8,128)(2,1)S(1)}, bf16[16,2048]{1,0:T(8,128)(2,1)S(1)}, u32[]{:S(2)}, u32[]{:S(2)}) collective-permute-start(bf16[16,2048]{1,0:T(8,128)(2,1)S(1)} %terms11.2), channel_id=1, source_target_pairs={{0,2},{2,0},{4,6},{6,4},{8,10},{10,8},{12,14},{14,12},{16,18},{18,... | collective-permute-start | bytes 196616 | tf_op jit(solution)/shard_map/ppermute | solution.py:207
  20.0 4.3 %collective-permute-start.10 = (bf16[16,2048]{1,0:T(8,128)(2,1)S(1)}, bf16[16,2048]{1,0:T(8,128)(2,1)S(1)}, u32[]{:S(2)}, u32[]{:S(2)}) collective-permute-start(bf16[16,2048]{1,0:T(8,128)(2,1)S(1)} %inner_sum0.2.own_ref), channel_id=1, source_target_pairs={{0,8},{1,17},{2,10},{3,19},{4,12},{5,21},{6,14},{7,23},{8,0},{9,25... | collective-permute-start | bytes 196616 | tf_op jit(solution)/shard_map/ppermute | solution.py:213
  22.4 5.5 %collective-permute-start.4 = (bf16[16,2048]{1,0:T(8,128)(2,1)S(1)}, bf16[16,2048]{1,0:T(8,128)(2,1)S(1)}, u32[]{:S(2)}, u32[]{:S(2)}) collective-permute-start(bf16[16,2048]{1,0:T(8,128)(2,1)S(1)} %inner_sum1.2.own_ref), channel_id=1, source_target_pairs={{0,8},{1,17},{2,10},{3,19},{4,12},{5,21},{6,14},{7,23},{8,0},{9,25... | collective-permute-start | bytes 196616 | tf_op jit(solution)/shard_map/ppermute | solution.py:213
  24.4 5.3 %collective-permute-start.11 = (bf16[16,2048]{1,0:T(8,128)(2,1)S(1)}, bf16[16,2048]{1,0:T(8,128)(2,1)S(1)}, u32[]{:S(2)}, u32[]{:S(2)}) collective-permute-start(bf16[16,2048]{1,0:T(8,128)(2,1)S(1)} %pair_sum0.2.own_ref), channel_id=1, source_target_pairs={{0,16},{1,9},{2,18},{3,11},{4,20},{5,13},{6,22},{7,15},{8,24},{9,1... | collective-permute-start | bytes 196616 | tf_op jit(solution)/shard_map/ppermute | solution.py:213
  27.9 5.2 %collective-permute-start.5 = (bf16[16,2048]{1,0:T(8,128)(2,1)S(1)}, bf16[16,2048]{1,0:T(8,128)(2,1)S(1)}, u32[]{:S(2)}, u32[]{:S(2)}) collective-permute-start(bf16[16,2048]{1,0:T(8,128)(2,1)S(1)} %pair_sum1.2.own_ref), channel_id=1, source_target_pairs={{0,16},{1,9},{2,18},{3,11},{4,20},{5,13},{6,22},{7,15},{8,24},{9,1... | collective-permute-start | bytes 196616 | tf_op jit(solution)/shard_map/ppermute | solution.py:213
  29.7 7.2 %collective-permute-start.13 = (bf16[16,2048]{1,0:T(8,128)(2,1)S(1)}, bf16[16,2048]{1,0:T(8,128)(2,1)S(1)}, u32[]{:S(2)}, u32[]{:S(2)}) collective-permute-start(bf16[16,2048]{1,0:T(8,128)(2,1)S(1)} %outer_sum0.2.refs_0_), channel_id=1, source_target_pairs={{0,4},{2,6},{4,0},{6,2},{8,12},{10,14},{12,8},{14,10},{16,20},{18,... | collective-permute-start | bytes 196616 | tf_op jit(solution)/shard_map/ppermute | solution.py:207
  31.3 5.6 %collective-permute-start.14 = (bf16[16,2048]{1,0:T(8,128)(2,1)S(1)}, bf16[16,2048]{1,0:T(8,128)(2,1)S(1)}, u32[]{:S(2)}, u32[]{:S(2)}) collective-permute-start(bf16[16,2048]{1,0:T(8,128)(2,1)S(1)} %outer_sum0.2.refs_0_), channel_id=1, source_target_pairs={{0,2},{2,0},{4,6},{6,4},{8,10},{10,8},{12,14},{14,12},{16,18},{18,... | collective-permute-start | bytes 196616 | tf_op jit(solution)/shard_map/ppermute | solution.py:207
  33.2 6.0 %collective-permute-start.12 = (bf16[16,4096]{1,0:T(8,128)(2,1)S(1)}, bf16[16,4096]{1,0:T(8,128)(2,1)S(1)}, u32[]{:S(2)}, u32[]{:S(2)}) collective-permute-start(bf16[16,4096]{1,0:T(8,128)(2,1)S(1)} %stack.2), channel_id=1, source_target_pairs={{0,6},{2,4},{4,2},{6,0},{8,14},{10,12},{12,10},{14,8},{16,22},{18,... | collective-permute-start | bytes 393224 | tf_op jit(solution)/shard_map/ppermute | solution.py:207
  34.9 5.0 %collective-permute-start.7 = (bf16[16,2048]{1,0:T(8,128)(2,1)S(1)}, bf16[16,2048]{1,0:T(8,128)(2,1)S(1)}, u32[]{:S(2)}, u32[]{:S(2)}) collective-permute-start(bf16[16,2048]{1,0:T(8,128)(2,1)S(1)} %outer_sum1.2.refs_1_.refs_3_), channel_id=1, source_target_pairs={{0,4},{2,6},{4,0},{6,2},{8,12},{10,14},{12,8},{14,10},{16,20},{18,... | collective-permute-start | bytes 196616 | tf_op jit(solution)/shard_map/ppermute | solution.py:207
  36.9 4.3 %collective-permute-start.6 = (bf16[16,2048]{1,0:T(8,128)(2,1)S(1)}, bf16[16,2048]{1,0:T(8,128)(2,1)S(1)}, u32[]{:S(2)}, u32[]{:S(2)}) collective-permute-start(bf16[16,2048]{1,0:T(8,128)(2,1)S(1)} %outer_sum1.2.refs_1_.refs_3_), channel_id=1, source_target_pairs={{0,2},{2,0},{4,6},{6,4},{8,10},{10,8},{12,14},{14,12},{16,18},{18,... | collective-permute-start | bytes 196616 | tf_op jit(solution)/shard_map/ppermute | solution.py:207
  41.6 1.2 %collective-permute-start.15 = (f32[16,640]{1,0:T(8,128)S(1)}, f32[16,640]{1,0:T(8,128)S(1)}, u32[]{:S(2)}, u32[]{:S(2)}) collective-permute-start(f32[16,640]{1,0:T(8,128)S(1)} %project6.2.own_ref), channel_id=1, source_target_pairs={{0,1},{1,0},{2,3},{3,2},{4,5},{5,4},{6,7},{7,6},{8,9},{9,8},{10,11... | collective-permute-start | bytes 122888 | tf_op jit(solution)/shard_map/ppermute | solution.py:207
  44.0 8.6 %collective-permute-start.18 = (bf16[16,4096]{1,0:T(8,128)(2,1)S(1)}, bf16[16,4096]{1,0:T(8,128)(2,1)S(1)}, u32[]{:S(2)}, u32[]{:S(2)}) collective-permute-start(bf16[16,4096]{1,0:T(8,128)(2,1)S(1)} %terms23.3), channel_id=1, source_target_pairs={{0,6},{2,4},{4,2},{6,0},{8,14},{10,12},{12,10},{14,8},{16,22},{18,... | collective-permute-start | bytes 393224 | tf_op jit(solution)/shard_map/ppermute | solution.py:207
  45.3 6.6 %collective-permute-start.24 = (bf16[16,2048]{1,0:T(8,128)(2,1)S(1)}, bf16[16,2048]{1,0:T(8,128)(2,1)S(1)}, u32[]{:S(2)}, u32[]{:S(2)}) collective-permute-start(bf16[16,2048]{1,0:T(8,128)(2,1)S(1)} %terms02.3), channel_id=1, source_target_pairs={{0,4},{2,6},{4,0},{6,2},{8,12},{10,14},{12,8},{14,10},{16,20},{18,... | collective-permute-start | bytes 196616 | tf_op jit(solution)/shard_map/ppermute | solution.py:207
  47.7 4.9 %collective-permute-start.23 = (bf16[16,2048]{1,0:T(8,128)(2,1)S(1)}, bf16[16,2048]{1,0:T(8,128)(2,1)S(1)}, u32[]{:S(2)}, u32[]{:S(2)}) collective-permute-start(bf16[16,2048]{1,0:T(8,128)(2,1)S(1)} %terms01.3), channel_id=1, source_target_pairs={{0,2},{2,0},{4,6},{6,4},{8,10},{10,8},{12,14},{14,12},{16,18},{18,... | collective-permute-start | bytes 196616 | tf_op jit(solution)/shard_map/ppermute | solution.py:207
  48.6 4.9 %collective-permute-start.17 = (bf16[16,2048]{1,0:T(8,128)(2,1)S(1)}, bf16[16,2048]{1,0:T(8,128)(2,1)S(1)}, u32[]{:S(2)}, u32[]{:S(2)}) collective-permute-start(bf16[16,2048]{1,0:T(8,128)(2,1)S(1)} %terms12.3), channel_id=1, source_target_pairs={{0,4},{2,6},{4,0},{6,2},{8,12},{10,14},{12,8},{14,10},{16,20},{18,... | collective-permute-start | bytes 196616 | tf_op jit(solution)/shard_map/ppermute | solution.py:207
  49.7 4.3 %collective-permute-start.16 = (bf16[16,2048]{1,0:T(8,128)(2,1)S(1)}, bf16[16,2048]{1,0:T(8,128)(2,1)S(1)}, u32[]{:S(2)}, u32[]{:S(2)}) collective-permute-start(bf16[16,2048]{1,0:T(8,128)(2,1)S(1)} %terms11.3), channel_id=1, source_target_pairs={{0,2},{2,0},{4,6},{6,4},{8,10},{10,8},{12,14},{14,12},{16,18},{18,... | collective-permute-start | bytes 196616 | tf_op jit(solution)/shard_map/ppermute | solution.py:207
  52.6 4.4 %collective-permute-start.25 = (bf16[16,2048]{1,0:T(8,128)(2,1)S(1)}, bf16[16,2048]{1,0:T(8,128)(2,1)S(1)}, u32[]{:S(2)}, u32[]{:S(2)}) collective-permute-start(bf16[16,2048]{1,0:T(8,128)(2,1)S(1)} %inner_sum0.3.own_ref), channel_id=1, source_target_pairs={{0,8},{1,17},{2,10},{3,19},{4,12},{5,21},{6,14},{7,23},{8,0},{9,25... | collective-permute-start | bytes 196616 | tf_op jit(solution)/shard_map/ppermute | solution.py:213
  54.1 4.6 %collective-permute-start.19 = (bf16[16,2048]{1,0:T(8,128)(2,1)S(1)}, bf16[16,2048]{1,0:T(8,128)(2,1)S(1)}, u32[]{:S(2)}, u32[]{:S(2)}) collective-permute-start(bf16[16,2048]{1,0:T(8,128)(2,1)S(1)} %inner_sum1.3.own_ref), channel_id=1, source_target_pairs={{0,8},{1,17},{2,10},{3,19},{4,12},{5,21},{6,14},{7,23},{8,0},{9,25... | collective-permute-start | bytes 196616 | tf_op jit(solution)/shard_map/ppermute | solution.py:213
  57.1 5.7 %collective-permute-start.26 = (bf16[16,2048]{1,0:T(8,128)(2,1)S(1)}, bf16[16,2048]{1,0:T(8,128)(2,1)S(1)}, u32[]{:S(2)}, u32[]{:S(2)}) collective-permute-start(bf16[16,2048]{1,0:T(8,128)(2,1)S(1)} %pair_sum0.3.own_ref), channel_id=1, source_target_pairs={{0,16},{1,9},{2,18},{3,11},{4,20},{5,13},{6,22},{7,15},{8,24},{9,1... | collective-permute-start | bytes 196616 | tf_op jit(solution)/shard_map/ppermute | solution.py:213
  58.6 5.2 %collective-permute-start.20 = (bf16[16,2048]{1,0:T(8,128)(2,1)S(1)}, bf16[16,2048]{1,0:T(8,128)(2,1)S(1)}, u32[]{:S(2)}, u32[]{:S(2)}) collective-permute-start(bf16[16,2048]{1,0:T(8,128)(2,1)S(1)} %pair_sum1.3.own_ref), channel_id=1, source_target_pairs={{0,16},{1,9},{2,18},{3,11},{4,20},{5,13},{6,22},{7,15},{8,24},{9,1... | collective-permute-start | bytes 196616 | tf_op jit(solution)/shard_map/ppermute | solution.py:213
  62.8 5.0 %collective-permute-start.28 = (bf16[16,2048]{1,0:T(8,128)(2,1)S(1)}, bf16[16,2048]{1,0:T(8,128)(2,1)S(1)}, u32[]{:S(2)}, u32[]{:S(2)}) collective-permute-start(bf16[16,2048]{1,0:T(8,128)(2,1)S(1)} %outer_sum0.3.refs_0_), channel_id=1, source_target_pairs={{0,4},{2,6},{4,0},{6,2},{8,12},{10,14},{12,8},{14,10},{16,20},{18,... | collective-permute-start | bytes 196616 | tf_op jit(solution)/shard_map/ppermute | solution.py:207
  62.9 4.9 %collective-permute-start.29 = (bf16[16,2048]{1,0:T(8,128)(2,1)S(1)}, bf16[16,2048]{1,0:T(8,128)(2,1)S(1)}, u32[]{:S(2)}, u32[]{:S(2)}) collective-permute-start(bf16[16,2048]{1,0:T(8,128)(2,1)S(1)} %outer_sum0.3.refs_0_), channel_id=1, source_target_pairs={{0,2},{2,0},{4,6},{6,4},{8,10},{10,8},{12,14},{14,12},{16,18},{18,... | collective-permute-start | bytes 196616 | tf_op jit(solution)/shard_map/ppermute | solution.py:207
  63.9 6.2 %collective-permute-start.27 = (bf16[16,4096]{1,0:T(8,128)(2,1)S(1)}, bf16[16,4096]{1,0:T(8,128)(2,1)S(1)}, u32[]{:S(2)}, u32[]{:S(2)}) collective-permute-start(bf16[16,4096]{1,0:T(8,128)(2,1)S(1)} %stack.3), channel_id=1, source_target_pairs={{0,6},{2,4},{4,2},{6,0},{8,14},{10,12},{12,10},{14,8},{16,22},{18,... | collective-permute-start | bytes 393224 | tf_op jit(solution)/shard_map/ppermute | solution.py:207
  67.2 4.3 %collective-permute-start.22 = (bf16[16,2048]{1,0:T(8,128)(2,1)S(1)}, bf16[16,2048]{1,0:T(8,128)(2,1)S(1)}, u32[]{:S(2)}, u32[]{:S(2)}) collective-permute-start(bf16[16,2048]{1,0:T(8,128)(2,1)S(1)} %outer_sum1.3.refs_1_.refs_3_), channel_id=1, source_target_pairs={{0,4},{2,6},{4,0},{6,2},{8,12},{10,14},{12,8},{14,10},{16,20},{18,... | collective-permute-start | bytes 196616 | tf_op jit(solution)/shard_map/ppermute | solution.py:207
  67.2 4.7 %collective-permute-start.21 = (bf16[16,2048]{1,0:T(8,128)(2,1)S(1)}, bf16[16,2048]{1,0:T(8,128)(2,1)S(1)}, u32[]{:S(2)}, u32[]{:S(2)}) collective-permute-start(bf16[16,2048]{1,0:T(8,128)(2,1)S(1)} %outer_sum1.3.refs_1_.refs_3_), channel_id=1, source_target_pairs={{0,2},{2,0},{4,6},{6,4},{8,10},{10,8},{12,14},{14,12},{16,18},{18,... | collective-permute-start | bytes 196616 | tf_op jit(solution)/shard_map/ppermute | solution.py:207
  72.4 1.2 %collective-permute-start.30 = (f32[16,640]{1,0:T(8,128)S(1)}, f32[16,640]{1,0:T(8,128)S(1)}, u32[]{:S(2)}, u32[]{:S(2)}) collective-permute-start(f32[16,640]{1,0:T(8,128)S(1)} %project6.3.own_ref), channel_id=1, source_target_pairs={{0,1},{1,0},{2,3},{3,2},{4,5},{5,4},{6,7},{7,6},{8,9},{9,8},{10,11... | collective-permute-start | bytes 122888 | tf_op jit(solution)/shard_map/ppermute | solution.py:207

commit v2 on v1

--- a/solution.py
+++ b/solution.py
@@ -216,14 +216,14 @@
 def sum_over_samples(sample_rows, kept, centre, root, inner):
     count, near, far = 4 * inner, inner, 2 * inner
     x, y, diagonal = 1, 2, 3
-    across = swap(terms(sample_rows, kept, centre, (diagonal, None), inner), "samp", count, diagonal)
+    across = [swap(terms(sample_rows, kept, centre, (t, None), inner), "samp", count, t) for t in (diagonal, y)]
     pieces = {}
     for h in range(HALVES):
-        received = [swap(terms(sample_rows, kept, centre, (t, h), inner), "samp", count, t) for t in (x, y)]
+        beside = swap(terms(sample_rows, kept, centre, (x, h), inner), "samp", count, x)
         own = terms(sample_rows, kept, centre, (0, h), inner, jnp.float32)
         piece = shape(own.shape)
         body = functools.partial(inner_sum_body, h)
-        plane = call(body, piece, (own, *received, across), own.size * inner, "inner_sum%d" % h)
+        plane = call(body, piece, (own, beside, *across[::-1]), own.size * inner, "inner_sum%d" % h)
         pair = call(pair_sum_body, piece, (plane, swap_across(plane, count, (near, far))), own.size, "pair_sum%d" % h)
         body = functools.partial(outer_sum_body, (0, h), inner)
         whole = call(body, piece, (root, pair, swap_across(pair, count, (far, near))), own.size, "outer_sum%d" % h)

time: 75.5 us -> 77.2 us (1.023)
  waiting for transfers between devices: 14.8 us -> 17.2 us
    ppermute x23 -> x21, waiting for transfers between devices: 8.66 us -> 10.6 us  [swap(): return lax.ppermute(x, axis, [(d, d ^ turn) for d in range(size)])]
    ppermute x23 -> x21, starting transfers between devices: 24.5 us -> 23.9 us  [swap(): return lax.ppermute(x, axis, [(d, d ^ turn) for d in range(size)])]
    pallas_call x37 -> x35, Pallas kernels: 13 us -> 12.8 us  [call(): pl.pallas_call(body, out_shape=out, in_specs=[HERE] * len(operands), out_...]
  transfers between devices with their start and end apart: 31 -> 29, of which waited for: 19 -> 16; matrix products, arithmetic and copies ran while one was open for 0% -> 0% of each run, Pallas kernels for 14% -> 13%
where the time goes in v2:
time: 77.2 us; the launch traced here: 77.1 us
  starting transfers between devices  37.1 us (48%)
  Pallas kernels  21.9 us (28%)
  waiting for transfers between devices  17.2 us (22%)
  between operations  0.91 us (1%)
    ppermute x21, starting transfers between devices, swap(): return lax.ppermute(x, axis, [(d, d ^ turn) for d in range(size)])  23.9 us
    ppermute x8, starting transfers between devices, swap_across(): return lax.ppermute(x, ('samp', 'var'), pairs)  13.2 us
    pallas_call x35, Pallas kernels, call(): pl.pallas_call(body, out_shape=out, in_specs=[HERE] * len(operands), out_...  12.8 us
    ppermute x21, waiting for transfers between devices, swap(): return lax.ppermute(x, axis, [(d, d ^ turn) for d in range(size)])  10.6 us
    pallas_call x1, Pallas kernels, load(): pl.pallas_call(functools.partial(load_body, width, 8), in_specs=[anywhere...  7.5 us
    ppermute x8, waiting for transfers between devices, swap_across(): return lax.ppermute(x, ('samp', 'var'), pairs)  6.65 us
    pallas_call x1, Pallas kernels, finish(): pl.pallas_call(functools.partial(finish_body, scaling, order, inner), out...  1.56 us
  transfers between devices with their start and end apart: 29, of which 16 were waited for; matrix products, arithmetic and copies ran while one was open for 0% of the time, Pallas kernels for 13%

profile of v2, /device:TPU:0, one launch (start us, length us, event | category | flops | bytes accessed | tf_op | source)
XLA Modules:
  0.0 77.1 jit_solution(15954604368645778269)
XLA Ops:
  0.6 7.5 %load.1 = (bf16[512,16384]{1,0:T(8,128)(2,1)S(1)}, bf16[16384,512]{1,0:T(8,128)(2,1)S(1)}, bf16[16,512]{1,0:T(8,128)(2,1)S(1)}, f32[1,16384]{1,0:T(1,128)S(1)}, ...) custom-call(bf16[512,16384]{1,0:T(8,128)(2,1)} %g_ref.1, f32[128,128]{1,0:T(8,128)} %bitcast.5, f32[16,16384]{1,0:T(8,128)} %bitcast.4), custom_call_target="tpu_custom_call" | custom-call | tf_op jit(solution)/shard_map/load/pallas_call | solution.py:129
  8.1 0.5 collective-permute-start
  8.7 0.8 %collective-permute-done.refs_1_ = bf16[16,512]{1,0:T(8,128)(2,1)S(1)} collective-permute-done((bf16[16,512]{1,0:T(8,128)(2,1)S(1)}, bf16[16,512]{1,0:T(8,128)(2,1)S(1)}, u32[]{:S(2)}, u32[]{:S(2)}) %collective-permute-start) | collective-permute-done | bytes 16416 | tf_op jit(solution)/shard_map/ppermute | solution.py:207
  9.5 0.7 terms23.2
  10.1 3.8 %collective-permute-start.3 = (bf16[16,4096]{1,0:T(8,128)(2,1)S(1)}, bf16[16,4096]{1,0:T(8,128)(2,1)S(1)}, u32[]{:S(2)}, u32[]{:S(2)}) collective-permute-start(bf16[16,4096]{1,0:T(8,128)(2,1)S(1)} %terms23.2), channel_id=1, source_target_pairs={{0,6},{2,4},{4,2},{6,0},{8,14},{10,12},{12,10},{14,8},{16,22},{18,... | collective-permute-start | bytes 393224 | tf_op jit(solution)/shard_map/ppermute | solution.py:207
  13.9 0.7 terms22.2
  14.6 0.5 collective-permute-start.2
  15.1 0.4 terms01.2
  15.6 0.4 terms11.2
  16.0 2.0 %collective-permute-start.1 = (bf16[16,2048]{1,0:T(8,128)(2,1)S(1)}, bf16[16,2048]{1,0:T(8,128)(2,1)S(1)}, u32[]{:S(2)}, u32[]{:S(2)}) collective-permute-start(bf16[16,2048]{1,0:T(8,128)(2,1)S(1)} %terms11.2), channel_id=1, source_target_pairs={{0,2},{2,0},{4,6},{6,4},{8,10},{10,8},{12,14},{14,12},{16,18},{18,... | collective-permute-start | bytes 196616 | tf_op jit(solution)/shard_map/ppermute | solution.py:207
  17.9 0.4 terms00.2.own_ref
  18.3 1.8 %collective-permute-done.8.refs_0_ = bf16[16,2048]{1,0:T(8,128)(2,1)S(1)} collective-permute-done((bf16[16,2048]{1,0:T(8,128)(2,1)S(1)}, bf16[16,2048]{1,0:T(8,128)(2,1)S(1)}, u32[]{:S(2)}, u32[]{:S(2)}) %collective-permute-start.8) | collective-permute-done | bytes 65568 | tf_op jit(solution)/shard_map/ppermute | solution.py:207
  20.1 0.4 collective-permute-done.2.refs_1_
  20.6 1.8 %collective-permute-start.9 = (bf16[16,2048]{1,0:T(8,128)(2,1)S(1)}, bf16[16,2048]{1,0:T(8,128)(2,1)S(1)}, u32[]{:S(2)}, u32[]{:S(2)}) collective-permute-start(bf16[16,2048]{1,0:T(8,128)(2,1)S(1)} %inner_sum0.2.own_ref), channel_id=1, source_target_pairs={{0,8},{1,17},{2,10},{3,19},{4,12},{5,21},{6,14},{7,23},{8,0},{9,25... | collective-permute-start | bytes 196616 | tf_op jit(solution)/shard_map/ppermute | solution.py:213
  22.5 0.4 terms10.2.own_ref
  22.9 0.3 collective-permute-start.4
  23.2 2.4 %collective-permute-done.9.other_ref = bf16[16,2048]{1,0:T(8,128)(2,1)S(1)} collective-permute-done((bf16[16,2048]{1,0:T(8,128)(2,1)S(1)}, bf16[16,2048]{1,0:T(8,128)(2,1)S(1)}, u32[]{:S(2)}, u32[]{:S(2)}) %collective-permute-start.9) | collective-permute-done | bytes 65568 | tf_op jit(solution)/shard_map/ppermute | solution.py:213
  25.6 2.2 %collective-permute-start.10 = (bf16[16,2048]{1,0:T(8,128)(2,1)S(1)}, bf16[16,2048]{1,0:T(8,128)(2,1)S(1)}, u32[]{:S(2)}, u32[]{:S(2)}) collective-permute-start(bf16[16,2048]{1,0:T(8,128)(2,1)S(1)} %pair_sum0.2.own_ref), channel_id=1, source_target_pairs={{0,16},{1,9},{2,18},{3,11},{4,20},{5,13},{6,22},{7,15},{8,24},{9,1... | collective-permute-start | bytes 196616 | tf_op jit(solution)/shard_map/ppermute | solution.py:213
  27.8 0.1 collective-permute-done.4.other_ref
  28.0 2.2 %collective-permute-start.5 = (bf16[16,2048]{1,0:T(8,128)(2,1)S(1)}, bf16[16,2048]{1,0:T(8,128)(2,1)S(1)}, u32[]{:S(2)}, u32[]{:S(2)}) collective-permute-start(bf16[16,2048]{1,0:T(8,128)(2,1)S(1)} %pair_sum1.2.own_ref), channel_id=1, source_target_pairs={{0,16},{1,9},{2,18},{3,11},{4,20},{5,13},{6,22},{7,15},{8,24},{9,1... | collective-permute-start | bytes 196616 | tf_op jit(solution)/shard_map/ppermute | solution.py:213
  30.1 0.8 collective-permute-done.10.other_ref
  31.0 1.8 %collective-permute-start.12 = (bf16[16,2048]{1,0:T(8,128)(2,1)S(1)}, bf16[16,2048]{1,0:T(8,128)(2,1)S(1)}, u32[]{:S(2)}, u32[]{:S(2)}) collective-permute-start(bf16[16,2048]{1,0:T(8,128)(2,1)S(1)} %outer_sum0.2.refs_0_), channel_id=1, source_target_pairs={{0,4},{2,6},{4,0},{6,2},{8,12},{10,14},{12,8},{14,10},{16,20},{18,... | collective-permute-start | bytes 196616 | tf_op jit(solution)/shard_map/ppermute | solution.py:207
  32.7 1.3 %collective-permute-start.13 = (bf16[16,2048]{1,0:T(8,128)(2,1)S(1)}, bf16[16,2048]{1,0:T(8,128)(2,1)S(1)}, u32[]{:S(2)}, u32[]{:S(2)}) collective-permute-start(bf16[16,2048]{1,0:T(8,128)(2,1)S(1)} %outer_sum0.2.refs_0_), channel_id=1, source_target_pairs={{0,2},{2,0},{4,6},{6,4},{8,10},{10,8},{12,14},{14,12},{16,18},{18,... | collective-permute-start | bytes 196616 | tf_op jit(solution)/shard_map/ppermute | solution.py:207
  34.1 1.6 %collective-permute-start.11 = (bf16[16,4096]{1,0:T(8,128)(2,1)S(1)}, bf16[16,4096]{1,0:T(8,128)(2,1)S(1)}, u32[]{:S(2)}, u32[]{:S(2)}) collective-permute-start(bf16[16,4096]{1,0:T(8,128)(2,1)S(1)} %stack.2), channel_id=1, source_target_pairs={{0,6},{2,4},{4,2},{6,0},{8,14},{10,12},{12,10},{14,8},{16,22},{18,... | collective-permute-start | bytes 393224 | tf_op jit(solution)/shard_map/ppermute | solution.py:207
  35.7 0.6 collective-permute-start.7
  36.3 1.3 %collective-permute-start.6 = (bf16[16,2048]{1,0:T(8,128)(2,1)S(1)}, bf16[16,2048]{1,0:T(8,128)(2,1)S(1)}, u32[]{:S(2)}, u32[]{:S(2)}) collective-permute-start(bf16[16,2048]{1,0:T(8,128)(2,1)S(1)} %outer_sum1.2.refs_1_.refs_3_), channel_id=1, source_target_pairs={{0,2},{2,0},{4,6},{6,4},{8,10},{10,8},{12,14},{14,12},{16,18},{18,... | collective-permute-start | bytes 196616 | tf_op jit(solution)/shard_map/ppermute | solution.py:207
  37.7 1.4 %project0.2.refs_1_ = f32[16,640]{1,0:T(8,128)S(1)} custom-call(bf16[16,16384]{1,0:T(8,128)(2,1)S(1)} %get-tuple-element.10.rows_ref, f32[1,16384]{1,0:T(1,128)S(1)} %get-tuple-element.11.root_ref, bf16[16384,512]{1,0:T(8,128)(2,1)S(1)} %get-tuple-element.12.turned_ref, bf16[16,2048]{1,0:T(8,128)(2,1)S(1)} %outer_sum0.2.refs_0_, ...), custom_call_target="tpu_custom_call" | custom-call | flops 939524096 | bytes 17629184 | tf_op jit(solution)/shard_map/project0/pallas_call | solution.py:28
  39.1 1.0 %collective-permute-done.11.refs_0_ = bf16[16,4096]{1,0:T(8,128)(2,1)S(1)} collective-permute-done((bf16[16,4096]{1,0:T(8,128)(2,1)S(1)}, bf16[16,4096]{1,0:T(8,128)(2,1)S(1)}, u32[]{:S(2)}, u32[]{:S(2)}) %collective-permute-start.11) | collective-permute-done | bytes 131104 | tf_op jit(solution)/shard_map/ppermute | solution.py:207
  40.1 0.8 %project4.2.refs_1_ = f32[16,640]{1,0:T(8,128)S(1)} custom-call(bf16[16,16384]{1,0:T(8,128)(2,1)S(1)} %get-tuple-element.10.rows_ref, f32[1,16384]{1,0:T(1,128)S(1)} %get-tuple-element.11.root_ref, bf16[16384,512]{1,0:T(8,128)(2,1)S(1)} %get-tuple-element.12.turned_ref, bf16[16,4096]{1,0:T(8,128)(2,1)S(1)} %collective-permute-done.11.refs_0_, ...), custom_call_target="tpu_custom_call" | custom-call | flops 67108864 | bytes 17539072 | tf_op jit(solution)/shard_map/project4/pallas_call | solution.py:28
  40.9 0.5 project5.2.refs_1_
  41.3 0.5 project6.2.own_ref
  41.8 1.2 %collective-permute-done.14.other_ref = f32[16,640]{1,0:T(8,128)S(1)} collective-permute-done((f32[16,640]{1,0:T(8,128)S(1)}, f32[16,640]{1,0:T(8,128)S(1)}, u32[]{:S(2)}, u32[]{:S(2)}) %collective-permute-start.14) | collective-permute-done | bytes 40992 | tf_op jit(solution)/shard_map/ppermute | solution.py:207
  43.0 0.4 solve.1.refs_0_
  43.4 0.7 terms23.3
  44.1 1.7 %collective-permute-start.17 = (bf16[16,4096]{1,0:T(8,128)(2,1)S(1)}, bf16[16,4096]{1,0:T(8,128)(2,1)S(1)}, u32[]{:S(2)}, u32[]{:S(2)}) collective-permute-start(bf16[16,4096]{1,0:T(8,128)(2,1)S(1)} %terms23.3), channel_id=1, source_target_pairs={{0,6},{2,4},{4,2},{6,0},{8,14},{10,12},{12,10},{14,8},{16,22},{18,... | collective-permute-start | bytes 393224 | tf_op jit(solution)/shard_map/ppermute | solution.py:207
  45.9 0.7 terms22.3
  46.5 0.7 collective-permute-start.16
  47.2 0.4 terms01.3
  47.6 1.1 %collective-permute-start.22 = (bf16[16,2048]{1,0:T(8,128)(2,1)S(1)}, bf16[16,2048]{1,0:T(8,128)(2,1)S(1)}, u32[]{:S(2)}, u32[]{:S(2)}) collective-permute-start(bf16[16,2048]{1,0:T(8,128)(2,1)S(1)} %terms01.3), channel_id=1, source_target_pairs={{0,2},{2,0},{4,6},{6,4},{8,10},{10,8},{12,14},{14,12},{16,18},{18,... | collective-permute-start | bytes 196616 | tf_op jit(solution)/shard_map/ppermute | solution.py:207
  48.7 0.4 terms11.3
  49.1 1.0 %collective-permute-start.15 = (bf16[16,2048]{1,0:T(8,128)(2,1)S(1)}, bf16[16,2048]{1,0:T(8,128)(2,1)S(1)}, u32[]{:S(2)}, u32[]{:S(2)}) collective-permute-start(bf16[16,2048]{1,0:T(8,128)(2,1)S(1)} %terms11.3), channel_id=1, source_target_pairs={{0,2},{2,0},{4,6},{6,4},{8,10},{10,8},{12,14},{14,12},{16,18},{18,... | collective-permute-start | bytes 196616 | tf_op jit(solution)/shard_map/ppermute | solution.py:207
  50.0 0.4 terms00.3.own_ref
  50.4 2.0 %collective-permute-done.22.refs_0_ = bf16[16,2048]{1,0:T(8,128)(2,1)S(1)} collective-permute-done((bf16[16,2048]{1,0:T(8,128)(2,1)S(1)}, bf16[16,2048]{1,0:T(8,128)(2,1)S(1)}, u32[]{:S(2)}, u32[]{:S(2)}) %collective-permute-start.22) | collective-permute-done | bytes 65568 | tf_op jit(solution)/shard_map/ppermute | solution.py:207
  52.4 1.0 %collective-permute-done.16.refs_1_ = bf16[16,4096]{1,0:T(8,128)(2,1)S(1)} collective-permute-done((bf16[16,4096]{1,0:T(8,128)(2,1)S(1)}, bf16[16,4096]{1,0:T(8,128)(2,1)S(1)}, u32[]{:S(2)}, u32[]{:S(2)}) %collective-permute-start.16) | collective-permute-done | bytes 131104 | tf_op jit(solution)/shard_map/ppermute | solution.py:207
  53.4 2.2 %collective-permute-start.23 = (bf16[16,2048]{1,0:T(8,128)(2,1)S(1)}, bf16[16,2048]{1,0:T(8,128)(2,1)S(1)}, u32[]{:S(2)}, u32[]{:S(2)}) collective-permute-start(bf16[16,2048]{1,0:T(8,128)(2,1)S(1)} %inner_sum0.3.own_ref), channel_id=1, source_target_pairs={{0,8},{1,17},{2,10},{3,19},{4,12},{5,21},{6,14},{7,23},{8,0},{9,25... | collective-permute-start | bytes 196616 | tf_op jit(solution)/shard_map/ppermute | solution.py:213
  55.7 0.4 terms10.3.own_ref
  56.2 2.2 %collective-permute-done.23.other_ref = bf16[16,2048]{1,0:T(8,128)(2,1)S(1)} collective-permute-done((bf16[16,2048]{1,0:T(8,128)(2,1)S(1)}, bf16[16,2048]{1,0:T(8,128)(2,1)S(1)}, u32[]{:S(2)}, u32[]{:S(2)}) %collective-permute-start.23) | collective-permute-done | bytes 65568 | tf_op jit(solution)/shard_map/ppermute | solution.py:213
  58.4 2.2 %collective-permute-start.24 = (bf16[16,2048]{1,0:T(8,128)(2,1)S(1)}, bf16[16,2048]{1,0:T(8,128)(2,1)S(1)}, u32[]{:S(2)}, u32[]{:S(2)}) collective-permute-start(bf16[16,2048]{1,0:T(8,128)(2,1)S(1)} %pair_sum0.3.own_ref), channel_id=1, source_target_pairs={{0,16},{1,9},{2,18},{3,11},{4,20},{5,13},{6,22},{7,15},{8,24},{9,1... | collective-permute-start | bytes 196616 | tf_op jit(solution)/shard_map/ppermute | solution.py:213
  60.7 0.2 collective-permute-done.18.other_ref
  60.9 2.2 %collective-permute-start.19 = (bf16[16,2048]{1,0:T(8,128)(2,1)S(1)}, bf16[16,2048]{1,0:T(8,128)(2,1)S(1)}, u32[]{:S(2)}, u32[]{:S(2)}) collective-permute-start(bf16[16,2048]{1,0:T(8,128)(2,1)S(1)} %pair_sum1.3.own_ref), channel_id=1, source_target_pairs={{0,16},{1,9},{2,18},{3,11},{4,20},{5,13},{6,22},{7,15},{8,24},{9,1... | collective-permute-start | bytes 196616 | tf_op jit(solution)/shard_map/ppermute | solution.py:213
  63.1 0.6 collective-permute-done.24.other_ref
  63.7 1.1 %collective-permute-start.26 = (bf16[16,2048]{1,0:T(8,128)(2,1)S(1)}, bf16[16,2048]{1,0:T(8,128)(2,1)S(1)}, u32[]{:S(2)}, u32[]{:S(2)}) collective-permute-start(bf16[16,2048]{1,0:T(8,128)(2,1)S(1)} %outer_sum0.3.refs_0_), channel_id=1, source_target_pairs={{0,4},{2,6},{4,0},{6,2},{8,12},{10,14},{12,8},{14,10},{16,20},{18,... | collective-permute-start | bytes 196616 | tf_op jit(solution)/shard_map/ppermute | solution.py:207
  64.8 1.3 %collective-permute-start.27 = (bf16[16,2048]{1,0:T(8,128)(2,1)S(1)}, bf16[16,2048]{1,0:T(8,128)(2,1)S(1)}, u32[]{:S(2)}, u32[]{:S(2)}) collective-permute-start(bf16[16,2048]{1,0:T(8,128)(2,1)S(1)} %outer_sum0.3.refs_0_), channel_id=1, source_target_pairs={{0,2},{2,0},{4,6},{6,4},{8,10},{10,8},{12,14},{14,12},{16,18},{18,... | collective-permute-start | bytes 196616 | tf_op jit(solution)/shard_map/ppermute | solution.py:207
  66.1 0.2 collective-permute-done.19.other_ref
  66.4 1.7 %collective-permute-start.25 = (bf16[16,4096]{1,0:T(8,128)(2,1)S(1)}, bf16[16,4096]{1,0:T(8,128)(2,1)S(1)}, u32[]{:S(2)}, u32[]{:S(2)}) collective-permute-start(bf16[16,4096]{1,0:T(8,128)(2,1)S(1)} %stack.3), channel_id=1, source_target_pairs={{0,6},{2,4},{4,2},{6,0},{8,14},{10,12},{12,10},{14,8},{16,22},{18,... | collective-permute-start | bytes 393224 | tf_op jit(solution)/shard_map/ppermute | solution.py:207
  68.2 0.5 collective-permute-start.21
  68.6 1.4 %collective-permute-start.20 = (bf16[16,2048]{1,0:T(8,128)(2,1)S(1)}, bf16[16,2048]{1,0:T(8,128)(2,1)S(1)}, u32[]{:S(2)}, u32[]{:S(2)}) collective-permute-start(bf16[16,2048]{1,0:T(8,128)(2,1)S(1)} %outer_sum1.3.refs_1_.refs_3_), channel_id=1, source_target_pairs={{0,2},{2,0},{4,6},{6,4},{8,10},{10,8},{12,14},{14,12},{16,18},{18,... | collective-permute-start | bytes 196616 | tf_op jit(solution)/shard_map/ppermute | solution.py:207
  70.0 1.5 %project0.3.refs_1_ = f32[16,640]{1,0:T(8,128)S(1)} custom-call(bf16[16,16384]{1,0:T(8,128)(2,1)S(1)} %get-tuple-element.10.rows_ref, f32[1,16384]{1,0:T(1,128)S(1)} %get-tuple-element.11.root_ref, bf16[16384,512]{1,0:T(8,128)(2,1)S(1)} %get-tuple-element.12.turned_ref, bf16[16,2048]{1,0:T(8,128)(2,1)S(1)} %outer_sum0.3.refs_0_, ...), custom_call_target="tpu_custom_call" | custom-call | flops 939524096 | bytes 17629184 | tf_op jit(solution)/shard_map/project0/pallas_call | solution.py:28
  71.4 1.0 %collective-permute-done.25.refs_0_.refs_4_ = bf16[16,4096]{1,0:T(8,128)(2,1)S(1)} collective-permute-done((bf16[16,4096]{1,0:T(8,128)(2,1)S(1)}, bf16[16,4096]{1,0:T(8,128)(2,1)S(1)}, u32[]{:S(2)}, u32[]{:S(2)}) %collective-permute-start.25) | collective-permute-done | bytes 131104 | tf_op jit(solution)/shard_map/ppermute | solution.py:207
  72.4 0.8 %project4.3.refs_1_ = f32[16,640]{1,0:T(8,128)S(1)} custom-call(bf16[16,16384]{1,0:T(8,128)(2,1)S(1)} %get-tuple-element.10.rows_ref, f32[1,16384]{1,0:T(1,128)S(1)} %get-tuple-element.11.root_ref, bf16[16384,512]{1,0:T(8,128)(2,1)S(1)} %get-tuple-element.12.turned_ref, bf16[16,4096]{1,0:T(8,128)(2,1)S(1)} %collective-permute-done.25.refs_0_.refs_4_, ...), custom_call_target="tpu_custom_call" | custom-call | flops 67108864 | bytes 17539072 | tf_op jit(solution)/shard_map/project4/pallas_call | solution.py:28
  73.2 0.5 project5.3.refs_1_
  73.7 0.5 project6.3.own_ref
  74.1 1.2 %collective-permute-done.28.other_ref = f32[16,640]{1,0:T(8,128)S(1)} collective-permute-done((f32[16,640]{1,0:T(8,128)S(1)}, f32[16,640]{1,0:T(8,128)S(1)}, u32[]{:S(2)}, u32[]{:S(2)}) %collective-permute-start.28) | collective-permute-done | bytes 40992 | tf_op jit(solution)/shard_map/ppermute | solution.py:207
  75.4 1.6 %finish.1 = (f32[16,16384]{1,0:T(8,128)}, f32[16,512]{1,0:T(8,128)}) custom-call(f32[16,640]{1,0:T(8,128)S(1)} %project6.3.own_ref, f32[16,640]{1,0:T(8,128)S(1)} %collective-permute-done.28.other_ref, f32[1,16384]{1,0:T(1,128)S(1)} %get-tuple-element.11.root_ref, bf16[16,2048]{1,0:T(8,128)(2,1)S(1)} %outer_sum0.3.refs_0_, ...), custom_call_target="tpu_custom_call" | custom-call | tf_op jit(solution)/shard_map/finish/pallas_call | solution.py:343
  (31 shorter events, 0.6 us)
Async XLA Ops:
  8.1 1.4 %collective-permute-start = (bf16[16,512]{1,0:T(8,128)(2,1)S(1)}, bf16[16,512]{1,0:T(8,128)(2,1)S(1)}, u32[]{:S(2)}, u32[]{:S(2)}) collective-permute-start(bf16[16,512]{1,0:T(8,128)(2,1)S(1)} %get-tuple-element.15.refs_0_), channel_id=1, source_target_pairs={{0,1},{1,0},{2,3},{3,2},{4,5},{5,4},{6,7},{7,6},{8,9},{9,8},{10,11... | collective-permute-start | bytes 49160 | tf_op jit(solution)/shard_map/ppermute | solution.py:207
  10.1 10.0 %collective-permute-start.3 = (bf16[16,4096]{1,0:T(8,128)(2,1)S(1)}, bf16[16,4096]{1,0:T(8,128)(2,1)S(1)}, u32[]{:S(2)}, u32[]{:S(2)}) collective-permute-start(bf16[16,4096]{1,0:T(8,128)(2,1)S(1)} %terms23.2), channel_id=1, source_target_pairs={{0,6},{2,4},{4,2},{6,0},{8,14},{10,12},{12,10},{14,8},{16,22},{18,... | collective-permute-start | bytes 393224 | tf_op jit(solution)/shard_map/ppermute | solution.py:207
  14.6 6.0 %collective-permute-start.2 = (bf16[16,4096]{1,0:T(8,128)(2,1)S(1)}, bf16[16,4096]{1,0:T(8,128)(2,1)S(1)}, u32[]{:S(2)}, u32[]{:S(2)}) collective-permute-start(bf16[16,4096]{1,0:T(8,128)(2,1)S(1)} %terms22.2), channel_id=1, source_target_pairs={{0,4},{2,6},{4,0},{6,2},{8,12},{10,14},{12,8},{14,10},{16,20},{18,... | collective-permute-start | bytes 393224 | tf_op jit(solution)/shard_map/ppermute | solution.py:207
  15.5 4.6 %collective-permute-start.8 = (bf16[16,2048]{1,0:T(8,128)(2,1)S(1)}, bf16[16,2048]{1,0:T(8,128)(2,1)S(1)}, u32[]{:S(2)}, u32[]{:S(2)}) collective-permute-start(bf16[16,2048]{1,0:T(8,128)(2,1)S(1)} %terms01.2), channel_id=1, source_target_pairs={{0,2},{2,0},{4,6},{6,4},{8,10},{10,8},{12,14},{14,12},{16,18},{18,... | collective-permute-start | bytes 196616 | tf_op jit(solution)/shard_map/ppermute | solution.py:207
  16.0 6.9 %collective-permute-start.1 = (bf16[16,2048]{1,0:T(8,128)(2,1)S(1)}, bf16[16,2048]{1,0:T(8,128)(2,1)S(1)}, u32[]{:S(2)}, u32[]{:S(2)}) collective-permute-start(bf16[16,2048]{1,0:T(8,128)(2,1)S(1)} %terms11.2), channel_id=1, source_target_pairs={{0,2},{2,0},{4,6},{6,4},{8,10},{10,8},{12,14},{14,12},{16,18},{18,... | collective-permute-start | bytes 196616 | tf_op jit(solution)/shard_map/ppermute | solution.py:207
  20.6 5.0 %collective-permute-start.9 = (bf16[16,2048]{1,0:T(8,128)(2,1)S(1)}, bf16[16,2048]{1,0:T(8,128)(2,1)S(1)}, u32[]{:S(2)}, u32[]{:S(2)}) collective-permute-start(bf16[16,2048]{1,0:T(8,128)(2,1)S(1)} %inner_sum0.2.own_ref), channel_id=1, source_target_pairs={{0,8},{1,17},{2,10},{3,19},{4,12},{5,21},{6,14},{7,23},{8,0},{9,25... | collective-permute-start | bytes 196616 | tf_op jit(solution)/shard_map/ppermute | solution.py:213
  22.9 5.1 %collective-permute-start.4 = (bf16[16,2048]{1,0:T(8,128)(2,1)S(1)}, bf16[16,2048]{1,0:T(8,128)(2,1)S(1)}, u32[]{:S(2)}, u32[]{:S(2)}) collective-permute-start(bf16[16,2048]{1,0:T(8,128)(2,1)S(1)} %inner_sum1.2.own_ref), channel_id=1, source_target_pairs={{0,8},{1,17},{2,10},{3,19},{4,12},{5,21},{6,14},{7,23},{8,0},{9,25... | collective-permute-start | bytes 196616 | tf_op jit(solution)/shard_map/ppermute | solution.py:213
  25.6 5.3 %collective-permute-start.10 = (bf16[16,2048]{1,0:T(8,128)(2,1)S(1)}, bf16[16,2048]{1,0:T(8,128)(2,1)S(1)}, u32[]{:S(2)}, u32[]{:S(2)}) collective-permute-start(bf16[16,2048]{1,0:T(8,128)(2,1)S(1)} %pair_sum0.2.own_ref), channel_id=1, source_target_pairs={{0,16},{1,9},{2,18},{3,11},{4,20},{5,13},{6,22},{7,15},{8,24},{9,1... | collective-permute-start | bytes 196616 | tf_op jit(solution)/shard_map/ppermute | solution.py:213
  28.0 6.0 %collective-permute-start.5 = (bf16[16,2048]{1,0:T(8,128)(2,1)S(1)}, bf16[16,2048]{1,0:T(8,128)(2,1)S(1)}, u32[]{:S(2)}, u32[]{:S(2)}) collective-permute-start(bf16[16,2048]{1,0:T(8,128)(2,1)S(1)} %pair_sum1.2.own_ref), channel_id=1, source_target_pairs={{0,16},{1,9},{2,18},{3,11},{4,20},{5,13},{6,22},{7,15},{8,24},{9,1... | collective-permute-start | bytes 196616 | tf_op jit(solution)/shard_map/ppermute | solution.py:213
  31.0 6.7 %collective-permute-start.12 = (bf16[16,2048]{1,0:T(8,128)(2,1)S(1)}, bf16[16,2048]{1,0:T(8,128)(2,1)S(1)}, u32[]{:S(2)}, u32[]{:S(2)}) collective-permute-start(bf16[16,2048]{1,0:T(8,128)(2,1)S(1)} %outer_sum0.2.refs_0_), channel_id=1, source_target_pairs={{0,4},{2,6},{4,0},{6,2},{8,12},{10,14},{12,8},{14,10},{16,20},{18,... | collective-permute-start | bytes 196616 | tf_op jit(solution)/shard_map/ppermute | solution.py:207
  32.7 5.0 %collective-permute-start.13 = (bf16[16,2048]{1,0:T(8,128)(2,1)S(1)}, bf16[16,2048]{1,0:T(8,128)(2,1)S(1)}, u32[]{:S(2)}, u32[]{:S(2)}) collective-permute-start(bf16[16,2048]{1,0:T(8,128)(2,1)S(1)} %outer_sum0.2.refs_0_), channel_id=1, source_target_pairs={{0,2},{2,0},{4,6},{6,4},{8,10},{10,8},{12,14},{14,12},{16,18},{18,... | collective-permute-start | bytes 196616 | tf_op jit(solution)/shard_map/ppermute | solution.py:207
  34.1 6.0 %collective-permute-start.11 = (bf16[16,4096]{1,0:T(8,128)(2,1)S(1)}, bf16[16,4096]{1,0:T(8,128)(2,1)S(1)}, u32[]{:S(2)}, u32[]{:S(2)}) collective-permute-start(bf16[16,4096]{1,0:T(8,128)(2,1)S(1)} %stack.2), channel_id=1, source_target_pairs={{0,6},{2,4},{4,2},{6,0},{8,14},{10,12},{12,10},{14,8},{16,22},{18,... | collective-permute-start | bytes 393224 | tf_op jit(solution)/shard_map/ppermute | solution.py:207
  35.7 5.2 %collective-permute-start.7 = (bf16[16,2048]{1,0:T(8,128)(2,1)S(1)}, bf16[16,2048]{1,0:T(8,128)(2,1)S(1)}, u32[]{:S(2)}, u32[]{:S(2)}) collective-permute-start(bf16[16,2048]{1,0:T(8,128)(2,1)S(1)} %outer_sum1.2.refs_1_.refs_3_), channel_id=1, source_target_pairs={{0,4},{2,6},{4,0},{6,2},{8,12},{10,14},{12,8},{14,10},{16,20},{18,... | collective-permute-start | bytes 196616 | tf_op jit(solution)/shard_map/ppermute | solution.py:207
  36.3 5.0 %collective-permute-start.6 = (bf16[16,2048]{1,0:T(8,128)(2,1)S(1)}, bf16[16,2048]{1,0:T(8,128)(2,1)S(1)}, u32[]{:S(2)}, u32[]{:S(2)}) collective-permute-start(bf16[16,2048]{1,0:T(8,128)(2,1)S(1)} %outer_sum1.2.refs_1_.refs_3_), channel_id=1, source_target_pairs={{0,2},{2,0},{4,6},{6,4},{8,10},{10,8},{12,14},{14,12},{16,18},{18,... | collective-permute-start | bytes 196616 | tf_op jit(solution)/shard_map/ppermute | solution.py:207
  41.8 1.2 %collective-permute-start.14 = (f32[16,640]{1,0:T(8,128)S(1)}, f32[16,640]{1,0:T(8,128)S(1)}, u32[]{:S(2)}, u32[]{:S(2)}) collective-permute-start(f32[16,640]{1,0:T(8,128)S(1)} %project6.2.own_ref), channel_id=1, source_target_pairs={{0,1},{1,0},{2,3},{3,2},{4,5},{5,4},{6,7},{7,6},{8,9},{9,8},{10,11... | collective-permute-start | bytes 122888 | tf_op jit(solution)/shard_map/ppermute | solution.py:207
  44.1 8.3 %collective-permute-start.17 = (bf16[16,4096]{1,0:T(8,128)(2,1)S(1)}, bf16[16,4096]{1,0:T(8,128)(2,1)S(1)}, u32[]{:S(2)}, u32[]{:S(2)}) collective-permute-start(bf16[16,4096]{1,0:T(8,128)(2,1)S(1)} %terms23.3), channel_id=1, source_target_pairs={{0,6},{2,4},{4,2},{6,0},{8,14},{10,12},{12,10},{14,8},{16,22},{18,... | collective-permute-start | bytes 393224 | tf_op jit(solution)/shard_map/ppermute | solution.py:207
  46.5 6.9 %collective-permute-start.16 = (bf16[16,4096]{1,0:T(8,128)(2,1)S(1)}, bf16[16,4096]{1,0:T(8,128)(2,1)S(1)}, u32[]{:S(2)}, u32[]{:S(2)}) collective-permute-start(bf16[16,4096]{1,0:T(8,128)(2,1)S(1)} %terms22.3), channel_id=1, source_target_pairs={{0,4},{2,6},{4,0},{6,2},{8,12},{10,14},{12,8},{14,10},{16,20},{18,... | collective-permute-start | bytes 393224 | tf_op jit(solution)/shard_map/ppermute | solution.py:207
  47.6 4.8 %collective-permute-start.22 = (bf16[16,2048]{1,0:T(8,128)(2,1)S(1)}, bf16[16,2048]{1,0:T(8,128)(2,1)S(1)}, u32[]{:S(2)}, u32[]{:S(2)}) collective-permute-start(bf16[16,2048]{1,0:T(8,128)(2,1)S(1)} %terms01.3), channel_id=1, source_target_pairs={{0,2},{2,0},{4,6},{6,4},{8,10},{10,8},{12,14},{14,12},{16,18},{18,... | collective-permute-start | bytes 196616 | tf_op jit(solution)/shard_map/ppermute | solution.py:207
  49.1 7.0 %collective-permute-start.15 = (bf16[16,2048]{1,0:T(8,128)(2,1)S(1)}, bf16[16,2048]{1,0:T(8,128)(2,1)S(1)}, u32[]{:S(2)}, u32[]{:S(2)}) collective-permute-start(bf16[16,2048]{1,0:T(8,128)(2,1)S(1)} %terms11.3), channel_id=1, source_target_pairs={{0,2},{2,0},{4,6},{6,4},{8,10},{10,8},{12,14},{14,12},{16,18},{18,... | collective-permute-start | bytes 196616 | tf_op jit(solution)/shard_map/ppermute | solution.py:207
  53.4 5.0 %collective-permute-start.23 = (bf16[16,2048]{1,0:T(8,128)(2,1)S(1)}, bf16[16,2048]{1,0:T(8,128)(2,1)S(1)}, u32[]{:S(2)}, u32[]{:S(2)}) collective-permute-start(bf16[16,2048]{1,0:T(8,128)(2,1)S(1)} %inner_sum0.3.own_ref), channel_id=1, source_target_pairs={{0,8},{1,17},{2,10},{3,19},{4,12},{5,21},{6,14},{7,23},{8,0},{9,25... | collective-permute-start | bytes 196616 | tf_op jit(solution)/shard_map/ppermute | solution.py:213
  56.1 4.8 %collective-permute-start.18 = (bf16[16,2048]{1,0:T(8,128)(2,1)S(1)}, bf16[16,2048]{1,0:T(8,128)(2,1)S(1)}, u32[]{:S(2)}, u32[]{:S(2)}) collective-permute-start(bf16[16,2048]{1,0:T(8,128)(2,1)S(1)} %inner_sum1.3.own_ref), channel_id=1, source_target_pairs={{0,8},{1,17},{2,10},{3,19},{4,12},{5,21},{6,14},{7,23},{8,0},{9,25... | collective-permute-start | bytes 196616 | tf_op jit(solution)/shard_map/ppermute | solution.py:213
  58.4 5.3 %collective-permute-start.24 = (bf16[16,2048]{1,0:T(8,128)(2,1)S(1)}, bf16[16,2048]{1,0:T(8,128)(2,1)S(1)}, u32[]{:S(2)}, u32[]{:S(2)}) collective-permute-start(bf16[16,2048]{1,0:T(8,128)(2,1)S(1)} %pair_sum0.3.own_ref), channel_id=1, source_target_pairs={{0,16},{1,9},{2,18},{3,11},{4,20},{5,13},{6,22},{7,15},{8,24},{9,1... | collective-permute-start | bytes 196616 | tf_op jit(solution)/shard_map/ppermute | solution.py:213
  60.9 5.5 %collective-permute-start.19 = (bf16[16,2048]{1,0:T(8,128)(2,1)S(1)}, bf16[16,2048]{1,0:T(8,128)(2,1)S(1)}, u32[]{:S(2)}, u32[]{:S(2)}) collective-permute-start(bf16[16,2048]{1,0:T(8,128)(2,1)S(1)} %pair_sum1.3.own_ref), channel_id=1, source_target_pairs={{0,16},{1,9},{2,18},{3,11},{4,20},{5,13},{6,22},{7,15},{8,24},{9,1... | collective-permute-start | bytes 196616 | tf_op jit(solution)/shard_map/ppermute | solution.py:213
  63.7 6.2 %collective-permute-start.26 = (bf16[16,2048]{1,0:T(8,128)(2,1)S(1)}, bf16[16,2048]{1,0:T(8,128)(2,1)S(1)}, u32[]{:S(2)}, u32[]{:S(2)}) collective-permute-start(bf16[16,2048]{1,0:T(8,128)(2,1)S(1)} %outer_sum0.3.refs_0_), channel_id=1, source_target_pairs={{0,4},{2,6},{4,0},{6,2},{8,12},{10,14},{12,8},{14,10},{16,20},{18,... | collective-permute-start | bytes 196616 | tf_op jit(solution)/shard_map/ppermute | solution.py:207
  64.8 5.2 %collective-permute-start.27 = (bf16[16,2048]{1,0:T(8,128)(2,1)S(1)}, bf16[16,2048]{1,0:T(8,128)(2,1)S(1)}, u32[]{:S(2)}, u32[]{:S(2)}) collective-permute-start(bf16[16,2048]{1,0:T(8,128)(2,1)S(1)} %outer_sum0.3.refs_0_), channel_id=1, source_target_pairs={{0,2},{2,0},{4,6},{6,4},{8,10},{10,8},{12,14},{14,12},{16,18},{18,... | collective-permute-start | bytes 196616 | tf_op jit(solution)/shard_map/ppermute | solution.py:207
  66.4 6.0 %collective-permute-start.25 = (bf16[16,4096]{1,0:T(8,128)(2,1)S(1)}, bf16[16,4096]{1,0:T(8,128)(2,1)S(1)}, u32[]{:S(2)}, u32[]{:S(2)}) collective-permute-start(bf16[16,4096]{1,0:T(8,128)(2,1)S(1)} %stack.3), channel_id=1, source_target_pairs={{0,6},{2,4},{4,2},{6,0},{8,14},{10,12},{12,10},{14,8},{16,22},{18,... | collective-permute-start | bytes 393224 | tf_op jit(solution)/shard_map/ppermute | solution.py:207
  68.2 5.0 %collective-permute-start.21 = (bf16[16,2048]{1,0:T(8,128)(2,1)S(1)}, bf16[16,2048]{1,0:T(8,128)(2,1)S(1)}, u32[]{:S(2)}, u32[]{:S(2)}) collective-permute-start(bf16[16,2048]{1,0:T(8,128)(2,1)S(1)} %outer_sum1.3.refs_1_.refs_3_), channel_id=1, source_target_pairs={{0,4},{2,6},{4,0},{6,2},{8,12},{10,14},{12,8},{14,10},{16,20},{18,... | collective-permute-start | bytes 196616 | tf_op jit(solution)/shard_map/ppermute | solution.py:207
  68.6 5.1 %collective-permute-start.20 = (bf16[16,2048]{1,0:T(8,128)(2,1)S(1)}, bf16[16,2048]{1,0:T(8,128)(2,1)S(1)}, u32[]{:S(2)}, u32[]{:S(2)}) collective-permute-start(bf16[16,2048]{1,0:T(8,128)(2,1)S(1)} %outer_sum1.3.refs_1_.refs_3_), channel_id=1, source_target_pairs={{0,2},{2,0},{4,6},{6,4},{8,10},{10,8},{12,14},{14,12},{16,18},{18,... | collective-permute-start | bytes 196616 | tf_op jit(solution)/shard_map/ppermute | solution.py:207
  74.1 1.2 %collective-permute-start.28 = (f32[16,640]{1,0:T(8,128)S(1)}, f32[16,640]{1,0:T(8,128)S(1)}, u32[]{:S(2)}, u32[]{:S(2)}) collective-permute-start(f32[16,640]{1,0:T(8,128)S(1)} %project6.3.own_ref), channel_id=1, source_target_pairs={{0,1},{1,0},{2,3},{3,2},{4,5},{5,4},{6,7},{7,6},{8,9},{9,8},{10,11... | collective-permute-start | bytes 122888 | tf_op jit(solution)/shard_map/ppermute | solution.py:207

commit v3 on v1

--- a/solution.py
+++ b/solution.py
@@ -52,8 +52,16 @@
     return parts
 
 
-def load_body(width, group, g_ref, f_ref, b_ref, a_ref, t_ref, s_ref, centre_ref, root_ref, rows_ref, *scratch):
-    f_vm, b_vm, inverse, parts, sems = scratch
+def centred(narrow, centre):
+    terms = narrow.astype(jnp.float32) * centre
+    total = terms[:, :LANES]
+    for first in range(LANES, terms.shape[1], LANES):
+        total = total + terms[:, first : first + LANES]
+    return total
+
+
+def load_body(width, group, g_ref, f_ref, b_ref, a_ref, t_ref, s_ref, centre_ref, root_ref, *scratch):
+    f_vm, b_vm, inverse, sems = scratch
     block = b_ref.shape[0]
     rows, cols = a_ref.shape
     steps = cols // width
@@ -79,7 +87,6 @@
         for k in range(group):
             chunk(i * group + k).start()
 
-    parts[...] = jnp.zeros(parts.shape, jnp.float32)
     table.wait()
 
     @pl.loop(0, f_vm.shape[0] // 8)
@@ -88,16 +95,12 @@
         centre = 2.0 * frequency
         root = jnp.sqrt(centre * (1.0 - frequency))
         scale = 1.0 / root
-        high, middle, low = in_parts(centre, 3)
         for r in range(8):
             here = columns(8 * i + r, LANES)
             one = slice(r, r + 1)
             centre_ref[:, here] = centre[one]
             root_ref[:, here] = root[one]
             inverse[:, here] = scale[one]
-            parts[0:1, here] = high[one]
-            parts[1:2, here] = middle[one]
-            parts[2:3, here] = low[one]
 
     def body(i, carry):
         total, shift = carry
@@ -105,18 +108,15 @@
         for k in range(group):
             at = i * group + k
             here = columns(at, width)
-            three = parts[:, here]
-            three = jnp.concatenate([three, jnp.zeros_like(three)], axis=0).astype(jnp.bfloat16)
-            rows_ref[:, here] = three
             narrow = (b_vm[:, here] * inverse[:, here]).astype(jnp.bfloat16)
-            shift = shift + dot(narrow, three, (1, 1))
+            shift = shift + centred(narrow, centre_ref[:, here])
             chunk(at).wait()
             turned = a_ref[:, here].T
             t_ref[here, :] = turned
             total = total + dot(narrow, turned, (1, 0))
         return total, shift
 
-    carry = (jnp.zeros((block, rows), jnp.float32), jnp.zeros((block, block), jnp.float32))
+    carry = (jnp.zeros((block, rows), jnp.float32), jnp.zeros((block, LANES), jnp.float32))
     total, shift = lax.fori_loop(0, bodies, body, carry)
     s_ref[...] = (total - jnp.sum(shift, axis=1, keepdims=True)).astype(jnp.bfloat16)
 
@@ -129,20 +129,18 @@
     return pl.pallas_call(
         functools.partial(load_body, width, 8),
         in_specs=[anywhere] * 3,
-        out_specs=[KEPT] * 2 + [HERE] * 4,
+        out_specs=[KEPT] * 2 + [HERE] * 3,
         out_shape=[
             pltpu.VMEM((rows, cols), jnp.bfloat16),
             pltpu.VMEM((cols, rows), jnp.bfloat16),
             shape((block, rows)),
             shape((1, cols), jnp.float32),
             shape((1, cols), jnp.float32),
-            shape((block, cols)),
         ],
         scratch_shapes=[
             pltpu.VMEM((cols // LANES, LANES), jnp.float32),
             pltpu.VMEM((block, cols), jnp.float32),
             pltpu.VMEM((1, cols), jnp.float32),
-            pltpu.VMEM((8, cols), jnp.float32),
             pltpu.SemaphoreType.DMA((cols // width + 3,)),
         ],
         compiler_params=pltpu.CompilerParams(vmem_limit_bytes=8 * MIB),
@@ -237,18 +235,18 @@
     return {key: pieces[key] for key in order}
 
 
-def project_body(keys, inner, rows_ref, root_ref, turned_ref, *refs):
+def project_body(keys, inner, centre_ref, root_ref, turned_ref, *refs):
     pieces, out = refs[: len(keys)], refs[-1]
     block = pieces[0].shape[0]
     cols, rows = turned_ref.shape
     total = jnp.zeros((block, rows), jnp.float32)
-    shift = jnp.zeros((block, block), jnp.float32)
+    shift = jnp.zeros((block, LANES), jnp.float32)
     gram = jnp.zeros((block, block), jnp.float32)
     for key, piece in zip(keys, pieces):
         columns = columns_of(key, inner, piece.shape[1], cols)
         value = (piece[...].astype(jnp.float32) * root_ref[:, columns]).astype(jnp.bfloat16)
         gram += dot(value, value, (1, 1))
-        shift += dot(piece[...], rows_ref[:, columns], (1, 1))
+        shift += centred(piece[...], centre_ref[:, columns])
         total += dot(piece[...], turned_ref[columns, :], (1, 0))
     total -= jnp.sum(shift, axis=1, keepdims=True)
     gram = jnp.concatenate([gram, jnp.zeros((block, LANES - block), jnp.float32)], axis=1)
@@ -259,14 +257,14 @@
     out[:, rows:] = gram
 
 
-def project(pieces, turned, centre_rows, root, inner):
+def project(pieces, turned, centre, root, inner):
     order = list(pieces)
-    block = centre_rows.shape[0]
+    block = pieces[0, 0].shape[0]
     rows = turned.shape[1]
     total = ()
     for first, last in ((0, 4), (4, 5), (5, 6), (6, 7)):
         keys = order[first:last]
-        operands = (centre_rows, root, in_vmem(turned), *(pieces[key] for key in keys)) + total
+        operands = (centre, root, in_vmem(turned), *(pieces[key] for key in keys)) + total
         body = functools.partial(project_body, keys, inner)
         out = shape((block, rows + LANES), jnp.float32)
         flops = (7 if first == 0 else 1) * 2 * rows * sum(pieces[key].size for key in keys)
@@ -358,11 +356,11 @@
 def make_local(inner, var):
     def local(genotypes, frequency, start_block):
         scaling = float(start_block.shape[0] * var) ** 0.5
-        kept, turned, own, centre, root, centre_rows = load(genotypes, frequency, start_block.T)
+        kept, turned, own, centre, root = load(genotypes, frequency, start_block.T)
         sample_rows = (own, swap(own, "var", var, 1))
         for iteration in range(ITERS):
             pieces = sum_over_samples(sample_rows, kept, centre, root, inner)
-            own = project(pieces, turned, centre_rows, root, inner)
+            own = project(pieces, turned, centre, root, inner)
             other = swap(own, "var", var, 1)
             if iteration < ITERS - 1:
                 sample_rows = (solve(own, other),)

time: 75.5 us -> 75.3 us (level)
  transfers between devices with their start and end apart: 31 -> 31, of which waited for: 19 -> 18; matrix products, arithmetic and copies ran while one was open for 0% -> 0% of each run, Pallas kernels for 14% -> 13%
where the time goes in v3:
time: 75.3 us; the launch traced here: 75.1 us
  starting transfers between devices  37.5 us (50%)
  Pallas kernels  21.5 us (29%)
  waiting for transfers between devices  15.2 us (20%)
  between operations  0.93 us (1%)
    ppermute x23, starting transfers between devices, swap(): return lax.ppermute(x, axis, [(d, d ^ turn) for d in range(size)])  24.4 us
    ppermute x8, starting transfers between devices, swap_across(): return lax.ppermute(x, ('samp', 'var'), pairs)  13 us
    pallas_call x37, Pallas kernels, call(): pl.pallas_call(body, out_shape=out, in_specs=[HERE] * len(operands), out_...  12.5 us
    ppermute x23, waiting for transfers between devices, swap(): return lax.ppermute(x, axis, [(d, d ^ turn) for d in range(size)])  9.03 us
    pallas_call x1, Pallas kernels, load(): pl.pallas_call(functools.partial(load_body, width, 8), in_specs=[anywhere...  7.41 us
    ppermute x8, waiting for transfers between devices, swap_across(): return lax.ppermute(x, ('samp', 'var'), pairs)  6.18 us
    pallas_call x1, Pallas kernels, finish(): pl.pallas_call(functools.partial(finish_body, scaling, order, inner), out...  1.56 us
  transfers between devices with their start and end apart: 31, of which 18 were waited for; matrix products, arithmetic and copies ran while one was open for 0% of the time, Pallas kernels for 13%

profile of v3, /device:TPU:0, one launch (start us, length us, event | category | flops | bytes accessed | tf_op | source)
XLA Modules:
  0.0 75.1 jit_solution(11908038770622889501)
XLA Ops:
  0.6 7.4 %load.1 = (bf16[512,16384]{1,0:T(8,128)(2,1)S(1)}, bf16[16384,512]{1,0:T(8,128)(2,1)S(1)}, bf16[16,512]{1,0:T(8,128)(2,1)S(1)}, f32[1,16384]{1,0:T(1,128)S(1)}, f32[1,16384]{1,0:T(1,128)S(1)}) custom-call(bf16[512,16384]{1,0:T(8,128)(2,1)} %g_ref.1, f32[128,128]{1,0:T(8,128)} %bitcast.5, f32[16,16384]{1,0:T(8,128)} %bitcast.4), custom_call_target="tpu_custom_call" | custom-call | tf_op jit(solution)/shard_map/load/pallas_call | solution.py:129
  8.1 0.5 collective-permute-start
  8.6 0.8 %collective-permute-done.refs_1_ = bf16[16,512]{1,0:T(8,128)(2,1)S(1)} collective-permute-done((bf16[16,512]{1,0:T(8,128)(2,1)S(1)}, bf16[16,512]{1,0:T(8,128)(2,1)S(1)}, u32[]{:S(2)}, u32[]{:S(2)}) %collective-permute-start) | collective-permute-done | bytes 16416 | tf_op jit(solution)/shard_map/ppermute | solution.py:205
  9.4 0.7 terms23.2
  10.1 3.8 %collective-permute-start.3 = (bf16[16,4096]{1,0:T(8,128)(2,1)S(1)}, bf16[16,4096]{1,0:T(8,128)(2,1)S(1)}, u32[]{:S(2)}, u32[]{:S(2)}) collective-permute-start(bf16[16,4096]{1,0:T(8,128)(2,1)S(1)} %terms23.2), channel_id=1, source_target_pairs={{0,6},{2,4},{4,2},{6,0},{8,14},{10,12},{12,10},{14,8},{16,22},{18,... | collective-permute-start | bytes 393224 | tf_op jit(solution)/shard_map/ppermute | solution.py:205
  13.9 0.4 terms02.2
  14.3 0.5 collective-permute-start.9
  14.8 0.4 terms01.2
  15.2 0.4 terms12.2
  15.6 2.0 %collective-permute-start.2 = (bf16[16,2048]{1,0:T(8,128)(2,1)S(1)}, bf16[16,2048]{1,0:T(8,128)(2,1)S(1)}, u32[]{:S(2)}, u32[]{:S(2)}) collective-permute-start(bf16[16,2048]{1,0:T(8,128)(2,1)S(1)} %terms12.2), channel_id=1, source_target_pairs={{0,4},{2,6},{4,0},{6,2},{8,12},{10,14},{12,8},{14,10},{16,20},{18,... | collective-permute-start | bytes 196616 | tf_op jit(solution)/shard_map/ppermute | solution.py:205
  17.6 0.4 terms11.2
  18.0 1.5 %collective-permute-start.1 = (bf16[16,2048]{1,0:T(8,128)(2,1)S(1)}, bf16[16,2048]{1,0:T(8,128)(2,1)S(1)}, u32[]{:S(2)}, u32[]{:S(2)}) collective-permute-start(bf16[16,2048]{1,0:T(8,128)(2,1)S(1)} %terms11.2), channel_id=1, source_target_pairs={{0,2},{2,0},{4,6},{6,4},{8,10},{10,8},{12,14},{14,12},{16,18},{18,... | collective-permute-start | bytes 196616 | tf_op jit(solution)/shard_map/ppermute | solution.py:205
  19.5 0.4 terms00.2.own_ref
  20.0 1.6 %collective-permute-start.10 = (bf16[16,2048]{1,0:T(8,128)(2,1)S(1)}, bf16[16,2048]{1,0:T(8,128)(2,1)S(1)}, u32[]{:S(2)}, u32[]{:S(2)}) collective-permute-start(bf16[16,2048]{1,0:T(8,128)(2,1)S(1)} %inner_sum0.2.own_ref), channel_id=1, source_target_pairs={{0,8},{1,17},{2,10},{3,19},{4,12},{5,21},{6,14},{7,23},{8,0},{9,25... | collective-permute-start | bytes 196616 | tf_op jit(solution)/shard_map/ppermute | solution.py:211
  21.6 0.4 terms10.2.own_ref
  22.3 1.6 %collective-permute-start.4 = (bf16[16,2048]{1,0:T(8,128)(2,1)S(1)}, bf16[16,2048]{1,0:T(8,128)(2,1)S(1)}, u32[]{:S(2)}, u32[]{:S(2)}) collective-permute-start(bf16[16,2048]{1,0:T(8,128)(2,1)S(1)} %inner_sum1.2.own_ref), channel_id=1, source_target_pairs={{0,8},{1,17},{2,10},{3,19},{4,12},{5,21},{6,14},{7,23},{8,0},{9,25... | collective-permute-start | bytes 196616 | tf_op jit(solution)/shard_map/ppermute | solution.py:211
  24.3 2.7 %collective-permute-start.11 = (bf16[16,2048]{1,0:T(8,128)(2,1)S(1)}, bf16[16,2048]{1,0:T(8,128)(2,1)S(1)}, u32[]{:S(2)}, u32[]{:S(2)}) collective-permute-start(bf16[16,2048]{1,0:T(8,128)(2,1)S(1)} %pair_sum0.2.own_ref), channel_id=1, source_target_pairs={{0,16},{1,9},{2,18},{3,11},{4,20},{5,13},{6,22},{7,15},{8,24},{9,1... | collective-permute-start | bytes 196616 | tf_op jit(solution)/shard_map/ppermute | solution.py:211
  27.0 0.8 %collective-permute-done.4.other_ref = bf16[16,2048]{1,0:T(8,128)(2,1)S(1)} collective-permute-done((bf16[16,2048]{1,0:T(8,128)(2,1)S(1)}, bf16[16,2048]{1,0:T(8,128)(2,1)S(1)}, u32[]{:S(2)}, u32[]{:S(2)}) %collective-permute-start.4) | collective-permute-done | bytes 65568 | tf_op jit(solution)/shard_map/ppermute | solution.py:211
  27.8 1.5 %collective-permute-start.5 = (bf16[16,2048]{1,0:T(8,128)(2,1)S(1)}, bf16[16,2048]{1,0:T(8,128)(2,1)S(1)}, u32[]{:S(2)}, u32[]{:S(2)}) collective-permute-start(bf16[16,2048]{1,0:T(8,128)(2,1)S(1)} %pair_sum1.2.own_ref), channel_id=1, source_target_pairs={{0,16},{1,9},{2,18},{3,11},{4,20},{5,13},{6,22},{7,15},{8,24},{9,1... | collective-permute-start | bytes 196616 | tf_op jit(solution)/shard_map/ppermute | solution.py:211
  29.6 1.6 %collective-permute-start.13 = (bf16[16,2048]{1,0:T(8,128)(2,1)S(1)}, bf16[16,2048]{1,0:T(8,128)(2,1)S(1)}, u32[]{:S(2)}, u32[]{:S(2)}) collective-permute-start(bf16[16,2048]{1,0:T(8,128)(2,1)S(1)} %outer_sum0.2.refs_0_), channel_id=1, source_target_pairs={{0,4},{2,6},{4,0},{6,2},{8,12},{10,14},{12,8},{14,10},{16,20},{18,... | collective-permute-start | bytes 196616 | tf_op jit(solution)/shard_map/ppermute | solution.py:205
  31.2 0.8 %collective-permute-start.14 = (bf16[16,2048]{1,0:T(8,128)(2,1)S(1)}, bf16[16,2048]{1,0:T(8,128)(2,1)S(1)}, u32[]{:S(2)}, u32[]{:S(2)}) collective-permute-start(bf16[16,2048]{1,0:T(8,128)(2,1)S(1)} %outer_sum0.2.refs_0_), channel_id=1, source_target_pairs={{0,2},{2,0},{4,6},{6,4},{8,10},{10,8},{12,14},{14,12},{16,18},{18,... | collective-permute-start | bytes 196616 | tf_op jit(solution)/shard_map/ppermute | solution.py:205
  32.0 1.0 %collective-permute-done.5.other_ref = bf16[16,2048]{1,0:T(8,128)(2,1)S(1)} collective-permute-done((bf16[16,2048]{1,0:T(8,128)(2,1)S(1)}, bf16[16,2048]{1,0:T(8,128)(2,1)S(1)}, u32[]{:S(2)}, u32[]{:S(2)}) %collective-permute-start.5) | collective-permute-done | bytes 65568 | tf_op jit(solution)/shard_map/ppermute | solution.py:211
  33.1 1.7 %collective-permute-start.12 = (bf16[16,4096]{1,0:T(8,128)(2,1)S(1)}, bf16[16,4096]{1,0:T(8,128)(2,1)S(1)}, u32[]{:S(2)}, u32[]{:S(2)}) collective-permute-start(bf16[16,4096]{1,0:T(8,128)(2,1)S(1)} %stack.2), channel_id=1, source_target_pairs={{0,6},{2,4},{4,2},{6,0},{8,14},{10,12},{12,10},{14,8},{16,22},{18,... | collective-permute-start | bytes 393224 | tf_op jit(solution)/shard_map/ppermute | solution.py:205
  34.9 2.0 %collective-permute-start.7 = (bf16[16,2048]{1,0:T(8,128)(2,1)S(1)}, bf16[16,2048]{1,0:T(8,128)(2,1)S(1)}, u32[]{:S(2)}, u32[]{:S(2)}) collective-permute-start(bf16[16,2048]{1,0:T(8,128)(2,1)S(1)} %outer_sum1.2.refs_1_.refs_3_), channel_id=1, source_target_pairs={{0,4},{2,6},{4,0},{6,2},{8,12},{10,14},{12,8},{14,10},{16,20},{18,... | collective-permute-start | bytes 196616 | tf_op jit(solution)/shard_map/ppermute | solution.py:205
  36.9 1.4 %project0.2.refs_1_ = f32[16,640]{1,0:T(8,128)S(1)} custom-call(f32[1,16384]{1,0:T(1,128)S(1)} %get-tuple-element.9.centre_ref, f32[1,16384]{1,0:T(1,128)S(1)} %get-tuple-element.10.root_ref, bf16[16384,512]{1,0:T(8,128)(2,1)S(1)} %get-tuple-element.11.turned_ref, bf16[16,2048]{1,0:T(8,128)(2,1)S(1)} %outer_sum0.2.refs_0_, ...), custom_call_target="tpu_custom_call" | custom-call | flops 939524096 | bytes 17170432 | tf_op jit(solution)/shard_map/project0/pallas_call | solution.py:28
  38.2 0.9 %collective-permute-done.12.refs_0_ = bf16[16,4096]{1,0:T(8,128)(2,1)S(1)} collective-permute-done((bf16[16,4096]{1,0:T(8,128)(2,1)S(1)}, bf16[16,4096]{1,0:T(8,128)(2,1)S(1)}, u32[]{:S(2)}, u32[]{:S(2)}) %collective-permute-start.12) | collective-permute-done | bytes 131104 | tf_op jit(solution)/shard_map/ppermute | solution.py:205
  39.1 0.7 project4.2.refs_1_
  39.8 0.5 project5.2.refs_1_
  40.3 0.8 %collective-permute-done.6.refs_0_ = bf16[16,2048]{1,0:T(8,128)(2,1)S(1)} collective-permute-done((bf16[16,2048]{1,0:T(8,128)(2,1)S(1)}, bf16[16,2048]{1,0:T(8,128)(2,1)S(1)}, u32[]{:S(2)}, u32[]{:S(2)}) %collective-permute-start.6) | collective-permute-done | bytes 65568 | tf_op jit(solution)/shard_map/ppermute | solution.py:205
  41.1 0.4 project6.2.own_ref
  41.5 1.2 %collective-permute-done.15.other_ref = f32[16,640]{1,0:T(8,128)S(1)} collective-permute-done((f32[16,640]{1,0:T(8,128)S(1)}, f32[16,640]{1,0:T(8,128)S(1)}, u32[]{:S(2)}, u32[]{:S(2)}) %collective-permute-start.15) | collective-permute-done | bytes 40992 | tf_op jit(solution)/shard_map/ppermute | solution.py:205
  42.8 0.4 solve.1.refs_0_
  43.2 0.7 terms23.3
  43.9 0.9 %collective-permute-start.18 = (bf16[16,4096]{1,0:T(8,128)(2,1)S(1)}, bf16[16,4096]{1,0:T(8,128)(2,1)S(1)}, u32[]{:S(2)}, u32[]{:S(2)}) collective-permute-start(bf16[16,4096]{1,0:T(8,128)(2,1)S(1)} %terms23.3), channel_id=1, source_target_pairs={{0,6},{2,4},{4,2},{6,0},{8,14},{10,12},{12,10},{14,8},{16,22},{18,... | collective-permute-start | bytes 393224 | tf_op jit(solution)/shard_map/ppermute | solution.py:205
  44.8 0.4 terms02.3
  45.2 2.0 %collective-permute-start.24 = (bf16[16,2048]{1,0:T(8,128)(2,1)S(1)}, bf16[16,2048]{1,0:T(8,128)(2,1)S(1)}, u32[]{:S(2)}, u32[]{:S(2)}) collective-permute-start(bf16[16,2048]{1,0:T(8,128)(2,1)S(1)} %terms02.3), channel_id=1, source_target_pairs={{0,4},{2,6},{4,0},{6,2},{8,12},{10,14},{12,8},{14,10},{16,20},{18,... | collective-permute-start | bytes 196616 | tf_op jit(solution)/shard_map/ppermute | solution.py:205
  47.2 0.4 terms01.3
  47.5 0.6 collective-permute-start.23
  48.1 0.4 terms12.3
  48.5 0.7 collective-permute-start.17
  49.2 0.4 terms11.3
  49.6 0.8 %collective-permute-start.16 = (bf16[16,2048]{1,0:T(8,128)(2,1)S(1)}, bf16[16,2048]{1,0:T(8,128)(2,1)S(1)}, u32[]{:S(2)}, u32[]{:S(2)}) collective-permute-start(bf16[16,2048]{1,0:T(8,128)(2,1)S(1)} %terms11.3), channel_id=1, source_target_pairs={{0,2},{2,0},{4,6},{6,4},{8,10},{10,8},{12,14},{14,12},{16,18},{18,... | collective-permute-start | bytes 196616 | tf_op jit(solution)/shard_map/ppermute | solution.py:205
  50.4 0.4 terms00.3.own_ref
  50.8 1.0 %collective-permute-done.24.refs_1_ = bf16[16,2048]{1,0:T(8,128)(2,1)S(1)} collective-permute-done((bf16[16,2048]{1,0:T(8,128)(2,1)S(1)}, bf16[16,2048]{1,0:T(8,128)(2,1)S(1)}, u32[]{:S(2)}, u32[]{:S(2)}) %collective-permute-start.24) | collective-permute-done | bytes 65568 | tf_op jit(solution)/shard_map/ppermute | solution.py:205
  51.8 0.6 collective-permute-done.23.refs_0_
  52.5 0.5 collective-permute-start.25
  53.0 0.4 terms10.3.own_ref
  53.4 0.5 collective-permute-done.16.refs_0_
  53.9 1.7 %collective-permute-start.19 = (bf16[16,2048]{1,0:T(8,128)(2,1)S(1)}, bf16[16,2048]{1,0:T(8,128)(2,1)S(1)}, u32[]{:S(2)}, u32[]{:S(2)}) collective-permute-start(bf16[16,2048]{1,0:T(8,128)(2,1)S(1)} %inner_sum1.3.own_ref), channel_id=1, source_target_pairs={{0,8},{1,17},{2,10},{3,19},{4,12},{5,21},{6,14},{7,23},{8,0},{9,25... | collective-permute-start | bytes 196616 | tf_op jit(solution)/shard_map/ppermute | solution.py:211
  55.6 1.3 %collective-permute-done.25.other_ref = bf16[16,2048]{1,0:T(8,128)(2,1)S(1)} collective-permute-done((bf16[16,2048]{1,0:T(8,128)(2,1)S(1)}, bf16[16,2048]{1,0:T(8,128)(2,1)S(1)}, u32[]{:S(2)}, u32[]{:S(2)}) %collective-permute-start.25) | collective-permute-done | bytes 65568 | tf_op jit(solution)/shard_map/ppermute | solution.py:211
  57.0 1.3 %collective-permute-start.26 = (bf16[16,2048]{1,0:T(8,128)(2,1)S(1)}, bf16[16,2048]{1,0:T(8,128)(2,1)S(1)}, u32[]{:S(2)}, u32[]{:S(2)}) collective-permute-start(bf16[16,2048]{1,0:T(8,128)(2,1)S(1)} %pair_sum0.3.own_ref), channel_id=1, source_target_pairs={{0,16},{1,9},{2,18},{3,11},{4,20},{5,13},{6,22},{7,15},{8,24},{9,1... | collective-permute-start | bytes 196616 | tf_op jit(solution)/shard_map/ppermute | solution.py:211
  58.5 2.0 %collective-permute-start.20 = (bf16[16,2048]{1,0:T(8,128)(2,1)S(1)}, bf16[16,2048]{1,0:T(8,128)(2,1)S(1)}, u32[]{:S(2)}, u32[]{:S(2)}) collective-permute-start(bf16[16,2048]{1,0:T(8,128)(2,1)S(1)} %pair_sum1.3.own_ref), channel_id=1, source_target_pairs={{0,16},{1,9},{2,18},{3,11},{4,20},{5,13},{6,22},{7,15},{8,24},{9,1... | collective-permute-start | bytes 196616 | tf_op jit(solution)/shard_map/ppermute | solution.py:211
  60.5 2.2 %collective-permute-done.26.other_ref = bf16[16,2048]{1,0:T(8,128)(2,1)S(1)} collective-permute-done((bf16[16,2048]{1,0:T(8,128)(2,1)S(1)}, bf16[16,2048]{1,0:T(8,128)(2,1)S(1)}, u32[]{:S(2)}, u32[]{:S(2)}) %collective-permute-start.26) | collective-permute-done | bytes 65568 | tf_op jit(solution)/shard_map/ppermute | solution.py:211
  62.8 0.9 %collective-permute-start.29 = (bf16[16,2048]{1,0:T(8,128)(2,1)S(1)}, bf16[16,2048]{1,0:T(8,128)(2,1)S(1)}, u32[]{:S(2)}, u32[]{:S(2)}) collective-permute-start(bf16[16,2048]{1,0:T(8,128)(2,1)S(1)} %outer_sum0.3.refs_0_), channel_id=1, source_target_pairs={{0,2},{2,0},{4,6},{6,4},{8,10},{10,8},{12,14},{14,12},{16,18},{18,... | collective-permute-start | bytes 196616 | tf_op jit(solution)/shard_map/ppermute | solution.py:205
  63.7 3.3 %collective-permute-start.27 = (bf16[16,4096]{1,0:T(8,128)(2,1)S(1)}, bf16[16,4096]{1,0:T(8,128)(2,1)S(1)}, u32[]{:S(2)}, u32[]{:S(2)}) collective-permute-start(bf16[16,4096]{1,0:T(8,128)(2,1)S(1)} %stack.3), channel_id=1, source_target_pairs={{0,6},{2,4},{4,2},{6,0},{8,14},{10,12},{12,10},{14,8},{16,22},{18,... | collective-permute-start | bytes 393224 | tf_op jit(solution)/shard_map/ppermute | solution.py:205
  67.0 0.6 collective-permute-start.21
  67.7 1.4 %project0.3.refs_1_ = f32[16,640]{1,0:T(8,128)S(1)} custom-call(f32[1,16384]{1,0:T(1,128)S(1)} %get-tuple-element.9.centre_ref, f32[1,16384]{1,0:T(1,128)S(1)} %get-tuple-element.10.root_ref, bf16[16384,512]{1,0:T(8,128)(2,1)S(1)} %get-tuple-element.11.turned_ref, bf16[16,2048]{1,0:T(8,128)(2,1)S(1)} %outer_sum0.3.refs_0_, ...), custom_call_target="tpu_custom_call" | custom-call | flops 939524096 | bytes 17170432 | tf_op jit(solution)/shard_map/project0/pallas_call | solution.py:28
  69.0 0.9 %collective-permute-done.27.refs_0_.refs_4_ = bf16[16,4096]{1,0:T(8,128)(2,1)S(1)} collective-permute-done((bf16[16,4096]{1,0:T(8,128)(2,1)S(1)}, bf16[16,4096]{1,0:T(8,128)(2,1)S(1)}, u32[]{:S(2)}, u32[]{:S(2)}) %collective-permute-start.27) | collective-permute-done | bytes 131104 | tf_op jit(solution)/shard_map/ppermute | solution.py:205
  70.0 0.7 project4.3.refs_1_
  70.7 0.6 collective-permute-done.22.refs_0_.refs_5_
  71.3 0.4 project5.3.refs_1_
  71.7 0.4 project6.3.own_ref
  72.2 1.2 %collective-permute-done.30.other_ref = f32[16,640]{1,0:T(8,128)S(1)} collective-permute-done((f32[16,640]{1,0:T(8,128)S(1)}, f32[16,640]{1,0:T(8,128)S(1)}, u32[]{:S(2)}, u32[]{:S(2)}) %collective-permute-start.30) | collective-permute-done | bytes 40992 | tf_op jit(solution)/shard_map/ppermute | solution.py:205
  73.4 1.6 %finish.1 = (f32[16,16384]{1,0:T(8,128)}, f32[16,512]{1,0:T(8,128)}) custom-call(f32[16,640]{1,0:T(8,128)S(1)} %project6.3.own_ref, f32[16,640]{1,0:T(8,128)S(1)} %collective-permute-done.30.other_ref, f32[1,16384]{1,0:T(1,128)S(1)} %get-tuple-element.10.root_ref, bf16[16,2048]{1,0:T(8,128)(2,1)S(1)} %outer_sum0.3.refs_0_, ...), custom_call_target="tpu_custom_call" | custom-call | tf_op jit(solution)/shard_map/finish/pallas_call | solution.py:341
  (37 shorter events, 1.7 us)
Async XLA Ops:
  8.1 1.4 %collective-permute-start = (bf16[16,512]{1,0:T(8,128)(2,1)S(1)}, bf16[16,512]{1,0:T(8,128)(2,1)S(1)}, u32[]{:S(2)}, u32[]{:S(2)}) collective-permute-start(bf16[16,512]{1,0:T(8,128)(2,1)S(1)} %get-tuple-element.13.refs_0_), channel_id=1, source_target_pairs={{0,1},{1,0},{2,3},{3,2},{4,5},{5,4},{6,7},{7,6},{8,9},{9,8},{10,11... | collective-permute-start | bytes 49160 | tf_op jit(solution)/shard_map/ppermute | solution.py:205
  10.1 9.8 %collective-permute-start.3 = (bf16[16,4096]{1,0:T(8,128)(2,1)S(1)}, bf16[16,4096]{1,0:T(8,128)(2,1)S(1)}, u32[]{:S(2)}, u32[]{:S(2)}) collective-permute-start(bf16[16,4096]{1,0:T(8,128)(2,1)S(1)} %terms23.2), channel_id=1, source_target_pairs={{0,6},{2,4},{4,2},{6,0},{8,14},{10,12},{12,10},{14,8},{16,22},{18,... | collective-permute-start | bytes 393224 | tf_op jit(solution)/shard_map/ppermute | solution.py:205
  14.3 5.6 %collective-permute-start.9 = (bf16[16,2048]{1,0:T(8,128)(2,1)S(1)}, bf16[16,2048]{1,0:T(8,128)(2,1)S(1)}, u32[]{:S(2)}, u32[]{:S(2)}) collective-permute-start(bf16[16,2048]{1,0:T(8,128)(2,1)S(1)} %terms02.2), channel_id=1, source_target_pairs={{0,4},{2,6},{4,0},{6,2},{8,12},{10,14},{12,8},{14,10},{16,20},{18,... | collective-permute-start | bytes 196616 | tf_op jit(solution)/shard_map/ppermute | solution.py:205
  15.2 4.7 %collective-permute-start.8 = (bf16[16,2048]{1,0:T(8,128)(2,1)S(1)}, bf16[16,2048]{1,0:T(8,128)(2,1)S(1)}, u32[]{:S(2)}, u32[]{:S(2)}) collective-permute-start(bf16[16,2048]{1,0:T(8,128)(2,1)S(1)} %terms01.2), channel_id=1, source_target_pairs={{0,2},{2,0},{4,6},{6,4},{8,10},{10,8},{12,14},{14,12},{16,18},{18,... | collective-permute-start | bytes 196616 | tf_op jit(solution)/shard_map/ppermute | solution.py:205
  15.6 6.4 %collective-permute-start.2 = (bf16[16,2048]{1,0:T(8,128)(2,1)S(1)}, bf16[16,2048]{1,0:T(8,128)(2,1)S(1)}, u32[]{:S(2)}, u32[]{:S(2)}) collective-permute-start(bf16[16,2048]{1,0:T(8,128)(2,1)S(1)} %terms12.2), channel_id=1, source_target_pairs={{0,4},{2,6},{4,0},{6,2},{8,12},{10,14},{12,8},{14,10},{16,20},{18,... | collective-permute-start | bytes 196616 | tf_op jit(solution)/shard_map/ppermute | solution.py:205
  18.0 4.3 %collective-permute-start.1 = (bf16[16,2048]{1,0:T(8,128)(2,1)S(1)}, bf16[16,2048]{1,0:T(8,128)(2,1)S(1)}, u32[]{:S(2)}, u32[]{:S(2)}) collective-permute-start(bf16[16,2048]{1,0:T(8,128)(2,1)S(1)} %terms11.2), channel_id=1, source_target_pairs={{0,2},{2,0},{4,6},{6,4},{8,10},{10,8},{12,14},{14,12},{16,18},{18,... | collective-permute-start | bytes 196616 | tf_op jit(solution)/shard_map/ppermute | solution.py:205
  20.0 4.3 %collective-permute-start.10 = (bf16[16,2048]{1,0:T(8,128)(2,1)S(1)}, bf16[16,2048]{1,0:T(8,128)(2,1)S(1)}, u32[]{:S(2)}, u32[]{:S(2)}) collective-permute-start(bf16[16,2048]{1,0:T(8,128)(2,1)S(1)} %inner_sum0.2.own_ref), channel_id=1, source_target_pairs={{0,8},{1,17},{2,10},{3,19},{4,12},{5,21},{6,14},{7,23},{8,0},{9,25... | collective-permute-start | bytes 196616 | tf_op jit(solution)/shard_map/ppermute | solution.py:211
  22.3 5.5 %collective-permute-start.4 = (bf16[16,2048]{1,0:T(8,128)(2,1)S(1)}, bf16[16,2048]{1,0:T(8,128)(2,1)S(1)}, u32[]{:S(2)}, u32[]{:S(2)}) collective-permute-start(bf16[16,2048]{1,0:T(8,128)(2,1)S(1)} %inner_sum1.2.own_ref), channel_id=1, source_target_pairs={{0,8},{1,17},{2,10},{3,19},{4,12},{5,21},{6,14},{7,23},{8,0},{9,25... | collective-permute-start | bytes 196616 | tf_op jit(solution)/shard_map/ppermute | solution.py:211
  24.3 5.3 %collective-permute-start.11 = (bf16[16,2048]{1,0:T(8,128)(2,1)S(1)}, bf16[16,2048]{1,0:T(8,128)(2,1)S(1)}, u32[]{:S(2)}, u32[]{:S(2)}) collective-permute-start(bf16[16,2048]{1,0:T(8,128)(2,1)S(1)} %pair_sum0.2.own_ref), channel_id=1, source_target_pairs={{0,16},{1,9},{2,18},{3,11},{4,20},{5,13},{6,22},{7,15},{8,24},{9,1... | collective-permute-start | bytes 196616 | tf_op jit(solution)/shard_map/ppermute | solution.py:211
  27.8 5.2 %collective-permute-start.5 = (bf16[16,2048]{1,0:T(8,128)(2,1)S(1)}, bf16[16,2048]{1,0:T(8,128)(2,1)S(1)}, u32[]{:S(2)}, u32[]{:S(2)}) collective-permute-start(bf16[16,2048]{1,0:T(8,128)(2,1)S(1)} %pair_sum1.2.own_ref), channel_id=1, source_target_pairs={{0,16},{1,9},{2,18},{3,11},{4,20},{5,13},{6,22},{7,15},{8,24},{9,1... | collective-permute-start | bytes 196616 | tf_op jit(solution)/shard_map/ppermute | solution.py:211
  29.6 7.2 %collective-permute-start.13 = (bf16[16,2048]{1,0:T(8,128)(2,1)S(1)}, bf16[16,2048]{1,0:T(8,128)(2,1)S(1)}, u32[]{:S(2)}, u32[]{:S(2)}) collective-permute-start(bf16[16,2048]{1,0:T(8,128)(2,1)S(1)} %outer_sum0.2.refs_0_), channel_id=1, source_target_pairs={{0,4},{2,6},{4,0},{6,2},{8,12},{10,14},{12,8},{14,10},{16,20},{18,... | collective-permute-start | bytes 196616 | tf_op jit(solution)/shard_map/ppermute | solution.py:205
  31.2 5.6 %collective-permute-start.14 = (bf16[16,2048]{1,0:T(8,128)(2,1)S(1)}, bf16[16,2048]{1,0:T(8,128)(2,1)S(1)}, u32[]{:S(2)}, u32[]{:S(2)}) collective-permute-start(bf16[16,2048]{1,0:T(8,128)(2,1)S(1)} %outer_sum0.2.refs_0_), channel_id=1, source_target_pairs={{0,2},{2,0},{4,6},{6,4},{8,10},{10,8},{12,14},{14,12},{16,18},{18,... | collective-permute-start | bytes 196616 | tf_op jit(solution)/shard_map/ppermute | solution.py:205
  33.1 6.0 %collective-permute-start.12 = (bf16[16,4096]{1,0:T(8,128)(2,1)S(1)}, bf16[16,4096]{1,0:T(8,128)(2,1)S(1)}, u32[]{:S(2)}, u32[]{:S(2)}) collective-permute-start(bf16[16,4096]{1,0:T(8,128)(2,1)S(1)} %stack.2), channel_id=1, source_target_pairs={{0,6},{2,4},{4,2},{6,0},{8,14},{10,12},{12,10},{14,8},{16,22},{18,... | collective-permute-start | bytes 393224 | tf_op jit(solution)/shard_map/ppermute | solution.py:205
  34.9 5.0 %collective-permute-start.7 = (bf16[16,2048]{1,0:T(8,128)(2,1)S(1)}, bf16[16,2048]{1,0:T(8,128)(2,1)S(1)}, u32[]{:S(2)}, u32[]{:S(2)}) collective-permute-start(bf16[16,2048]{1,0:T(8,128)(2,1)S(1)} %outer_sum1.2.refs_1_.refs_3_), channel_id=1, source_target_pairs={{0,4},{2,6},{4,0},{6,2},{8,12},{10,14},{12,8},{14,10},{16,20},{18,... | collective-permute-start | bytes 196616 | tf_op jit(solution)/shard_map/ppermute | solution.py:205
  36.8 4.3 %collective-permute-start.6 = (bf16[16,2048]{1,0:T(8,128)(2,1)S(1)}, bf16[16,2048]{1,0:T(8,128)(2,1)S(1)}, u32[]{:S(2)}, u32[]{:S(2)}) collective-permute-start(bf16[16,2048]{1,0:T(8,128)(2,1)S(1)} %outer_sum1.2.refs_1_.refs_3_), channel_id=1, source_target_pairs={{0,2},{2,0},{4,6},{6,4},{8,10},{10,8},{12,14},{14,12},{16,18},{18,... | collective-permute-start | bytes 196616 | tf_op jit(solution)/shard_map/ppermute | solution.py:205
  41.5 1.2 %collective-permute-start.15 = (f32[16,640]{1,0:T(8,128)S(1)}, f32[16,640]{1,0:T(8,128)S(1)}, u32[]{:S(2)}, u32[]{:S(2)}) collective-permute-start(f32[16,640]{1,0:T(8,128)S(1)} %project6.2.own_ref), channel_id=1, source_target_pairs={{0,1},{1,0},{2,3},{3,2},{4,5},{5,4},{6,7},{7,6},{8,9},{9,8},{10,11... | collective-permute-start | bytes 122888 | tf_op jit(solution)/shard_map/ppermute | solution.py:205
  43.9 8.6 %collective-permute-start.18 = (bf16[16,4096]{1,0:T(8,128)(2,1)S(1)}, bf16[16,4096]{1,0:T(8,128)(2,1)S(1)}, u32[]{:S(2)}, u32[]{:S(2)}) collective-permute-start(bf16[16,4096]{1,0:T(8,128)(2,1)S(1)} %terms23.3), channel_id=1, source_target_pairs={{0,6},{2,4},{4,2},{6,0},{8,14},{10,12},{12,10},{14,8},{16,22},{18,... | collective-permute-start | bytes 393224 | tf_op jit(solution)/shard_map/ppermute | solution.py:205
  45.2 6.7 %collective-permute-start.24 = (bf16[16,2048]{1,0:T(8,128)(2,1)S(1)}, bf16[16,2048]{1,0:T(8,128)(2,1)S(1)}, u32[]{:S(2)}, u32[]{:S(2)}) collective-permute-start(bf16[16,2048]{1,0:T(8,128)(2,1)S(1)} %terms02.3), channel_id=1, source_target_pairs={{0,4},{2,6},{4,0},{6,2},{8,12},{10,14},{12,8},{14,10},{16,20},{18,... | collective-permute-start | bytes 196616 | tf_op jit(solution)/shard_map/ppermute | solution.py:205
  47.5 4.9 %collective-permute-start.23 = (bf16[16,2048]{1,0:T(8,128)(2,1)S(1)}, bf16[16,2048]{1,0:T(8,128)(2,1)S(1)}, u32[]{:S(2)}, u32[]{:S(2)}) collective-permute-start(bf16[16,2048]{1,0:T(8,128)(2,1)S(1)} %terms01.3), channel_id=1, source_target_pairs={{0,2},{2,0},{4,6},{6,4},{8,10},{10,8},{12,14},{14,12},{16,18},{18,... | collective-permute-start | bytes 196616 | tf_op jit(solution)/shard_map/ppermute | solution.py:205
  48.5 4.8 %collective-permute-start.17 = (bf16[16,2048]{1,0:T(8,128)(2,1)S(1)}, bf16[16,2048]{1,0:T(8,128)(2,1)S(1)}, u32[]{:S(2)}, u32[]{:S(2)}) collective-permute-start(bf16[16,2048]{1,0:T(8,128)(2,1)S(1)} %terms12.3), channel_id=1, source_target_pairs={{0,4},{2,6},{4,0},{6,2},{8,12},{10,14},{12,8},{14,10},{16,20},{18,... | collective-permute-start | bytes 196616 | tf_op jit(solution)/shard_map/ppermute | solution.py:205
  49.6 4.3 %collective-permute-start.16 = (bf16[16,2048]{1,0:T(8,128)(2,1)S(1)}, bf16[16,2048]{1,0:T(8,128)(2,1)S(1)}, u32[]{:S(2)}, u32[]{:S(2)}) collective-permute-start(bf16[16,2048]{1,0:T(8,128)(2,1)S(1)} %terms11.3), channel_id=1, source_target_pairs={{0,2},{2,0},{4,6},{6,4},{8,10},{10,8},{12,14},{14,12},{16,18},{18,... | collective-permute-start | bytes 196616 | tf_op jit(solution)/shard_map/ppermute | solution.py:205
  52.5 4.5 %collective-permute-start.25 = (bf16[16,2048]{1,0:T(8,128)(2,1)S(1)}, bf16[16,2048]{1,0:T(8,128)(2,1)S(1)}, u32[]{:S(2)}, u32[]{:S(2)}) collective-permute-start(bf16[16,2048]{1,0:T(8,128)(2,1)S(1)} %inner_sum0.3.own_ref), channel_id=1, source_target_pairs={{0,8},{1,17},{2,10},{3,19},{4,12},{5,21},{6,14},{7,23},{8,0},{9,25... | collective-permute-start | bytes 196616 | tf_op jit(solution)/shard_map/ppermute | solution.py:211
  53.9 4.6 %collective-permute-start.19 = (bf16[16,2048]{1,0:T(8,128)(2,1)S(1)}, bf16[16,2048]{1,0:T(8,128)(2,1)S(1)}, u32[]{:S(2)}, u32[]{:S(2)}) collective-permute-start(bf16[16,2048]{1,0:T(8,128)(2,1)S(1)} %inner_sum1.3.own_ref), channel_id=1, source_target_pairs={{0,8},{1,17},{2,10},{3,19},{4,12},{5,21},{6,14},{7,23},{8,0},{9,25... | collective-permute-start | bytes 196616 | tf_op jit(solution)/shard_map/ppermute | solution.py:211
  57.0 5.7 %collective-permute-start.26 = (bf16[16,2048]{1,0:T(8,128)(2,1)S(1)}, bf16[16,2048]{1,0:T(8,128)(2,1)S(1)}, u32[]{:S(2)}, u32[]{:S(2)}) collective-permute-start(bf16[16,2048]{1,0:T(8,128)(2,1)S(1)} %pair_sum0.3.own_ref), channel_id=1, source_target_pairs={{0,16},{1,9},{2,18},{3,11},{4,20},{5,13},{6,22},{7,15},{8,24},{9,1... | collective-permute-start | bytes 196616 | tf_op jit(solution)/shard_map/ppermute | solution.py:211
  58.5 5.2 %collective-permute-start.20 = (bf16[16,2048]{1,0:T(8,128)(2,1)S(1)}, bf16[16,2048]{1,0:T(8,128)(2,1)S(1)}, u32[]{:S(2)}, u32[]{:S(2)}) collective-permute-start(bf16[16,2048]{1,0:T(8,128)(2,1)S(1)} %pair_sum1.3.own_ref), channel_id=1, source_target_pairs={{0,16},{1,9},{2,18},{3,11},{4,20},{5,13},{6,22},{7,15},{8,24},{9,1... | collective-permute-start | bytes 196616 | tf_op jit(solution)/shard_map/ppermute | solution.py:211
  62.7 5.0 %collective-permute-start.28 = (bf16[16,2048]{1,0:T(8,128)(2,1)S(1)}, bf16[16,2048]{1,0:T(8,128)(2,1)S(1)}, u32[]{:S(2)}, u32[]{:S(2)}) collective-permute-start(bf16[16,2048]{1,0:T(8,128)(2,1)S(1)} %outer_sum0.3.refs_0_), channel_id=1, source_target_pairs={{0,4},{2,6},{4,0},{6,2},{8,12},{10,14},{12,8},{14,10},{16,20},{18,... | collective-permute-start | bytes 196616 | tf_op jit(solution)/shard_map/ppermute | solution.py:205
  62.8 4.9 %collective-permute-start.29 = (bf16[16,2048]{1,0:T(8,128)(2,1)S(1)}, bf16[16,2048]{1,0:T(8,128)(2,1)S(1)}, u32[]{:S(2)}, u32[]{:S(2)}) collective-permute-start(bf16[16,2048]{1,0:T(8,128)(2,1)S(1)} %outer_sum0.3.refs_0_), channel_id=1, source_target_pairs={{0,2},{2,0},{4,6},{6,4},{8,10},{10,8},{12,14},{14,12},{16,18},{18,... | collective-permute-start | bytes 196616 | tf_op jit(solution)/shard_map/ppermute | solution.py:205
  63.7 6.2 %collective-permute-start.27 = (bf16[16,4096]{1,0:T(8,128)(2,1)S(1)}, bf16[16,4096]{1,0:T(8,128)(2,1)S(1)}, u32[]{:S(2)}, u32[]{:S(2)}) collective-permute-start(bf16[16,4096]{1,0:T(8,128)(2,1)S(1)} %stack.3), channel_id=1, source_target_pairs={{0,6},{2,4},{4,2},{6,0},{8,14},{10,12},{12,10},{14,8},{16,22},{18,... | collective-permute-start | bytes 393224 | tf_op jit(solution)/shard_map/ppermute | solution.py:205
  67.0 4.3 %collective-permute-start.22 = (bf16[16,2048]{1,0:T(8,128)(2,1)S(1)}, bf16[16,2048]{1,0:T(8,128)(2,1)S(1)}, u32[]{:S(2)}, u32[]{:S(2)}) collective-permute-start(bf16[16,2048]{1,0:T(8,128)(2,1)S(1)} %outer_sum1.3.refs_1_.refs_3_), channel_id=1, source_target_pairs={{0,4},{2,6},{4,0},{6,2},{8,12},{10,14},{12,8},{14,10},{16,20},{18,... | collective-permute-start | bytes 196616 | tf_op jit(solution)/shard_map/ppermute | solution.py:205
  67.0 4.7 %collective-permute-start.21 = (bf16[16,2048]{1,0:T(8,128)(2,1)S(1)}, bf16[16,2048]{1,0:T(8,128)(2,1)S(1)}, u32[]{:S(2)}, u32[]{:S(2)}) collective-permute-start(bf16[16,2048]{1,0:T(8,128)(2,1)S(1)} %outer_sum1.3.refs_1_.refs_3_), channel_id=1, source_target_pairs={{0,2},{2,0},{4,6},{6,4},{8,10},{10,8},{12,14},{14,12},{16,18},{18,... | collective-permute-start | bytes 196616 | tf_op jit(solution)/shard_map/ppermute | solution.py:205
  72.2 1.2 %collective-permute-start.30 = (f32[16,640]{1,0:T(8,128)S(1)}, f32[16,640]{1,0:T(8,128)S(1)}, u32[]{:S(2)}, u32[]{:S(2)}) collective-permute-start(f32[16,640]{1,0:T(8,128)S(1)} %project6.3.own_ref), channel_id=1, source_target_pairs={{0,1},{1,0},{2,3},{3,2},{4,5},{5,4},{6,7},{7,6},{8,9},{9,8},{10,11... | collective-permute-start | bytes 122888 | tf_op jit(solution)/shard_map/ppermute | solution.py:205

commit v4 on v3

--- a/solution.py
+++ b/solution.py
@@ -9,6 +9,7 @@
 
 ITERS = 2
 HALVES = 2
+DIAGONAL, SIDE, OTHER_SIDE = 3, 4, 5
 MIB = 1 << 20
 LANES = 128
 HERE = pl.BlockSpec(memory_space=pltpu.VMEM)
@@ -150,6 +151,8 @@
 
 def columns_of(key, inner, width, cols):
     turn, half = key
+    core = lax.axis_index("var")
+    turn = {SIDE: 2 - core, OTHER_SIDE: 1 + core}.get(turn, turn)
     group = cols // inner
     place = lax.rem(lax.axis_index("samp"), inner) ^ turn
     return pl.ds(pl.multiple_of(place * group + (half or 0) * (group // HALVES), group // HALVES), width)
@@ -213,11 +216,12 @@
 
 def sum_over_samples(sample_rows, kept, centre, root, inner):
     count, near, far = 4 * inner, inner, 2 * inner
-    x, y, diagonal = 1, 2, 3
-    across = swap(terms(sample_rows, kept, centre, (diagonal, None), inner), "samp", count, diagonal)
+    meet = {DIAGONAL: (3, 3), SIDE: (2, 1), OTHER_SIDE: (1, 2)}
+    across = swap_across(terms(sample_rows, kept, centre, (DIAGONAL, None), inner), count, meet[DIAGONAL])
     pieces = {}
     for h in range(HALVES):
-        received = [swap(terms(sample_rows, kept, centre, (t, h), inner), "samp", count, t) for t in (x, y)]
+        sides = OTHER_SIDE, SIDE
+        received = [swap_across(terms(sample_rows, kept, centre, (t, h), inner), count, meet[t]) for t in sides]
         own = terms(sample_rows, kept, centre, (0, h), inner, jnp.float32)
         piece = shape(own.shape)
         body = functools.partial(inner_sum_body, h)
@@ -226,12 +230,12 @@
         body = functools.partial(outer_sum_body, (0, h), inner)
         whole = call(body, piece, (root, pair, swap_across(pair, count, (far, near))), own.size, "outer_sum%d" % h)
         pieces[0, h] = whole
-        for t in (y, x):
-            pieces[t, h] = swap(whole, "samp", count, t)
+        for t in (SIDE, OTHER_SIDE):
+            pieces[t, h] = swap_across(whole, count, meet[t])
     both = [pieces[0, h] for h in range(HALVES)]
     group = shape((both[0].shape[0], HALVES * both[0].shape[1]))
-    pieces[diagonal, None] = swap(call(stack_body, group, tuple(both), 0, "stack"), "samp", count, diagonal)
-    order = [(0, 0), (y, 0), (x, 0), (0, 1), (diagonal, None), (y, 1), (x, 1)]
+    pieces[DIAGONAL, None] = swap_across(call(stack_body, group, tuple(both), 0, "stack"), count, meet[DIAGONAL])
+    order = [(0, 0), (SIDE, 0), (OTHER_SIDE, 0), (0, 1), (DIAGONAL, None), (SIDE, 1), (OTHER_SIDE, 1)]
     return {key: pieces[key] for key in order}
 
 
@@ -290,21 +294,24 @@
     return (right * scale)[:, :block]
 
 
-def solve_both(own_ref, other_ref):
+def inverse_of(own_ref, other_ref):
     rows = own_ref.shape[1] - LANES
-    inverse = inverse_factor(own_ref[:, rows:] + other_ref[:, rows:])
-    projected = lax.dot_general(
+    return inverse_factor(own_ref[:, rows:] + other_ref[:, rows:])
+
+
+def applied(inverse, own_ref, other_ref):
+    rows = own_ref.shape[1] - LANES
+    return lax.dot_general(
         inverse,
         own_ref[:, :rows] + other_ref[:, :rows],
         (((1,), (0,)), ((), ())),
         precision=lax.Precision.HIGHEST,
         preferred_element_type=jnp.float32,
     )
-    return inverse, projected
 
 
 def solve_body(own_ref, other_ref, out_ref):
-    out_ref[...] = solve_both(own_ref, other_ref)[1].astype(out_ref.dtype)
+    out_ref[...] = applied(inverse_of(own_ref, other_ref), own_ref, other_ref).astype(out_ref.dtype)
 
 
 def solve(own, other):
@@ -315,10 +322,8 @@
 def finish_body(scaling, order, inner, own_ref, other_ref, root_ref, *refs):
     pieces, (out, scores, held, kept_scores, sems) = refs[:-5], refs[-5:]
     block, cols = held.shape
-    inverse, projected = solve_both(own_ref, other_ref)
-    kept_scores[...] = projected
-    copies = [pltpu.make_async_copy(kept_scores, scores, sems.at[len(order)])]
-    copies[0].start()
+    inverse = inverse_of(own_ref, other_ref)
+    copies = []
     split = jnp.concatenate(in_parts(inverse * scaling, 2), axis=0).astype(jnp.bfloat16)
     done = 0
     for at, (key, piece) in enumerate(zip(order, pieces)):
@@ -330,6 +335,9 @@
         copies.append(pltpu.make_async_copy(held.at[:, here], out.at[:, columns], sems.at[at]))
         copies[-1].start()
         done += width
+    kept_scores[...] = applied(inverse, own_ref, other_ref)
+    copies.append(pltpu.make_async_copy(kept_scores, scores, sems.at[len(order)]))
+    copies[-1].start()
     for copy in copies:
         copy.wait()
 

time: 75.3 us -> 75.3 us (level)
  waiting for transfers between devices: 15.2 us -> 12.6 us
  starting transfers between devices: 37.5 us -> 40 us
    ppermute x8 -> x28, starting transfers between devices: 13 us -> 39.5 us  [swap_across(): return lax.ppermute(x, ('samp', 'var'), pairs)]
    ppermute x23 -> x3, starting transfers between devices: 24.4 us -> 0.52 us  [swap(): return lax.ppermute(x, axis, [(d, d ^ turn) for d in range(size)])]
    ppermute x23 -> x3, waiting for transfers between devices: 9.03 us -> 3.31 us  [swap(): return lax.ppermute(x, axis, [(d, d ^ turn) for d in range(size)])]
    ppermute x8 -> x28, waiting for transfers between devices: 6.18 us -> 9.32 us  [swap_across(): return lax.ppermute(x, ('samp', 'var'), pairs)]
where the time goes in v4:
time: 75.3 us; the launch traced here: 75.1 us
  starting transfers between devices  40 us (53%)
  Pallas kernels  21.5 us (29%)
  waiting for transfers between devices  12.6 us (17%)
  between operations  0.93 us (1%)
    ppermute x28, starting transfers between devices, swap_across(): return lax.ppermute(x, ('samp', 'var'), pairs)  39.5 us
    pallas_call x37, Pallas kernels, call(): pl.pallas_call(body, out_shape=out, in_specs=[HERE] * len(operands), out_...  12.6 us
    ppermute x28, waiting for transfers between devices, swap_across(): return lax.ppermute(x, ('samp', 'var'), pairs)  9.32 us
    pallas_call x1, Pallas kernels, load(): pl.pallas_call(functools.partial(load_body, width, 8), in_specs=[anywhere...  7.41 us
    ppermute x3, waiting for transfers between devices, swap(): return lax.ppermute(x, axis, [(d, d ^ turn) for d in range(size)])  3.31 us
    pallas_call x1, Pallas kernels, finish(): pl.pallas_call(functools.partial(finish_body, scaling, order, inner), out...  1.53 us
  transfers between devices with their start and end apart: 31, of which 18 were waited for; matrix products, arithmetic and copies ran while one was open for 0% of the time, Pallas kernels for 13%

profile of v4, /device:TPU:0, one launch (start us, length us, event | category | flops | bytes accessed | tf_op | source)
XLA Modules:
  0.0 75.1 jit_solution(10717615955368989403)
XLA Ops:
  0.6 7.4 %load.1 = (bf16[512,16384]{1,0:T(8,128)(2,1)S(1)}, bf16[16384,512]{1,0:T(8,128)(2,1)S(1)}, bf16[16,512]{1,0:T(8,128)(2,1)S(1)}, f32[1,16384]{1,0:T(1,128)S(1)}, f32[1,16384]{1,0:T(1,128)S(1)}) custom-call(bf16[512,16384]{1,0:T(8,128)(2,1)} %g_ref.1, f32[128,128]{1,0:T(8,128)} %bitcast.5, f32[16,16384]{1,0:T(8,128)} %bitcast.4), custom_call_target="tpu_custom_call" | custom-call | tf_op jit(solution)/shard_map/load/pallas_call | solution.py:130
  8.1 0.5 collective-permute-start
  8.6 0.8 %collective-permute-done.refs_1_ = bf16[16,512]{1,0:T(8,128)(2,1)S(1)} collective-permute-done((bf16[16,512]{1,0:T(8,128)(2,1)S(1)}, bf16[16,512]{1,0:T(8,128)(2,1)S(1)}, u32[]{:S(2)}, u32[]{:S(2)}) %collective-permute-start) | collective-permute-done | bytes 16416 | tf_op jit(solution)/shard_map/ppermute | solution.py:208
  9.4 0.7 terms23.2
  10.1 3.8 %collective-permute-start.3 = (bf16[16,4096]{1,0:T(8,128)(2,1)S(1)}, bf16[16,4096]{1,0:T(8,128)(2,1)S(1)}, u32[]{:S(2)}, u32[]{:S(2)}) collective-permute-start(bf16[16,4096]{1,0:T(8,128)(2,1)S(1)} %terms23.2), channel_id=1, source_target_pairs={{0,6},{1,7},{2,4},{3,5},{4,2},{5,3},{6,0},{7,1},{8,14},{9,15},{10,... | collective-permute-start | bytes 393224 | tf_op jit(solution)/shard_map/ppermute | solution.py:214
  13.9 0.4 terms04.2
  14.3 0.5 collective-permute-start.9
  14.8 0.4 terms05.2
  15.2 0.4 terms14.2
  15.6 2.0 %collective-permute-start.2 = (bf16[16,2048]{1,0:T(8,128)(2,1)S(1)}, bf16[16,2048]{1,0:T(8,128)(2,1)S(1)}, u32[]{:S(2)}, u32[]{:S(2)}) collective-permute-start(bf16[16,2048]{1,0:T(8,128)(2,1)S(1)} %terms14.2), channel_id=1, source_target_pairs={{0,4},{1,3},{2,6},{3,1},{4,0},{5,7},{6,2},{7,5},{8,12},{9,11},{10,... | collective-permute-start | bytes 196616 | tf_op jit(solution)/shard_map/ppermute | solution.py:214
  17.6 0.4 terms15.2
  18.0 1.5 %collective-permute-start.1 = (bf16[16,2048]{1,0:T(8,128)(2,1)S(1)}, bf16[16,2048]{1,0:T(8,128)(2,1)S(1)}, u32[]{:S(2)}, u32[]{:S(2)}) collective-permute-start(bf16[16,2048]{1,0:T(8,128)(2,1)S(1)} %terms15.2), channel_id=1, source_target_pairs={{0,2},{1,5},{2,0},{3,7},{4,6},{5,1},{6,4},{7,3},{8,10},{9,13},{10,... | collective-permute-start | bytes 196616 | tf_op jit(solution)/shard_map/ppermute | solution.py:214
  19.5 0.4 terms00.2.own_ref
  20.1 1.6 %collective-permute-start.10 = (bf16[16,2048]{1,0:T(8,128)(2,1)S(1)}, bf16[16,2048]{1,0:T(8,128)(2,1)S(1)}, u32[]{:S(2)}, u32[]{:S(2)}) collective-permute-start(bf16[16,2048]{1,0:T(8,128)(2,1)S(1)} %inner_sum0.2.own_ref), channel_id=1, source_target_pairs={{0,8},{1,17},{2,10},{3,19},{4,12},{5,21},{6,14},{7,23},{8,0},{9,25... | collective-permute-start | bytes 196616 | tf_op jit(solution)/shard_map/ppermute | solution.py:214
  21.7 0.4 terms10.2.own_ref
  22.3 1.6 %collective-permute-start.4 = (bf16[16,2048]{1,0:T(8,128)(2,1)S(1)}, bf16[16,2048]{1,0:T(8,128)(2,1)S(1)}, u32[]{:S(2)}, u32[]{:S(2)}) collective-permute-start(bf16[16,2048]{1,0:T(8,128)(2,1)S(1)} %inner_sum1.2.own_ref), channel_id=1, source_target_pairs={{0,8},{1,17},{2,10},{3,19},{4,12},{5,21},{6,14},{7,23},{8,0},{9,25... | collective-permute-start | bytes 196616 | tf_op jit(solution)/shard_map/ppermute | solution.py:214
  24.0 0.5 collective-permute-done.10.other_ref
  24.4 2.7 %collective-permute-start.11 = (bf16[16,2048]{1,0:T(8,128)(2,1)S(1)}, bf16[16,2048]{1,0:T(8,128)(2,1)S(1)}, u32[]{:S(2)}, u32[]{:S(2)}) collective-permute-start(bf16[16,2048]{1,0:T(8,128)(2,1)S(1)} %pair_sum0.2.own_ref), channel_id=1, source_target_pairs={{0,16},{1,9},{2,18},{3,11},{4,20},{5,13},{6,22},{7,15},{8,24},{9,1... | collective-permute-start | bytes 196616 | tf_op jit(solution)/shard_map/ppermute | solution.py:214
  27.1 0.7 collective-permute-done.4.other_ref
  27.9 1.6 %collective-permute-start.5 = (bf16[16,2048]{1,0:T(8,128)(2,1)S(1)}, bf16[16,2048]{1,0:T(8,128)(2,1)S(1)}, u32[]{:S(2)}, u32[]{:S(2)}) collective-permute-start(bf16[16,2048]{1,0:T(8,128)(2,1)S(1)} %pair_sum1.2.own_ref), channel_id=1, source_target_pairs={{0,16},{1,9},{2,18},{3,11},{4,20},{5,13},{6,22},{7,15},{8,24},{9,1... | collective-permute-start | bytes 196616 | tf_op jit(solution)/shard_map/ppermute | solution.py:214
  29.8 1.5 %collective-permute-start.13 = (bf16[16,2048]{1,0:T(8,128)(2,1)S(1)}, bf16[16,2048]{1,0:T(8,128)(2,1)S(1)}, u32[]{:S(2)}, u32[]{:S(2)}) collective-permute-start(bf16[16,2048]{1,0:T(8,128)(2,1)S(1)} %outer_sum0.2.refs_0_), channel_id=1, source_target_pairs={{0,4},{1,3},{2,6},{3,1},{4,0},{5,7},{6,2},{7,5},{8,12},{9,11},{10,... | collective-permute-start | bytes 196616 | tf_op jit(solution)/shard_map/ppermute | solution.py:214
  31.3 1.4 %collective-permute-start.14 = (bf16[16,2048]{1,0:T(8,128)(2,1)S(1)}, bf16[16,2048]{1,0:T(8,128)(2,1)S(1)}, u32[]{:S(2)}, u32[]{:S(2)}) collective-permute-start(bf16[16,2048]{1,0:T(8,128)(2,1)S(1)} %outer_sum0.2.refs_0_), channel_id=1, source_target_pairs={{0,2},{1,5},{2,0},{3,7},{4,6},{5,1},{6,4},{7,3},{8,10},{9,13},{10,... | collective-permute-start | bytes 196616 | tf_op jit(solution)/shard_map/ppermute | solution.py:214
  32.7 0.4 collective-permute-done.5.other_ref
  33.1 1.0 %collective-permute-start.12 = (bf16[16,4096]{1,0:T(8,128)(2,1)S(1)}, bf16[16,4096]{1,0:T(8,128)(2,1)S(1)}, u32[]{:S(2)}, u32[]{:S(2)}) collective-permute-start(bf16[16,4096]{1,0:T(8,128)(2,1)S(1)} %stack.2), channel_id=1, source_target_pairs={{0,6},{1,7},{2,4},{3,5},{4,2},{5,3},{6,0},{7,1},{8,14},{9,15},{10,... | collective-permute-start | bytes 393224 | tf_op jit(solution)/shard_map/ppermute | solution.py:214
  34.1 2.1 %collective-permute-start.7 = (bf16[16,2048]{1,0:T(8,128)(2,1)S(1)}, bf16[16,2048]{1,0:T(8,128)(2,1)S(1)}, u32[]{:S(2)}, u32[]{:S(2)}) collective-permute-start(bf16[16,2048]{1,0:T(8,128)(2,1)S(1)} %outer_sum1.2.refs_1_.refs_3_), channel_id=1, source_target_pairs={{0,4},{1,3},{2,6},{3,1},{4,0},{5,7},{6,2},{7,5},{8,12},{9,11},{10,... | collective-permute-start | bytes 196616 | tf_op jit(solution)/shard_map/ppermute | solution.py:214
  36.2 0.5 collective-permute-start.6
  36.7 1.4 %project0.2.refs_1_ = f32[16,640]{1,0:T(8,128)S(1)} custom-call(f32[1,16384]{1,0:T(1,128)S(1)} %get-tuple-element.9.centre_ref, f32[1,16384]{1,0:T(1,128)S(1)} %get-tuple-element.10.root_ref, bf16[16384,512]{1,0:T(8,128)(2,1)S(1)} %get-tuple-element.11.turned_ref, bf16[16,2048]{1,0:T(8,128)(2,1)S(1)} %outer_sum0.2.refs_0_, ...), custom_call_target="tpu_custom_call" | custom-call | flops 939524096 | bytes 17170432 | tf_op jit(solution)/shard_map/project0/pallas_call | solution.py:29
  38.1 1.1 %collective-permute-done.12.refs_0_ = bf16[16,4096]{1,0:T(8,128)(2,1)S(1)} collective-permute-done((bf16[16,4096]{1,0:T(8,128)(2,1)S(1)}, bf16[16,4096]{1,0:T(8,128)(2,1)S(1)}, u32[]{:S(2)}, u32[]{:S(2)}) %collective-permute-start.12) | collective-permute-done | bytes 131104 | tf_op jit(solution)/shard_map/ppermute | solution.py:214
  39.2 0.7 project4.2.refs_1_
  39.9 0.5 project5.2.refs_1_
  40.5 0.4 project6.2.own_ref
  40.9 1.2 %collective-permute-done.15.other_ref = f32[16,640]{1,0:T(8,128)S(1)} collective-permute-done((f32[16,640]{1,0:T(8,128)S(1)}, f32[16,640]{1,0:T(8,128)S(1)}, u32[]{:S(2)}, u32[]{:S(2)}) %collective-permute-start.15) | collective-permute-done | bytes 40992 | tf_op jit(solution)/shard_map/ppermute | solution.py:208
  42.1 0.4 solve.1.refs_0_
  42.5 0.7 terms23.3
  43.2 1.1 %collective-permute-start.18 = (bf16[16,4096]{1,0:T(8,128)(2,1)S(1)}, bf16[16,4096]{1,0:T(8,128)(2,1)S(1)}, u32[]{:S(2)}, u32[]{:S(2)}) collective-permute-start(bf16[16,4096]{1,0:T(8,128)(2,1)S(1)} %terms23.3), channel_id=1, source_target_pairs={{0,6},{1,7},{2,4},{3,5},{4,2},{5,3},{6,0},{7,1},{8,14},{9,15},{10,... | collective-permute-start | bytes 393224 | tf_op jit(solution)/shard_map/ppermute | solution.py:214
  44.4 0.4 terms04.3
  44.8 1.7 %collective-permute-start.24 = (bf16[16,2048]{1,0:T(8,128)(2,1)S(1)}, bf16[16,2048]{1,0:T(8,128)(2,1)S(1)}, u32[]{:S(2)}, u32[]{:S(2)}) collective-permute-start(bf16[16,2048]{1,0:T(8,128)(2,1)S(1)} %terms04.3), channel_id=1, source_target_pairs={{0,4},{1,3},{2,6},{3,1},{4,0},{5,7},{6,2},{7,5},{8,12},{9,11},{10,... | collective-permute-start | bytes 196616 | tf_op jit(solution)/shard_map/ppermute | solution.py:214
  46.4 0.4 terms05.3
  46.8 0.7 collective-permute-start.23
  47.5 0.4 terms14.3
  47.9 0.4 collective-permute-start.17
  48.3 0.4 terms15.3
  48.7 1.3 %collective-permute-start.16 = (bf16[16,2048]{1,0:T(8,128)(2,1)S(1)}, bf16[16,2048]{1,0:T(8,128)(2,1)S(1)}, u32[]{:S(2)}, u32[]{:S(2)}) collective-permute-start(bf16[16,2048]{1,0:T(8,128)(2,1)S(1)} %terms15.3), channel_id=1, source_target_pairs={{0,2},{1,5},{2,0},{3,7},{4,6},{5,1},{6,4},{7,3},{8,10},{9,13},{10,... | collective-permute-start | bytes 196616 | tf_op jit(solution)/shard_map/ppermute | solution.py:214
  50.4 0.7 collective-permute-done.24.refs_1_
  51.3 2.0 %collective-permute-start.25 = (bf16[16,2048]{1,0:T(8,128)(2,1)S(1)}, bf16[16,2048]{1,0:T(8,128)(2,1)S(1)}, u32[]{:S(2)}, u32[]{:S(2)}) collective-permute-start(bf16[16,2048]{1,0:T(8,128)(2,1)S(1)} %inner_sum0.3.own_ref), channel_id=1, source_target_pairs={{0,8},{1,17},{2,10},{3,19},{4,12},{5,21},{6,14},{7,23},{8,0},{9,25... | collective-permute-start | bytes 196616 | tf_op jit(solution)/shard_map/ppermute | solution.py:214
  53.2 0.4 terms10.3.own_ref
  53.7 1.8 %collective-permute-start.19 = (bf16[16,2048]{1,0:T(8,128)(2,1)S(1)}, bf16[16,2048]{1,0:T(8,128)(2,1)S(1)}, u32[]{:S(2)}, u32[]{:S(2)}) collective-permute-start(bf16[16,2048]{1,0:T(8,128)(2,1)S(1)} %inner_sum1.3.own_ref), channel_id=1, source_target_pairs={{0,8},{1,17},{2,10},{3,19},{4,12},{5,21},{6,14},{7,23},{8,0},{9,25... | collective-permute-start | bytes 196616 | tf_op jit(solution)/shard_map/ppermute | solution.py:214
  55.5 0.8 %collective-permute-done.25.other_ref = bf16[16,2048]{1,0:T(8,128)(2,1)S(1)} collective-permute-done((bf16[16,2048]{1,0:T(8,128)(2,1)S(1)}, bf16[16,2048]{1,0:T(8,128)(2,1)S(1)}, u32[]{:S(2)}, u32[]{:S(2)}) %collective-permute-start.25) | collective-permute-done | bytes 65568 | tf_op jit(solution)/shard_map/ppermute | solution.py:214
  56.2 2.0 %collective-permute-start.26 = (bf16[16,2048]{1,0:T(8,128)(2,1)S(1)}, bf16[16,2048]{1,0:T(8,128)(2,1)S(1)}, u32[]{:S(2)}, u32[]{:S(2)}) collective-permute-start(bf16[16,2048]{1,0:T(8,128)(2,1)S(1)} %pair_sum0.3.own_ref), channel_id=1, source_target_pairs={{0,16},{1,9},{2,18},{3,11},{4,20},{5,13},{6,22},{7,15},{8,24},{9,1... | collective-permute-start | bytes 196616 | tf_op jit(solution)/shard_map/ppermute | solution.py:214
  58.2 1.0 %collective-permute-done.19.other_ref = bf16[16,2048]{1,0:T(8,128)(2,1)S(1)} collective-permute-done((bf16[16,2048]{1,0:T(8,128)(2,1)S(1)}, bf16[16,2048]{1,0:T(8,128)(2,1)S(1)}, u32[]{:S(2)}, u32[]{:S(2)}) %collective-permute-start.19) | collective-permute-done | bytes 65568 | tf_op jit(solution)/shard_map/ppermute | solution.py:214
  59.3 1.2 %collective-permute-start.20 = (bf16[16,2048]{1,0:T(8,128)(2,1)S(1)}, bf16[16,2048]{1,0:T(8,128)(2,1)S(1)}, u32[]{:S(2)}, u32[]{:S(2)}) collective-permute-start(bf16[16,2048]{1,0:T(8,128)(2,1)S(1)} %pair_sum1.3.own_ref), channel_id=1, source_target_pairs={{0,16},{1,9},{2,18},{3,11},{4,20},{5,13},{6,22},{7,15},{8,24},{9,1... | collective-permute-start | bytes 196616 | tf_op jit(solution)/shard_map/ppermute | solution.py:214
  60.5 1.1 %collective-permute-done.26.other_ref = bf16[16,2048]{1,0:T(8,128)(2,1)S(1)} collective-permute-done((bf16[16,2048]{1,0:T(8,128)(2,1)S(1)}, bf16[16,2048]{1,0:T(8,128)(2,1)S(1)}, u32[]{:S(2)}, u32[]{:S(2)}) %collective-permute-start.26) | collective-permute-done | bytes 65568 | tf_op jit(solution)/shard_map/ppermute | solution.py:214
  61.6 0.8 %collective-permute-start.28 = (bf16[16,2048]{1,0:T(8,128)(2,1)S(1)}, bf16[16,2048]{1,0:T(8,128)(2,1)S(1)}, u32[]{:S(2)}, u32[]{:S(2)}) collective-permute-start(bf16[16,2048]{1,0:T(8,128)(2,1)S(1)} %outer_sum0.3.refs_0_), channel_id=1, source_target_pairs={{0,4},{1,3},{2,6},{3,1},{4,0},{5,7},{6,2},{7,5},{8,12},{9,11},{10,... | collective-permute-start | bytes 196616 | tf_op jit(solution)/shard_map/ppermute | solution.py:214
  62.4 1.1 %collective-permute-start.29 = (bf16[16,2048]{1,0:T(8,128)(2,1)S(1)}, bf16[16,2048]{1,0:T(8,128)(2,1)S(1)}, u32[]{:S(2)}, u32[]{:S(2)}) collective-permute-start(bf16[16,2048]{1,0:T(8,128)(2,1)S(1)} %outer_sum0.3.refs_0_), channel_id=1, source_target_pairs={{0,2},{1,5},{2,0},{3,7},{4,6},{5,1},{6,4},{7,3},{8,10},{9,13},{10,... | collective-permute-start | bytes 196616 | tf_op jit(solution)/shard_map/ppermute | solution.py:214
  63.5 1.0 %collective-permute-done.20.other_ref = bf16[16,2048]{1,0:T(8,128)(2,1)S(1)} collective-permute-done((bf16[16,2048]{1,0:T(8,128)(2,1)S(1)}, bf16[16,2048]{1,0:T(8,128)(2,1)S(1)}, u32[]{:S(2)}, u32[]{:S(2)}) %collective-permute-start.20) | collective-permute-done | bytes 65568 | tf_op jit(solution)/shard_map/ppermute | solution.py:214
  64.5 1.1 %collective-permute-start.27 = (bf16[16,4096]{1,0:T(8,128)(2,1)S(1)}, bf16[16,4096]{1,0:T(8,128)(2,1)S(1)}, u32[]{:S(2)}, u32[]{:S(2)}) collective-permute-start(bf16[16,4096]{1,0:T(8,128)(2,1)S(1)} %stack.3), channel_id=1, source_target_pairs={{0,6},{1,7},{2,4},{3,5},{4,2},{5,3},{6,0},{7,1},{8,14},{9,15},{10,... | collective-permute-start | bytes 393224 | tf_op jit(solution)/shard_map/ppermute | solution.py:214
  66.1 2.0 %collective-permute-start.21 = (bf16[16,2048]{1,0:T(8,128)(2,1)S(1)}, bf16[16,2048]{1,0:T(8,128)(2,1)S(1)}, u32[]{:S(2)}, u32[]{:S(2)}) collective-permute-start(bf16[16,2048]{1,0:T(8,128)(2,1)S(1)} %outer_sum1.3.refs_1_.refs_3_), channel_id=1, source_target_pairs={{0,2},{1,5},{2,0},{3,7},{4,6},{5,1},{6,4},{7,3},{8,10},{9,13},{10,... | collective-permute-start | bytes 196616 | tf_op jit(solution)/shard_map/ppermute | solution.py:214
  68.1 1.4 %project0.3.refs_1_ = f32[16,640]{1,0:T(8,128)S(1)} custom-call(f32[1,16384]{1,0:T(1,128)S(1)} %get-tuple-element.9.centre_ref, f32[1,16384]{1,0:T(1,128)S(1)} %get-tuple-element.10.root_ref, bf16[16384,512]{1,0:T(8,128)(2,1)S(1)} %get-tuple-element.11.turned_ref, bf16[16,2048]{1,0:T(8,128)(2,1)S(1)} %outer_sum0.3.refs_0_, ...), custom_call_target="tpu_custom_call" | custom-call | flops 939524096 | bytes 17170432 | tf_op jit(solution)/shard_map/project0/pallas_call | solution.py:29
  69.5 1.1 %collective-permute-done.27.refs_0_.refs_4_ = bf16[16,4096]{1,0:T(8,128)(2,1)S(1)} collective-permute-done((bf16[16,4096]{1,0:T(8,128)(2,1)S(1)}, bf16[16,4096]{1,0:T(8,128)(2,1)S(1)}, u32[]{:S(2)}, u32[]{:S(2)}) %collective-permute-start.27) | collective-permute-done | bytes 131104 | tf_op jit(solution)/shard_map/ppermute | solution.py:214
  70.6 0.7 project4.3.refs_1_
  71.3 0.5 project5.3.refs_1_
  71.7 0.4 project6.3.own_ref
  72.2 1.2 %collective-permute-done.30.other_ref = f32[16,640]{1,0:T(8,128)S(1)} collective-permute-done((f32[16,640]{1,0:T(8,128)S(1)}, f32[16,640]{1,0:T(8,128)S(1)}, u32[]{:S(2)}, u32[]{:S(2)}) %collective-permute-start.30) | collective-permute-done | bytes 40992 | tf_op jit(solution)/shard_map/ppermute | solution.py:208
  73.4 1.5 %finish.1 = (f32[16,16384]{1,0:T(8,128)}, f32[16,512]{1,0:T(8,128)}) custom-call(f32[16,640]{1,0:T(8,128)S(1)} %project6.3.own_ref, f32[16,640]{1,0:T(8,128)S(1)} %collective-permute-done.30.other_ref, f32[1,16384]{1,0:T(1,128)S(1)} %get-tuple-element.10.root_ref, bf16[16,2048]{1,0:T(8,128)(2,1)S(1)} %outer_sum0.3.refs_0_, ...), custom_call_target="tpu_custom_call" | custom-call | tf_op jit(solution)/shard_map/finish/pallas_call | solution.py:349
  (37 shorter events, 2.1 us)
Async XLA Ops:
  8.1 1.4 %collective-permute-start = (bf16[16,512]{1,0:T(8,128)(2,1)S(1)}, bf16[16,512]{1,0:T(8,128)(2,1)S(1)}, u32[]{:S(2)}, u32[]{:S(2)}) collective-permute-start(bf16[16,512]{1,0:T(8,128)(2,1)S(1)} %get-tuple-element.13.refs_0_), channel_id=1, source_target_pairs={{0,1},{1,0},{2,3},{3,2},{4,5},{5,4},{6,7},{7,6},{8,9},{9,8},{10,11... | collective-permute-start | bytes 49160 | tf_op jit(solution)/shard_map/ppermute | solution.py:208
  10.1 10.0 %collective-permute-start.3 = (bf16[16,4096]{1,0:T(8,128)(2,1)S(1)}, bf16[16,4096]{1,0:T(8,128)(2,1)S(1)}, u32[]{:S(2)}, u32[]{:S(2)}) collective-permute-start(bf16[16,4096]{1,0:T(8,128)(2,1)S(1)} %terms23.2), channel_id=1, source_target_pairs={{0,6},{1,7},{2,4},{3,5},{4,2},{5,3},{6,0},{7,1},{8,14},{9,15},{10,... | collective-permute-start | bytes 393224 | tf_op jit(solution)/shard_map/ppermute | solution.py:214
  14.3 5.6 %collective-permute-start.9 = (bf16[16,2048]{1,0:T(8,128)(2,1)S(1)}, bf16[16,2048]{1,0:T(8,128)(2,1)S(1)}, u32[]{:S(2)}, u32[]{:S(2)}) collective-permute-start(bf16[16,2048]{1,0:T(8,128)(2,1)S(1)} %terms04.2), channel_id=1, source_target_pairs={{0,4},{1,3},{2,6},{3,1},{4,0},{5,7},{6,2},{7,5},{8,12},{9,11},{10,... | collective-permute-start | bytes 196616 | tf_op jit(solution)/shard_map/ppermute | solution.py:214
  15.2 4.9 %collective-permute-start.8 = (bf16[16,2048]{1,0:T(8,128)(2,1)S(1)}, bf16[16,2048]{1,0:T(8,128)(2,1)S(1)}, u32[]{:S(2)}, u32[]{:S(2)}) collective-permute-start(bf16[16,2048]{1,0:T(8,128)(2,1)S(1)} %terms05.2), channel_id=1, source_target_pairs={{0,2},{1,5},{2,0},{3,7},{4,6},{5,1},{6,4},{7,3},{8,10},{9,13},{10,... | collective-permute-start | bytes 196616 | tf_op jit(solution)/shard_map/ppermute | solution.py:214
  15.6 6.5 %collective-permute-start.2 = (bf16[16,2048]{1,0:T(8,128)(2,1)S(1)}, bf16[16,2048]{1,0:T(8,128)(2,1)S(1)}, u32[]{:S(2)}, u32[]{:S(2)}) collective-permute-start(bf16[16,2048]{1,0:T(8,128)(2,1)S(1)} %terms14.2), channel_id=1, source_target_pairs={{0,4},{1,3},{2,6},{3,1},{4,0},{5,7},{6,2},{7,5},{8,12},{9,11},{10,... | collective-permute-start | bytes 196616 | tf_op jit(solution)/shard_map/ppermute | solution.py:214
  18.0 4.3 %collective-permute-start.1 = (bf16[16,2048]{1,0:T(8,128)(2,1)S(1)}, bf16[16,2048]{1,0:T(8,128)(2,1)S(1)}, u32[]{:S(2)}, u32[]{:S(2)}) collective-permute-start(bf16[16,2048]{1,0:T(8,128)(2,1)S(1)} %terms15.2), channel_id=1, source_target_pairs={{0,2},{1,5},{2,0},{3,7},{4,6},{5,1},{6,4},{7,3},{8,10},{9,13},{10,... | collective-permute-start | bytes 196616 | tf_op jit(solution)/shard_map/ppermute | solution.py:214
  20.1 4.3 %collective-permute-start.10 = (bf16[16,2048]{1,0:T(8,128)(2,1)S(1)}, bf16[16,2048]{1,0:T(8,128)(2,1)S(1)}, u32[]{:S(2)}, u32[]{:S(2)}) collective-permute-start(bf16[16,2048]{1,0:T(8,128)(2,1)S(1)} %inner_sum0.2.own_ref), channel_id=1, source_target_pairs={{0,8},{1,17},{2,10},{3,19},{4,12},{5,21},{6,14},{7,23},{8,0},{9,25... | collective-permute-start | bytes 196616 | tf_op jit(solution)/shard_map/ppermute | solution.py:214
  22.3 5.5 %collective-permute-start.4 = (bf16[16,2048]{1,0:T(8,128)(2,1)S(1)}, bf16[16,2048]{1,0:T(8,128)(2,1)S(1)}, u32[]{:S(2)}, u32[]{:S(2)}) collective-permute-start(bf16[16,2048]{1,0:T(8,128)(2,1)S(1)} %inner_sum1.2.own_ref), channel_id=1, source_target_pairs={{0,8},{1,17},{2,10},{3,19},{4,12},{5,21},{6,14},{7,23},{8,0},{9,25... | collective-permute-start | bytes 196616 | tf_op jit(solution)/shard_map/ppermute | solution.py:214
  24.4 5.3 %collective-permute-start.11 = (bf16[16,2048]{1,0:T(8,128)(2,1)S(1)}, bf16[16,2048]{1,0:T(8,128)(2,1)S(1)}, u32[]{:S(2)}, u32[]{:S(2)}) collective-permute-start(bf16[16,2048]{1,0:T(8,128)(2,1)S(1)} %pair_sum0.2.own_ref), channel_id=1, source_target_pairs={{0,16},{1,9},{2,18},{3,11},{4,20},{5,13},{6,22},{7,15},{8,24},{9,1... | collective-permute-start | bytes 196616 | tf_op jit(solution)/shard_map/ppermute | solution.py:214
  27.9 5.2 %collective-permute-start.5 = (bf16[16,2048]{1,0:T(8,128)(2,1)S(1)}, bf16[16,2048]{1,0:T(8,128)(2,1)S(1)}, u32[]{:S(2)}, u32[]{:S(2)}) collective-permute-start(bf16[16,2048]{1,0:T(8,128)(2,1)S(1)} %pair_sum1.2.own_ref), channel_id=1, source_target_pairs={{0,16},{1,9},{2,18},{3,11},{4,20},{5,13},{6,22},{7,15},{8,24},{9,1... | collective-permute-start | bytes 196616 | tf_op jit(solution)/shard_map/ppermute | solution.py:214
  29.8 6.9 %collective-permute-start.13 = (bf16[16,2048]{1,0:T(8,128)(2,1)S(1)}, bf16[16,2048]{1,0:T(8,128)(2,1)S(1)}, u32[]{:S(2)}, u32[]{:S(2)}) collective-permute-start(bf16[16,2048]{1,0:T(8,128)(2,1)S(1)} %outer_sum0.2.refs_0_), channel_id=1, source_target_pairs={{0,4},{1,3},{2,6},{3,1},{4,0},{5,7},{6,2},{7,5},{8,12},{9,11},{10,... | collective-permute-start | bytes 196616 | tf_op jit(solution)/shard_map/ppermute | solution.py:214
  31.3 5.4 %collective-permute-start.14 = (bf16[16,2048]{1,0:T(8,128)(2,1)S(1)}, bf16[16,2048]{1,0:T(8,128)(2,1)S(1)}, u32[]{:S(2)}, u32[]{:S(2)}) collective-permute-start(bf16[16,2048]{1,0:T(8,128)(2,1)S(1)} %outer_sum0.2.refs_0_), channel_id=1, source_target_pairs={{0,2},{1,5},{2,0},{3,7},{4,6},{5,1},{6,4},{7,3},{8,10},{9,13},{10,... | collective-permute-start | bytes 196616 | tf_op jit(solution)/shard_map/ppermute | solution.py:214
  33.1 6.0 %collective-permute-start.12 = (bf16[16,4096]{1,0:T(8,128)(2,1)S(1)}, bf16[16,4096]{1,0:T(8,128)(2,1)S(1)}, u32[]{:S(2)}, u32[]{:S(2)}) collective-permute-start(bf16[16,4096]{1,0:T(8,128)(2,1)S(1)} %stack.2), channel_id=1, source_target_pairs={{0,6},{1,7},{2,4},{3,5},{4,2},{5,3},{6,0},{7,1},{8,14},{9,15},{10,... | collective-permute-start | bytes 393224 | tf_op jit(solution)/shard_map/ppermute | solution.py:214
  34.1 5.8 %collective-permute-start.7 = (bf16[16,2048]{1,0:T(8,128)(2,1)S(1)}, bf16[16,2048]{1,0:T(8,128)(2,1)S(1)}, u32[]{:S(2)}, u32[]{:S(2)}) collective-permute-start(bf16[16,2048]{1,0:T(8,128)(2,1)S(1)} %outer_sum1.2.refs_1_.refs_3_), channel_id=1, source_target_pairs={{0,4},{1,3},{2,6},{3,1},{4,0},{5,7},{6,2},{7,5},{8,12},{9,11},{10,... | collective-permute-start | bytes 196616 | tf_op jit(solution)/shard_map/ppermute | solution.py:214
  36.2 4.3 %collective-permute-start.6 = (bf16[16,2048]{1,0:T(8,128)(2,1)S(1)}, bf16[16,2048]{1,0:T(8,128)(2,1)S(1)}, u32[]{:S(2)}, u32[]{:S(2)}) collective-permute-start(bf16[16,2048]{1,0:T(8,128)(2,1)S(1)} %outer_sum1.2.refs_1_.refs_3_), channel_id=1, source_target_pairs={{0,2},{1,5},{2,0},{3,7},{4,6},{5,1},{6,4},{7,3},{8,10},{9,13},{10,... | collective-permute-start | bytes 196616 | tf_op jit(solution)/shard_map/ppermute | solution.py:214
  40.9 1.2 %collective-permute-start.15 = (f32[16,640]{1,0:T(8,128)S(1)}, f32[16,640]{1,0:T(8,128)S(1)}, u32[]{:S(2)}, u32[]{:S(2)}) collective-permute-start(f32[16,640]{1,0:T(8,128)S(1)} %project6.2.own_ref), channel_id=1, source_target_pairs={{0,1},{1,0},{2,3},{3,2},{4,5},{5,4},{6,7},{7,6},{8,9},{9,8},{10,11... | collective-permute-start | bytes 122888 | tf_op jit(solution)/shard_map/ppermute | solution.py:208
  43.2 8.0 %collective-permute-start.18 = (bf16[16,4096]{1,0:T(8,128)(2,1)S(1)}, bf16[16,4096]{1,0:T(8,128)(2,1)S(1)}, u32[]{:S(2)}, u32[]{:S(2)}) collective-permute-start(bf16[16,4096]{1,0:T(8,128)(2,1)S(1)} %terms23.3), channel_id=1, source_target_pairs={{0,6},{1,7},{2,4},{3,5},{4,2},{5,3},{6,0},{7,1},{8,14},{9,15},{10,... | collective-permute-start | bytes 393224 | tf_op jit(solution)/shard_map/ppermute | solution.py:214
  44.8 6.3 %collective-permute-start.24 = (bf16[16,2048]{1,0:T(8,128)(2,1)S(1)}, bf16[16,2048]{1,0:T(8,128)(2,1)S(1)}, u32[]{:S(2)}, u32[]{:S(2)}) collective-permute-start(bf16[16,2048]{1,0:T(8,128)(2,1)S(1)} %terms04.3), channel_id=1, source_target_pairs={{0,4},{1,3},{2,6},{3,1},{4,0},{5,7},{6,2},{7,5},{8,12},{9,11},{10,... | collective-permute-start | bytes 196616 | tf_op jit(solution)/shard_map/ppermute | solution.py:214
  46.8 4.4 %collective-permute-start.23 = (bf16[16,2048]{1,0:T(8,128)(2,1)S(1)}, bf16[16,2048]{1,0:T(8,128)(2,1)S(1)}, u32[]{:S(2)}, u32[]{:S(2)}) collective-permute-start(bf16[16,2048]{1,0:T(8,128)(2,1)S(1)} %terms05.3), channel_id=1, source_target_pairs={{0,2},{1,5},{2,0},{3,7},{4,6},{5,1},{6,4},{7,3},{8,10},{9,13},{10,... | collective-permute-start | bytes 196616 | tf_op jit(solution)/shard_map/ppermute | solution.py:214
  47.9 5.7 %collective-permute-start.17 = (bf16[16,2048]{1,0:T(8,128)(2,1)S(1)}, bf16[16,2048]{1,0:T(8,128)(2,1)S(1)}, u32[]{:S(2)}, u32[]{:S(2)}) collective-permute-start(bf16[16,2048]{1,0:T(8,128)(2,1)S(1)} %terms14.3), channel_id=1, source_target_pairs={{0,4},{1,3},{2,6},{3,1},{4,0},{5,7},{6,2},{7,5},{8,12},{9,11},{10,... | collective-permute-start | bytes 196616 | tf_op jit(solution)/shard_map/ppermute | solution.py:214
  48.7 4.9 %collective-permute-start.16 = (bf16[16,2048]{1,0:T(8,128)(2,1)S(1)}, bf16[16,2048]{1,0:T(8,128)(2,1)S(1)}, u32[]{:S(2)}, u32[]{:S(2)}) collective-permute-start(bf16[16,2048]{1,0:T(8,128)(2,1)S(1)} %terms15.3), channel_id=1, source_target_pairs={{0,2},{1,5},{2,0},{3,7},{4,6},{5,1},{6,4},{7,3},{8,10},{9,13},{10,... | collective-permute-start | bytes 196616 | tf_op jit(solution)/shard_map/ppermute | solution.py:214
  51.3 4.9 %collective-permute-start.25 = (bf16[16,2048]{1,0:T(8,128)(2,1)S(1)}, bf16[16,2048]{1,0:T(8,128)(2,1)S(1)}, u32[]{:S(2)}, u32[]{:S(2)}) collective-permute-start(bf16[16,2048]{1,0:T(8,128)(2,1)S(1)} %inner_sum0.3.own_ref), channel_id=1, source_target_pairs={{0,8},{1,17},{2,10},{3,19},{4,12},{5,21},{6,14},{7,23},{8,0},{9,25... | collective-permute-start | bytes 196616 | tf_op jit(solution)/shard_map/ppermute | solution.py:214
  53.7 5.5 %collective-permute-start.19 = (bf16[16,2048]{1,0:T(8,128)(2,1)S(1)}, bf16[16,2048]{1,0:T(8,128)(2,1)S(1)}, u32[]{:S(2)}, u32[]{:S(2)}) collective-permute-start(bf16[16,2048]{1,0:T(8,128)(2,1)S(1)} %inner_sum1.3.own_ref), channel_id=1, source_target_pairs={{0,8},{1,17},{2,10},{3,19},{4,12},{5,21},{6,14},{7,23},{8,0},{9,25... | collective-permute-start | bytes 196616 | tf_op jit(solution)/shard_map/ppermute | solution.py:214
  56.2 5.3 %collective-permute-start.26 = (bf16[16,2048]{1,0:T(8,128)(2,1)S(1)}, bf16[16,2048]{1,0:T(8,128)(2,1)S(1)}, u32[]{:S(2)}, u32[]{:S(2)}) collective-permute-start(bf16[16,2048]{1,0:T(8,128)(2,1)S(1)} %pair_sum0.3.own_ref), channel_id=1, source_target_pairs={{0,16},{1,9},{2,18},{3,11},{4,20},{5,13},{6,22},{7,15},{8,24},{9,1... | collective-permute-start | bytes 196616 | tf_op jit(solution)/shard_map/ppermute | solution.py:214
  59.3 5.2 %collective-permute-start.20 = (bf16[16,2048]{1,0:T(8,128)(2,1)S(1)}, bf16[16,2048]{1,0:T(8,128)(2,1)S(1)}, u32[]{:S(2)}, u32[]{:S(2)}) collective-permute-start(bf16[16,2048]{1,0:T(8,128)(2,1)S(1)} %pair_sum1.3.own_ref), channel_id=1, source_target_pairs={{0,16},{1,9},{2,18},{3,11},{4,20},{5,13},{6,22},{7,15},{8,24},{9,1... | collective-permute-start | bytes 196616 | tf_op jit(solution)/shard_map/ppermute | solution.py:214
  61.6 6.5 %collective-permute-start.28 = (bf16[16,2048]{1,0:T(8,128)(2,1)S(1)}, bf16[16,2048]{1,0:T(8,128)(2,1)S(1)}, u32[]{:S(2)}, u32[]{:S(2)}) collective-permute-start(bf16[16,2048]{1,0:T(8,128)(2,1)S(1)} %outer_sum0.3.refs_0_), channel_id=1, source_target_pairs={{0,4},{1,3},{2,6},{3,1},{4,0},{5,7},{6,2},{7,5},{8,12},{9,11},{10,... | collective-permute-start | bytes 196616 | tf_op jit(solution)/shard_map/ppermute | solution.py:214
  62.4 5.7 %collective-permute-start.29 = (bf16[16,2048]{1,0:T(8,128)(2,1)S(1)}, bf16[16,2048]{1,0:T(8,128)(2,1)S(1)}, u32[]{:S(2)}, u32[]{:S(2)}) collective-permute-start(bf16[16,2048]{1,0:T(8,128)(2,1)S(1)} %outer_sum0.3.refs_0_), channel_id=1, source_target_pairs={{0,2},{1,5},{2,0},{3,7},{4,6},{5,1},{6,4},{7,3},{8,10},{9,13},{10,... | collective-permute-start | bytes 196616 | tf_op jit(solution)/shard_map/ppermute | solution.py:214
  64.5 6.0 %collective-permute-start.27 = (bf16[16,4096]{1,0:T(8,128)(2,1)S(1)}, bf16[16,4096]{1,0:T(8,128)(2,1)S(1)}, u32[]{:S(2)}, u32[]{:S(2)}) collective-permute-start(bf16[16,4096]{1,0:T(8,128)(2,1)S(1)} %stack.3), channel_id=1, source_target_pairs={{0,6},{1,7},{2,4},{3,5},{4,2},{5,3},{6,0},{7,1},{8,14},{9,15},{10,... | collective-permute-start | bytes 393224 | tf_op jit(solution)/shard_map/ppermute | solution.py:214
  65.7 5.6 %collective-permute-start.22 = (bf16[16,2048]{1,0:T(8,128)(2,1)S(1)}, bf16[16,2048]{1,0:T(8,128)(2,1)S(1)}, u32[]{:S(2)}, u32[]{:S(2)}) collective-permute-start(bf16[16,2048]{1,0:T(8,128)(2,1)S(1)} %outer_sum1.3.refs_1_.refs_3_), channel_id=1, source_target_pairs={{0,4},{1,3},{2,6},{3,1},{4,0},{5,7},{6,2},{7,5},{8,12},{9,11},{10,... | collective-permute-start | bytes 196616 | tf_op jit(solution)/shard_map/ppermute | solution.py:214
  66.1 5.7 %collective-permute-start.21 = (bf16[16,2048]{1,0:T(8,128)(2,1)S(1)}, bf16[16,2048]{1,0:T(8,128)(2,1)S(1)}, u32[]{:S(2)}, u32[]{:S(2)}) collective-permute-start(bf16[16,2048]{1,0:T(8,128)(2,1)S(1)} %outer_sum1.3.refs_1_.refs_3_), channel_id=1, source_target_pairs={{0,2},{1,5},{2,0},{3,7},{4,6},{5,1},{6,4},{7,3},{8,10},{9,13},{10,... | collective-permute-start | bytes 196616 | tf_op jit(solution)/shard_map/ppermute | solution.py:214
  72.2 1.2 %collective-permute-start.30 = (f32[16,640]{1,0:T(8,128)S(1)}, f32[16,640]{1,0:T(8,128)S(1)}, u32[]{:S(2)}, u32[]{:S(2)}) collective-permute-start(f32[16,640]{1,0:T(8,128)S(1)} %project6.3.own_ref), channel_id=1, source_target_pairs={{0,1},{1,0},{2,3},{3,2},{4,5},{5,4},{6,7},{7,6},{8,9},{9,8},{10,11... | collective-permute-start | bytes 122888 | tf_op jit(solution)/shard_map/ppermute | solution.py:208
